TPU v7x, 32 devices: a whole 2x2x4 slice. The times are simulated.
32 devices in a mesh: dp: 8 (over y, x, core), tensor: 4 (over z).
Axes of the slice: x: 2, y: 2, z: 4, core: 2. Of those that a mesh axis runs over, the one named last changes fastest.
Arguments:
- tokens: bfloat16 [64, 256, 768], P('dp'), may hold values from -6 to 6
- lengths: int32 [64], P('dp'), may hold values from 64 to 256, as said below
- adapter_mask: int32 [64], P('dp'), may hold values from 1 to 65535, as said below
- cotangent: bfloat16 [64, 256, 768], P(('dp', 'tensor')), may hold values from -6 to 6
- att_query: bfloat16 [768, 768], P(None, 'tensor'), may hold values from -0.3125 to 0.3125
- att_key: bfloat16 [768, 768], P(None, 'tensor'), may hold values from -0.3125 to 0.3125
- att_value: bfloat16 [768, 768], P(None, 'tensor'), may hold values from -0.21875 to 0.21875
- att_out: bfloat16 [768, 768], P('tensor'), may hold values from -0.875 to 0.875
- norm1_gain: float32 [768], replicated, may hold values from 0.5 to 1.5
- norm1_bias: float32 [768], replicated, may hold values from -1.25 to 1.25
- ffn_in: bfloat16 [768, 3072], P(None, 'tensor'), may hold values from -0.21875 to 0.21875
- ffn_bias: float32 [3072], replicated, may hold values from -1.75 to 1.75
- ffn_out: bfloat16 [3072, 768], P('tensor'), may hold values from -0.109375 to 0.109375
- adapt_down: bfloat16 [768, 768], replicated, may hold values from -0.21875 to 0.21875
- adapt_up: bfloat16 [16, 48, 768], replicated, may hold values from -1.5 to 1.5
- norm2_gain: float32 [768], replicated, may hold values from 0.5 to 1.5
- norm2_bias: float32 [768], replicated, may hold values from -1.25 to 1.25
- joining_query: bfloat16 [768, 768], P(('dp', 'tensor')), may hold values from -0.4375 to 0.4375
- joining_key: bfloat16 [768, 768], P(('dp', 'tensor')), may hold values from -0.4375 to 0.4375
- joining_value: bfloat16 [768, 768], P(('dp', 'tensor')), may hold values from -0.21875 to 0.21875
- joining_qbias: bfloat16 [768], P(('dp', 'tensor')), may hold values from -1.75 to 1.75
- joining_vbias: bfloat16 [768], P(('dp', 'tensor')), may hold values from -1.75 to 1.75
Outputs:
- layer_out: bfloat16 [64, 256, 768], P(('dp', 'tensor'))
- input_grad: bfloat16 [64, 256, 768], P(('dp', 'tensor'))
- grad_joining_query: float32 [768, 768], P(('dp', 'tensor'))
- grad_joining_key: float32 [768, 768], P(('dp', 'tensor'))
- grad_joining_value: float32 [768, 768], P(('dp', 'tensor'))
- grad_joining_qbias: float32 [768], P(('dp', 'tensor'))
- grad_joining_vbias: float32 [768], P(('dp', 'tensor'))
Inputs may be any that keep to these rules, and one draw needn't show every extreme that they name: Padding lengths; some sequence is full and some has exactly 64 tokens. `adapter_mask`: bit m (m below 16) tells whether adapter m is available to the sequence; every sequence has one available adapter or more, some sequence all of them, some only adapter 0.
All inputs are finite; a program needn't handle non-finite values.
Results may differ from a plain program's by a relative error of at most 0.039.
Values may be sent and summed in bfloat16 or wider, within the bound.
No kernel may reach another device: no remote copies, remote signals or barrier semaphores. Data moves between devices by JAX's collectives and lax.ppermute only.
A program may use at most 256 MiB of HBM per device.

v0:
```python
from functools import partial
import math

import jax
import jax.numpy as jnp
from jax import lax
from jax.sharding import PartitionSpec as P

HEADS = 12
MICRO = 2


norm_epsilon = 1e-05
masked_score = -1e30


def layer_norm(values, gain_vec, bias_vec):
    average = jnp.mean(values, axis=-1, keepdims=True)
    centered = values - average
    variance = jnp.mean(centered * centered, axis=-1, keepdims=True)
    return centered * lax.rsqrt(variance + norm_epsilon) * gain_vec + bias_vec


def exact_gelu(values):
    return jax.nn.gelu(values, approximate=False)


def matmul(left, right):
    return jnp.dot(left, right, preferred_element_type=jnp.float32)


def times_transpose(left, right):
    return lax.dot_general(
        left, right, (((1,), (1,)), ((), ())), preferred_element_type=jnp.float32
    )


def contract_rows(left, right):
    return lax.dot_general(
        left, right, (((0,), (0,)), ((), ())), preferred_element_type=jnp.float32
    )


def softmax_rows(scores):
    row_max = jnp.max(scores, axis=-1, keepdims=True)
    weights_exp = jnp.exp(scores - row_max)
    row_total = jnp.sum(weights_exp, axis=-1, keepdims=True)
    return (weights_exp / row_total, row_max + jnp.log(row_total))


def attention_forward(x_seqs, len_seqs, w_query, w_key, w_value, head_dim):
    seq_count, seq_len, model_dim = x_seqs.shape
    flat_tokens = x_seqs.reshape(seq_count * seq_len, model_dim)
    local_heads = w_query.shape[1] // head_dim
    scale = 1.0 / math.sqrt(head_dim)

    def project(weight):
        return (
            matmul(flat_tokens, weight)
            .astype(jnp.bfloat16)
            .reshape(seq_count, seq_len, local_heads, head_dim)
        )

    queries = project(w_query)
    att_keys = project(w_key)
    att_values = project(w_value)
    positions = jnp.arange(seq_len, dtype=jnp.int32)
    valid_keys = (positions[None, :] < len_seqs[:, None])[:, None, None, :]
    scores = (
        jnp.einsum("sqhe,skhe->shqk", queries, att_keys, preferred_element_type=jnp.float32) * scale
    )
    att_probs, log_total = softmax_rows(jnp.where(valid_keys, scores, masked_score))
    context = jnp.einsum(
        "shqk,skhe->sqhe",
        att_probs.astype(jnp.bfloat16),
        att_values,
        preferred_element_type=jnp.float32,
    )
    context_flat = context.astype(jnp.bfloat16).reshape(seq_count * seq_len, local_heads * head_dim)
    return (context_flat, (queries, att_keys, att_values, valid_keys, log_total))


def attention_backward(saved, grad_context_flat, w_query, w_key, w_value, head_dim):
    queries, att_keys, att_values, valid_keys, log_total = saved
    scale = 1.0 / math.sqrt(head_dim)
    grad_context = grad_context_flat.astype(jnp.bfloat16).reshape(queries.shape)
    scores = (
        jnp.einsum("sqhe,skhe->shqk", queries, att_keys, preferred_element_type=jnp.float32) * scale
    )
    att_probs = jnp.exp(jnp.where(valid_keys, scores, masked_score) - log_total)
    grad_probs = jnp.einsum(
        "sqhe,skhe->shqk", grad_context, att_values, preferred_element_type=jnp.float32
    )
    grad_values = jnp.einsum(
        "shqk,sqhe->skhe",
        att_probs.astype(jnp.bfloat16),
        grad_context,
        preferred_element_type=jnp.float32,
    )
    row_dot = jnp.sum(grad_probs * att_probs, axis=-1, keepdims=True)
    grad_scores = (att_probs * (grad_probs - row_dot)).astype(jnp.bfloat16)
    grad_queries = (
        jnp.einsum("shqk,skhe->sqhe", grad_scores, att_keys, preferred_element_type=jnp.float32)
        * scale
    )
    grad_keys = (
        jnp.einsum("shqk,sqhe->skhe", grad_scores, queries, preferred_element_type=jnp.float32)
        * scale
    )
    row_count = queries.shape[0] * queries.shape[1]
    total = times_transpose(grad_queries.astype(jnp.bfloat16).reshape(row_count, -1), w_query)
    total = total + times_transpose(grad_keys.astype(jnp.bfloat16).reshape(row_count, -1), w_key)
    return total + times_transpose(grad_values.astype(jnp.bfloat16).reshape(row_count, -1), w_value)


def ffn_forward(normed, w_in, b_in, w_out):
    pre_act = matmul(normed.astype(jnp.bfloat16), w_in) + b_in
    activated, gelu_pull = jax.vjp(exact_gelu, pre_act)
    return (matmul(activated.astype(jnp.bfloat16), w_out), gelu_pull)


def ffn_backward(grad_ffn, gelu_pull, w_in, w_out):
    grad_pre_act = gelu_pull(times_transpose(grad_ffn, w_out))[0]
    return times_transpose(grad_pre_act.astype(jnp.bfloat16), w_in)


def adapter_joining(
    ffn_output,
    normed_mine,
    available,
    out_grad,
    joining_set,
    adapt_down,
    adapt_up,
    norm2_gain,
    norm2_bias,
):
    joining_query, joining_key, joining_value, joining_qbias, joining_vbias = joining_set
    row_count, model_dim = ffn_output.shape
    adapter_count = adapt_up.shape[0]
    bottleneck = adapt_up.shape[1]
    scale = 1.0 / math.sqrt(model_dim)
    ffn_low = ffn_output.astype(jnp.bfloat16)
    down_pre = matmul(ffn_low, adapt_down)
    down_act, down_pull = jax.vjp(exact_gelu, down_pre)
    down_low = down_act.astype(jnp.bfloat16).reshape(row_count, adapter_count, bottleneck)
    branch = jnp.einsum("rmb,mbd->rmd", down_low, adapt_up, preferred_element_type=jnp.float32)
    adapted_flat = (
        (ffn_output[:, None, :] + branch)
        .astype(jnp.bfloat16)
        .reshape(row_count * adapter_count, model_dim)
    )
    joining_q = matmul(ffn_low, joining_query) + joining_qbias.astype(jnp.float32)
    adapter_keys = matmul(adapted_flat, joining_key).reshape(row_count, adapter_count, model_dim)
    adapter_vals = (
        matmul(adapted_flat, joining_value) + joining_vbias.astype(jnp.float32)
    ).reshape(row_count, adapter_count, model_dim)
    fscores = jnp.sum(joining_q[:, None, :] * adapter_keys, axis=-1) * scale
    fprobs = softmax_rows(jnp.where(available, fscores, masked_score))[0]
    mixture = jnp.sum(fprobs[:, :, None] * adapter_vals, axis=1)
    layer_out, norm_pull = jax.vjp(
        partial(layer_norm, gain_vec=norm2_gain, bias_vec=norm2_bias), normed_mine + mixture
    )
    grad_pre2 = norm_pull(out_grad)[0]
    grad_vals = (
        (fprobs[:, :, None] * grad_pre2[:, None, :])
        .astype(jnp.bfloat16)
        .reshape(row_count * adapter_count, model_dim)
    )
    grad_fprobs = jnp.sum(grad_pre2[:, None, :] * adapter_vals, axis=-1)
    grad_fscores = (
        fprobs * (grad_fprobs - jnp.sum(grad_fprobs * fprobs, axis=-1, keepdims=True)) * scale
    )
    grad_query = jnp.sum(grad_fscores[:, :, None] * adapter_keys, axis=1).astype(jnp.bfloat16)
    grad_keys = (
        (grad_fscores[:, :, None] * joining_q[:, None, :])
        .astype(jnp.bfloat16)
        .reshape(row_count * adapter_count, model_dim)
    )
    weight_grads = (
        contract_rows(ffn_low, grad_query),
        contract_rows(adapted_flat, grad_keys),
        contract_rows(adapted_flat, grad_vals),
        jnp.sum(grad_query.astype(jnp.float32), axis=0),
        jnp.sum(grad_vals.astype(jnp.float32), axis=0),
    )
    grad_adapted = (
        times_transpose(grad_keys, joining_key) + times_transpose(grad_vals, joining_value)
    ).reshape(row_count, adapter_count, model_dim)
    grad_active = jnp.einsum(
        "rmd,mbd->rmb",
        grad_adapted.astype(jnp.bfloat16),
        adapt_up,
        preferred_element_type=jnp.float32,
    )
    grad_down = down_pull(grad_active.reshape(row_count, adapter_count * bottleneck))[0].astype(
        jnp.bfloat16
    )
    grad_ffn = (
        jnp.sum(grad_adapted, axis=1)
        + times_transpose(grad_down, adapt_down)
        + times_transpose(grad_query, joining_query)
    )
    return (layer_out.astype(jnp.bfloat16), grad_pre2, grad_ffn.astype(jnp.bfloat16), weight_grads)


def shards(
    tokens,
    lengths,
    adapter_mask,
    cotangent,
    att_query,
    att_key,
    att_value,
    att_out,
    norm1_gain,
    norm1_bias,
    ffn_in,
    ffn_bias,
    ffn_out,
    adapt_down,
    adapt_up,
    norm2_gain,
    norm2_bias,
    joining_query,
    joining_key,
    joining_value,
    joining_qbias,
    joining_vbias,
):
    groups = lax.axis_size("tensor")
    tensor_rank = lax.axis_index("tensor")
    seq_local, seq_len, model_dim = tokens.shape
    per_micro = seq_local // MICRO
    seq_mine = per_micro // groups
    head_dim = model_dim // HEADS
    tokens_mb = tokens.reshape(per_micro, MICRO, seq_len, model_dim)
    lengths_mb = lengths.reshape(per_micro, MICRO)
    mask_mb = adapter_mask.reshape(per_micro, MICRO)
    cot_mb = cotangent.reshape(seq_mine, MICRO, seq_len, model_dim)
    shifts = jnp.arange(adapt_up.shape[0], dtype=jnp.int32)
    joining_local = (joining_query, joining_key, joining_value, joining_qbias, joining_vbias)
    units_mine = ffn_in.shape[1]
    bias_mine = lax.dynamic_slice_in_dim(ffn_bias, tensor_rank * units_mine, units_mine, 0)
    grad_sums = (
        jnp.zeros((model_dim, model_dim), jnp.float32),
        jnp.zeros((model_dim, model_dim), jnp.float32),
        jnp.zeros((model_dim, model_dim), jnp.float32),
        jnp.zeros((model_dim,), jnp.float32),
        jnp.zeros((model_dim,), jnp.float32),
    )
    out_list = []
    grad_list = []
    for micro_idx in range(MICRO):
        joining_set = (
            lax.all_gather(joining_local[0], ("dp", "tensor"), axis=0, tiled=True),
            lax.all_gather(joining_local[1], ("dp", "tensor"), axis=0, tiled=True),
            lax.all_gather(joining_local[2], ("dp", "tensor"), axis=0, tiled=True),
            lax.all_gather(joining_local[3], ("dp", "tensor"), axis=0, tiled=True),
            lax.all_gather(joining_local[4], ("dp", "tensor"), axis=0, tiled=True),
        )
        x_micro = tokens_mb[:, micro_idx]
        len_micro = lengths_mb[:, micro_idx]
        mask_mine = lax.dynamic_slice_in_dim(
            mask_mb[:, micro_idx], tensor_rank * seq_mine, seq_mine, 0
        )
        mask_bits = jnp.right_shift(mask_mine[:, None], shifts[None, :]) % 2
        available = jnp.broadcast_to(
            (mask_bits == 1)[:, None, :], (seq_mine, seq_len, shifts.shape[0])
        ).reshape(seq_mine * seq_len, shifts.shape[0])
        out_grad = cot_mb[:, micro_idx].reshape(seq_mine * seq_len, model_dim).astype(jnp.float32)
        context_flat, saved = attention_forward(
            x_micro, len_micro, att_query, att_key, att_value, head_dim
        )
        attended = lax.psum(matmul(context_flat, att_out), "tensor")
        pre_norm1 = x_micro.reshape(per_micro * seq_len, model_dim).astype(jnp.float32) + attended
        normed1 = layer_norm(pre_norm1, norm1_gain, norm1_bias)
        ffn_part, gelu_pull = ffn_forward(normed1, ffn_in, bias_mine, ffn_out)
        ffn_mine = lax.psum_scatter(
            ffn_part.reshape(per_micro, seq_len, model_dim),
            "tensor",
            scatter_dimension=0,
            tiled=True,
        ).reshape(seq_mine * seq_len, model_dim)
        pre1_mine = lax.dynamic_slice_in_dim(
            pre_norm1.reshape(per_micro, seq_len, model_dim), tensor_rank * seq_mine, seq_mine, 0
        ).reshape(seq_mine * seq_len, model_dim)
        normed_mine = lax.dynamic_slice_in_dim(
            normed1.reshape(per_micro, seq_len, model_dim), tensor_rank * seq_mine, seq_mine, 0
        ).reshape(seq_mine * seq_len, model_dim)
        layer_out, grad_pre2, grad_ffn, weight_grads = adapter_joining(
            ffn_mine,
            normed_mine,
            available,
            out_grad,
            joining_set,
            adapt_down,
            adapt_up,
            norm2_gain,
            norm2_bias,
        )
        grad_ffn_all = lax.all_gather(
            grad_ffn.reshape(seq_mine, seq_len, model_dim), "tensor", axis=0, tiled=True
        ).reshape(per_micro * seq_len, model_dim)
        grad_normed_part = ffn_backward(grad_ffn_all, gelu_pull, ffn_in, ffn_out).reshape(
            per_micro, seq_len, model_dim
        )
        grad_normed = (
            lax.psum_scatter(grad_normed_part, "tensor", scatter_dimension=0, tiled=True).reshape(
                seq_mine * seq_len, model_dim
            )
            + grad_pre2
        )
        norm1_pull = jax.vjp(
            partial(layer_norm, gain_vec=norm1_gain, bias_vec=norm1_bias), pre1_mine
        )[1]
        grad_pre1 = norm1_pull(grad_normed)[0]
        grad_att_all = lax.all_gather(
            grad_pre1.astype(jnp.bfloat16).reshape(seq_mine, seq_len, model_dim),
            "tensor",
            axis=0,
            tiled=True,
        ).reshape(per_micro * seq_len, model_dim)
        grad_context = times_transpose(grad_att_all, att_out)
        input_part = attention_backward(
            saved, grad_context, att_query, att_key, att_value, head_dim
        ).reshape(per_micro, seq_len, model_dim)
        input_grad = (
            lax.psum_scatter(input_part, "tensor", scatter_dimension=0, tiled=True).reshape(
                seq_mine * seq_len, model_dim
            )
            + grad_pre1
        )
        grad_sums = jax.tree.map(jnp.add, grad_sums, weight_grads)
        out_list.append(layer_out.reshape(seq_mine, seq_len, model_dim))
        grad_list.append(input_grad.astype(jnp.bfloat16).reshape(seq_mine, seq_len, model_dim))
    layer_all = jnp.stack(out_list, axis=1).reshape(seq_mine * MICRO, seq_len, model_dim)
    input_all = jnp.stack(grad_list, axis=1).reshape(seq_mine * MICRO, seq_len, model_dim)
    final_grads = (
        lax.psum_scatter(grad_sums[0], ("dp", "tensor"), scatter_dimension=0, tiled=True),
        lax.psum_scatter(grad_sums[1], ("dp", "tensor"), scatter_dimension=0, tiled=True),
        lax.psum_scatter(grad_sums[2], ("dp", "tensor"), scatter_dimension=0, tiled=True),
        lax.psum_scatter(grad_sums[3], ("dp", "tensor"), scatter_dimension=0, tiled=True),
        lax.psum_scatter(grad_sums[4], ("dp", "tensor"), scatter_dimension=0, tiled=True),
    )
    return (
        layer_all,
        input_all,
        final_grads[0],
        final_grads[1],
        final_grads[2],
        final_grads[3],
        final_grads[4],
    )


def solution(mesh):
    return jax.shard_map(
        shards,
        mesh=mesh,
        in_specs=(
            P("dp", None, None),
            P("dp"),
            P("dp"),
            P(("dp", "tensor"), None, None),
            P(None, "tensor"),
            P(None, "tensor"),
            P(None, "tensor"),
            P("tensor", None),
            P(),
            P(),
            P(None, "tensor"),
            P(),
            P("tensor", None),
            P(),
            P(),
            P(),
            P(),
            P(("dp", "tensor"), None),
            P(("dp", "tensor"), None),
            P(("dp", "tensor"), None),
            P(("dp", "tensor")),
            P(("dp", "tensor")),
        ),
        out_specs=(
            P(("dp", "tensor"), None, None),
            P(("dp", "tensor"), None, None),
            P(("dp", "tensor"), None),
            P(("dp", "tensor"), None),
            P(("dp", "tensor"), None),
            P(("dp", "tensor")),
            P(("dp", "tensor")),
        ),
        check_vma=False,
    )
```

profile of v0, /device:TPU:0, one launch (start us, length us, event | category | flops | bytes accessed | tf_op | source)
XLA Modules:
  0.0 1360.7 jit_solution(8010205849413040821)
XLA Ops:
  38.4 225.0 %all-reduce.9.cloned.1.call-done = (f32[1024,768]{1,0:T(8,128)}, f32[1024,768]{1,0:T(8,128)}) async-done(((f32[1024,768]{1,0:T(8,128)}, f32[1024,768]{1,0:T(8,128)}), (f32[1024,768]{1,0:T(8,128)}, f32[1024,768]{1,0:T(8,128)})) %all-reduce.9.cloned.1.call-update) | async-done | bytes 6291472 | tf_op jit(solution)/shard_map/psum | solution.py:275
  274.2 16.3 %fusion.25 = (f32[1024,768]{1,0:T(8,128)S(1)}, f32[1024,768]{1,0:T(8,128)}, f32[1024,768]{1,0:T(8,128)S(1)}) fusion(f32[768]{0:T(1024)S(1)} %dynamic_slice.23, f32[1024,768]{1,0:T(8,128)S(1)} %fusion.54, bf16[768,768]{1,0:T(8,128)(2,1)S(1)} %copy-done.131, f32[1024,768]{1,0:T(8,128)S(1)} %get-tuple-element.52), kind=kOutput, calls=%fused_computation.53 | convolution fusion | flops 1307836416 | bytes 16911360 | tf_op jit(solution)/shard_map/dot_general | solution.py:29
  302.4 44.1 %all-reduce.6 = (bf16[768]{0:T(1024)(128)(2,1)S(1)}, bf16[768]{0:T(1024)(128)(2,1)S(1)}) all-reduce(bf16[768]{0:T(1024)(128)(2,1)S(1)} %dynamic-update-slice.1, bf16[768]{0:T(1024)(128)(2,1)S(1)} %dynamic-update-slice), channel_id=1, replica_groups=mesh['dp'=8,'tensor'=4] {'dp','tensor'}, use_global_device_ids=true, to_apply=%add.1 | all-reduce | flops 1536 | bytes 6144
  358.9 59.7 %reduce-scatter.10.cloned.1.call-done = f32[1,256,768]{2,1,0:T(8,128)} async-done(((f32[4,256,768]{2,1,0:T(8,128)}), f32[1,256,768]{2,1,0:T(8,128)}) %reduce-scatter.10.cloned.1.call-update) | async-done | bytes 786448 | tf_op jit(solution)/shard_map/reduce_scatter | solution.py:279
  434.6 49.2 %all-gather.12.cloned.1.call-done = bf16[768,768]{1,0:T(8,128)(2,1)} async-done(((bf16[24,768]{1,0:T(8,128)(2,1)}), bf16[768,768]{1,0:T(8,128)(2,1)}) %all-gather.12.cloned.1.call-update) | async-done | bytes 1179664 | tf_op jit(solution)/shard_map/all_gather | solution.py:257
  483.8 10.8 multiply_reduce_fusion.2
  501.0 9.1 copy.200
  511.4 10.7 multiply_reduce_fusion.3
  523.1 16.5 %all-gather.14.cloned.1.call-done = bf16[768,768]{1,0:T(8,128)(2,1)} async-done(((bf16[24,768]{1,0:T(8,128)(2,1)}), bf16[768,768]{1,0:T(8,128)(2,1)}) %all-gather.14.cloned.1.call-update) | async-done | bytes 1179664 | tf_op jit(solution)/shard_map/all_gather | solution.py:258
  610.0 10.8 bitcast_reduce_fusion.1
  635.3 10.5 fusion.251
  645.8 11.0 bitcast_reduce_fusion
  681.3 28.1 %all-gather.22.cloned.1.call-done = bf16[1024,768]{1,0:T(8,128)(2,1)} async-done(((bf16[256,768]{1,0:T(8,128)(2,1)}), bf16[1024,768]{1,0:T(8,128)(2,1)}) %all-gather.22.cloned.1.call-update) | async-done | bytes 1572880 | tf_op jit(solution)/shard_map/all_gather | solution.py:302
  719.4 51.3 %reduce-scatter.14.cloned.1.call-done = f32[1,256,768]{2,1,0:T(8,128)} async-done(((f32[4,256,768]{2,1,0:T(8,128)}), f32[1,256,768]{2,1,0:T(8,128)}) %reduce-scatter.14.cloned.1.call-update) | async-done | bytes 786448 | tf_op jit(solution)/shard_map/reduce_scatter | solution.py:309
  772.7 60.6 %reduce-scatter.18.cloned.1.call-done = f32[1,256,768]{2,1,0:T(8,128)} async-done(((f32[4,256,768]{2,1,0:T(8,128)}), f32[1,256,768]{2,1,0:T(8,128)}) %reduce-scatter.18.cloned.1.call-update) | async-done | bytes 786448 | tf_op jit(solution)/shard_map/reduce_scatter | solution.py:309
  845.0 31.5 %all-gather.16.cloned.1.call-done = bf16[4,256,768]{2,1,0:T(8,128)(2,1)} async-done(((bf16[1,256,768]{2,1,0:T(8,128)(2,1)}), bf16[4,256,768]{2,1,0:T(8,128)(2,1)}) %all-gather.16.cloned.1.call-update) | async-done | bytes 1572880 | tf_op jit(solution)/shard_map/all_gather | solution.py:318
  891.9 22.7 %all-gather.18.cloned.1.call-done = bf16[4,256,768]{2,1,0:T(8,128)(2,1)} async-done(((bf16[1,256,768]{2,1,0:T(8,128)(2,1)}), bf16[4,256,768]{2,1,0:T(8,128)(2,1)}) %all-gather.18.cloned.1.call-update) | async-done | bytes 1572880 | tf_op jit(solution)/shard_map/all_gather | solution.py:318
  942.1 9.9 bitcast_add_fusion.1
  960.1 9.9 bitcast_add_fusion
  974.9 43.8 %all-reduce.4 = (f32[768]{0:T(1024)S(1)}, f32[768]{0:T(1024)S(1)}) all-reduce(f32[768]{0:T(1024)S(1)} %add.416, f32[768]{0:T(1024)} %add.417), channel_id=13, replica_groups=mesh['dp'=8,'tensor'=4] {'dp','tensor'}, use_global_device_ids=true, to_apply=%region_55.56.clone | all-reduce | flops 1536 | bytes 12288
  1022.5 17.1 %reduce-scatter.20.cloned.1.call-done = f32[1,256,768]{2,1,0:T(8,128)} async-done(((f32[4,256,768]{2,1,0:T(8,128)}), f32[1,256,768]{2,1,0:T(8,128)}) %reduce-scatter.20.cloned.1.call-update) | async-done | bytes 786448 | tf_op jit(solution)/shard_map/reduce_scatter | solution.py:329
  1044.1 100.2 %reduce-scatter.22.cloned.1.call-done = f32[24,768]{1,0:T(8,128)} async-done(((f32[768,768]{1,0:T(8,128)}), f32[24,768]{1,0:T(8,128)}) %reduce-scatter.22.cloned.1.call-update) | async-done | bytes 73744 | tf_op jit(solution)/shard_map/reduce_scatter | solution.py:340
  1144.3 104.8 %reduce-scatter.24.cloned.1.call-done = f32[24,768]{1,0:T(8,128)} async-done(((f32[768,768]{1,0:T(8,128)}), f32[24,768]{1,0:T(8,128)}) %reduce-scatter.24.cloned.1.call-update) | async-done | bytes 73744 | tf_op jit(solution)/shard_map/reduce_scatter | solution.py:341
  1249.1 103.9 %reduce-scatter.26.cloned.1.call-done = f32[24,768]{1,0:T(8,128)} async-done(((f32[768,768]{1,0:T(8,128)}), f32[24,768]{1,0:T(8,128)}) %reduce-scatter.26.cloned.1.call-update) | async-done | bytes 73744 | tf_op jit(solution)/shard_map/reduce_scatter | solution.py:342
  (515 shorter events, 285.0 us)
Async XLA Ops:
  8.0 415.1 %copy-start = (bf16[16,48,768]{2,1,0:T(8,128)(2,1)S(1)}, bf16[16,48,768]{2,1,0:T(8,128)(2,1)}, u32[]{:S(2)}) copy-start(bf16[16,48,768]{2,1,0:T(8,128)(2,1)} %param.36) | copy-start | bytes 3538948
  8.0 255.4 %all-reduce.9.cloned.1.call-start = ((), (), s32[]{:S(2)}) async-start(), calls=%async_computation.25 | async-start | bytes 12582912 | tf_op jit(solution)/shard_map/psum | solution.py:275
  37.4 317.5 %reduce-scatter.12.cloned.1.call-start = ((), (), s32[]{:S(2)}) async-start(), calls=%async_computation.13 | async-start | bytes 3932160 | tf_op jit(solution)/shard_map/reduce_scatter | solution.py:279
  38.4 255.7 %copy-start.85 = (f32[768]{0:T(1024)}, f32[768]{0:T(1024)S(1)}, u32[]{:S(2)}) copy-start(f32[768]{0:T(1024)S(1)} %dynamic_slice.23) | copy-start | bytes 9220
  294.0 124.5 %reduce-scatter.10.cloned.1.call-start = ((), (), s32[]{:S(2)}) async-start(), calls=%async_computation.9 | async-start | bytes 3932160 | tf_op jit(solution)/shard_map/reduce_scatter | solution.py:279
  300.0 132.0 %all-gather.10.cloned.1.call-start = ((), (), s32[]{:S(2)}) async-start(), calls=%async_computation.10 | async-start | bytes 1216512 | tf_op jit(solution)/shard_map/all_gather | solution.py:256
  300.6 183.2 %all-gather.12.cloned.1.call-start = ((), (), s32[]{:S(2)}) async-start(), calls=%async_computation.11 | async-start | bytes 1216512 | tf_op jit(solution)/shard_map/all_gather | solution.py:257
  301.2 238.4 %all-gather.14.cloned.1.call-start = ((), (), s32[]{:S(2)}) async-start(), calls=%async_computation.12 | async-start | bytes 1216512 | tf_op jit(solution)/shard_map/all_gather | solution.py:258
  301.8 370.7 %all-gather.20.cloned.1.call-start = ((), (), s32[]{:S(2)}) async-start(), calls=%async_computation.23 | async-start | bytes 1966080 | tf_op jit(solution)/shard_map/all_gather | solution.py:302
  635.2 74.1 %all-gather.22.cloned.1.call-start = ((), (), s32[]{:S(2)}) async-start(), calls=%async_computation.24 | async-start | bytes 1966080 | tf_op jit(solution)/shard_map/all_gather | solution.py:302
  672.2 98.5 %reduce-scatter.14.cloned.1.call-start = ((), (), s32[]{:S(2)}) async-start(), calls=%async_computation.14 | async-start | bytes 3932160 | tf_op jit(solution)/shard_map/reduce_scatter | solution.py:309
  681.2 152.0 %reduce-scatter.18.cloned.1.call-start = ((), (), s32[]{:S(2)}) async-start(), calls=%async_computation.17 | async-start | bytes 3932160 | tf_op jit(solution)/shard_map/reduce_scatter | solution.py:309
  717.7 158.8 %all-gather.16.cloned.1.call-start = ((), (), s32[]{:S(2)}) async-start(), calls=%async_computation.15 | async-start | bytes 1966080 | tf_op jit(solution)/shard_map/all_gather | solution.py:318
  719.3 122.1 %copy-start.97 = (f32[256]{0:T(256)}, f32[256]{0:T(256)S(1)}, u32[]{:S(2)}) copy-start(f32[256]{0:T(256)S(1)} %broadcast_multiply_fusion.4) | copy-start | bytes 3076
  719.3 117.0 %copy-start.102 = (f32[256]{0:T(256)}, f32[256]{0:T(256)S(1)}, u32[]{:S(2)}) copy-start(f32[256]{0:T(256)S(1)} %broadcast_multiply_fusion.5) | copy-start | bytes 3076
  719.3 117.0 %copy-start.12 = (f32[256,768]{1,0:T(8,128)S(1)}, f32[256,768]{1,0:T(8,128)}, u32[]{:S(2)}) copy-start(f32[256,768]{1,0:T(8,128)} %copy-done.11) | copy-start | bytes 2359300
  719.3 117.0 %copy-start.76 = (f32[768]{0:T(1024)S(1)}, f32[768]{0:T(1024)}, u32[]{:S(2)}) copy-start(f32[768]{0:T(1024)} %param.37) | copy-start | bytes 9220
  719.4 117.0 %copy-start.101 = (f32[256]{0:T(256)S(1)}, f32[256]{0:T(256)}, u32[]{:S(2)}) copy-start(f32[256]{0:T(256)} %copy-done.100) | copy-start | bytes 3076
  839.2 75.4 %all-gather.18.cloned.1.call-start = ((), (), s32[]{:S(2)}) async-start(), calls=%async_computation.18 | async-start | bytes 1966080 | tf_op jit(solution)/shard_map/all_gather | solution.py:318
  844.5 175.4 %reduce-scatter.16.cloned.1.call-start = ((), (), s32[]{:S(2)}) async-start(), calls=%async_computation.16 | async-start | bytes 3932160 | tf_op jit(solution)/shard_map/reduce_scatter | solution.py:329
  891.2 148.4 %reduce-scatter.20.cloned.1.call-start = ((), (), s32[]{:S(2)}) async-start(), calls=%async_computation.19 | async-start | bytes 3932160 | tf_op jit(solution)/shard_map/reduce_scatter | solution.py:329
  929.2 215.1 %reduce-scatter.22.cloned.1.call-start = ((), (), s32[]{:S(2)}) async-start(), calls=%async_computation.20 | async-start | bytes 2433024 | tf_op jit(solution)/shard_map/reduce_scatter | solution.py:340
  934.1 314.9 %reduce-scatter.24.cloned.1.call-start = ((), (), s32[]{:S(2)}) async-start(), calls=%async_computation.21 | async-start | bytes 2433024 | tf_op jit(solution)/shard_map/reduce_scatter | solution.py:341
  952.1 400.9 %reduce-scatter.26.cloned.1.call-start = ((), (), s32[]{:S(2)}) async-start(), calls=%async_computation.22 | async-start | bytes 2433024 | tf_op jit(solution)/shard_map/reduce_scatter | solution.py:342
  (134 other events, 1836.2 us)
Sparse Core Ops, SparseCore 0:
  37.5 225.9 all-reduce.8
  294.1 60.6 reduce-scatter.11
  357.2 61.3 reduce-scatter.9
  635.3 35.9 all-gather.19
  673.3 35.9 all-gather.21
  711.5 59.1 reduce-scatter.13
  772.9 60.2 reduce-scatter.17
  839.4 37.1 all-gather.15
  878.7 35.9 all-gather.17
  916.8 59.0 reduce-scatter.15
  978.3 61.3 reduce-scatter.19
  1045.3 98.9 reduce-scatter.21
  1151.0 98.0 reduce-scatter.23
  1254.8 98.1 reduce-scatter.25
Sparse Core Ops, SparseCore 1:
  303.3 123.9 all-gather.9
  430.0 53.8 all-gather.11
  486.5 53.1 all-gather.13
where the time goes:
time: 1370 us; the launch traced here: 1360 us
  waiting for transfers between devices  876 us (64%)
  matrix products  231 us (17%)
  other arithmetic  90.7 us (7%)
  blocking collectives  87.9 us (6%)
  local copies, waits for them, and re-layouts  54.9 us (4%)
  between operations  18.3 us (1%)
    psum x1, waiting for transfers between devices, shards(): attended = lax.psum(matmul(context_flat, att_out), 'tensor')  225 us
    reduce_scatter x2, waiting for transfers between devices, shards(): lax.psum_scatter(grad_normed_part, 'tensor', scatter_dimension=0, tiled=T...  112 us
    reduce_scatter x1, waiting for transfers between devices, shards(): lax.psum_scatter(grad_sums[1], ('dp', 'tensor'), scatter_dimension=0, til...  105 us
    reduce_scatter x1, waiting for transfers between devices, shards(): lax.psum_scatter(grad_sums[2], ('dp', 'tensor'), scatter_dimension=0, til...  104 us
    reduce_scatter x1, waiting for transfers between devices, shards(): lax.psum_scatter(grad_sums[0], ('dp', 'tensor'), scatter_dimension=0, til...  100 us
    unnamed x2, blocking collectives  87.9 us
    dot_general x20, matrix products, matmul(): return jnp.dot(left, right, preferred_element_type=jnp.float32)  86.7 us
    dot_general x18, matrix products, times_transpose(): lax.dot_general(left, right, (((1,), (1,)), ((), ())), preferred_element_...  77.2 us
  transfers between devices with their start and end apart: 17, of which 14 were waited for; matrix products, arithmetic and copies ran while one was open for 16% of the time, Pallas kernels for 0%

commit v1 on v0

v1 whole, which is shorter than its diff:
```python
import math

import jax
import jax.numpy as jnp
from jax import lax
from jax.sharding import PartitionSpec as P

HEADS = 12
EPS = 1e-05
MASKED = -1e30
ALL = ("dp", "tensor")
BF = jnp.bfloat16
F32 = jnp.float32


def mm(left, right):
    return jnp.dot(left, right, preferred_element_type=F32)


def mm_t(left, right):
    return lax.dot_general(left, right, (((1,), (1,)), ((), ())), preferred_element_type=F32)


def t_mm(left, right):
    return lax.dot_general(left, right, (((0,), (0,)), ((), ())), preferred_element_type=F32)


def norm_parts(values):
    average = jnp.mean(values, axis=-1, keepdims=True)
    centered = values - average
    variance = jnp.mean(centered * centered, axis=-1, keepdims=True)
    rstd = lax.rsqrt(variance + EPS)
    return centered * rstd, rstd


def norm_back(grad, gain, xhat, rstd):
    scaled = grad * gain
    return rstd * (
        scaled
        - jnp.mean(scaled, axis=-1, keepdims=True)
        - xhat * jnp.mean(scaled * xhat, axis=-1, keepdims=True)
    )


def gelu_parts(pre):
    cdf = 0.5 * (1.0 + lax.erf(pre * (1.0 / math.sqrt(2.0))))
    pdf = jnp.exp(-0.5 * pre * pre) * (1.0 / math.sqrt(2.0 * math.pi))
    return pre * cdf, cdf + pre * pdf


def shards(
    tokens, lengths, adapter_mask, cotangent, att_query, att_key, att_value, att_out,
    norm1_gain, norm1_bias, ffn_in, ffn_bias, ffn_out, adapt_down, adapt_up, norm2_gain,
    norm2_bias, joining_query, joining_key, joining_value, joining_qbias, joining_vbias,
):
    groups = lax.axis_size("tensor")
    dp_size = lax.axis_size("dp")
    t_rank = lax.axis_index("tensor")
    d_rank = lax.axis_index("dp")
    seq_local, seq_len, dim = tokens.shape
    mine = seq_local // groups
    rows = mine * seq_len
    head_dim = dim // HEADS
    adapters, neck = adapt_up.shape[0], adapt_up.shape[1]

    def my_slice(array):
        return lax.dynamic_slice_in_dim(array, t_rank * mine, mine, 0)

    def my_part(weight):
        part = weight.shape[0] // dp_size
        return lax.dynamic_slice_in_dim(weight, d_rank * part, part, 0)

    def gather(part):
        return lax.all_gather(part, ALL, axis=0, tiled=False).reshape((dp_size, groups) + part.shape)

    def cols_whole(weight):
        g = gather(my_part(weight))
        return g.transpose(0, 2, 1, 3).reshape(weight.shape[0], groups * weight.shape[1])

    def rows_whole(weight):
        g = gather(my_part(weight))
        return g.transpose(1, 0, 2, 3).reshape(groups * weight.shape[0], weight.shape[1])

    w_q, w_k, w_v = cols_whole(att_query), cols_whole(att_key), cols_whole(att_value)
    w_o = rows_whole(att_out)
    w_in = cols_whole(ffn_in)
    w_out = rows_whole(ffn_out)
    j_q = lax.all_gather(joining_query, ALL, axis=0, tiled=True)
    j_k = lax.all_gather(joining_key, ALL, axis=0, tiled=True)
    j_v = lax.all_gather(joining_value, ALL, axis=0, tiled=True)
    j_qb = lax.all_gather(joining_qbias, ALL, axis=0, tiled=True).astype(F32)
    j_vb = lax.all_gather(joining_vbias, ALL, axis=0, tiled=True).astype(F32)

    x_low = my_slice(tokens).reshape(rows, dim)
    x_mine = x_low.astype(F32)
    len_mine = my_slice(lengths)
    mask_mine = my_slice(adapter_mask)
    shifts = jnp.arange(adapters, dtype=jnp.int32)
    bits = jnp.right_shift(mask_mine[:, None], shifts[None, :]) % 2
    available = jnp.broadcast_to((bits == 1)[:, None, :], (mine, seq_len, adapters)).reshape(rows, adapters)
    cot = cotangent.reshape(rows, dim).astype(F32)

    def heads_of(weight):
        return mm(x_low, weight).astype(BF).reshape(mine, seq_len, HEADS, head_dim)

    q, k, v = heads_of(w_q), heads_of(w_k), heads_of(w_v)
    scale = 1.0 / math.sqrt(head_dim)
    valid = (jnp.arange(seq_len, dtype=jnp.int32)[None, :] < len_mine[:, None])[:, None, None, :]
    scores = jnp.einsum("sqhe,skhe->shqk", q, k, preferred_element_type=F32) * scale
    scores = jnp.where(valid, scores, MASKED)
    row_max = jnp.max(scores, axis=-1, keepdims=True)
    exps = jnp.exp(scores - row_max)
    probs = exps / jnp.sum(exps, axis=-1, keepdims=True)
    probs_low = probs.astype(BF)
    ctx = jnp.einsum("shqk,skhe->sqhe", probs_low, v, preferred_element_type=F32)
    ctx = ctx.astype(BF).reshape(rows, dim)
    xhat1, rstd1 = norm_parts(x_mine + mm(ctx, w_o))
    normed1 = xhat1 * norm1_gain + norm1_bias

    act, act_slope = gelu_parts(mm(normed1.astype(BF), w_in) + ffn_bias)
    ffn = mm(act.astype(BF), w_out)

    up = adapt_up.reshape(adapters * neck, dim)
    x_ffn = ffn.astype(BF)
    down, down_slope = gelu_parts(mm(x_ffn, adapt_down))
    down_low = down.astype(BF).astype(F32)
    jq = mm(x_ffn, j_q) + j_qb
    jq_low = jq.astype(BF)
    u = mm_t(jq_low, j_k)
    big_u = mm_t(u.astype(BF), up)

    def per_adapter(values):
        return jnp.sum(values.reshape(rows, adapters, neck), axis=-1)

    def spread(values):
        return jnp.broadcast_to(values[:, :, None], (rows, adapters, neck)).reshape(rows, adapters * neck)

    fscale = 1.0 / math.sqrt(dim)
    fscores = (per_adapter(down_low * big_u) + jnp.sum(ffn * u, axis=-1, keepdims=True)) * fscale
    fscores = jnp.where(available, fscores, MASKED)
    fexp = jnp.exp(fscores - jnp.max(fscores, axis=-1, keepdims=True))
    fprobs = fexp / jnp.sum(fexp, axis=-1, keepdims=True)
    p_wide = spread(fprobs)
    mixed = ffn + mm((p_wide * down_low).astype(BF), up)
    mixed_low = mixed.astype(BF)
    xhat2, rstd2 = norm_parts(normed1 + mm(mixed_low, j_v) + j_vb)
    layer_out = (xhat2 * norm2_gain + norm2_bias).astype(BF)

    g2 = norm_back(cot, norm2_gain, xhat2, rstd2)
    g2_low = g2.astype(BF)
    w = mm_t(g2_low, j_v)
    big_w = mm_t(w.astype(BF), up)
    gvals = per_adapter(down_low * big_w) + jnp.sum(ffn * w, axis=-1, keepdims=True) + jnp.sum(g2 * j_vb, axis=-1, keepdims=True)
    gs = fprobs * (gvals - jnp.sum(gvals * fprobs, axis=-1, keepdims=True)) * fscale
    gs_wide = spread(gs)
    gs_sum = jnp.sum(gs, axis=-1, keepdims=True)
    t = mm((gs_wide * down_low).astype(BF), up) + gs_sum * ffn
    t_low = t.astype(BF)
    gq_low = mm(t_low, j_k).astype(BF)
    d_jq = t_mm(x_ffn, gq_low)
    d_jk = t_mm(t_low, jq_low)
    d_jv = t_mm(mixed_low, g2_low)
    d_qb = jnp.sum(gq_low.astype(F32), axis=0)
    d_vb = jnp.sum(g2, axis=0)
    g_down = ((gs_wide * big_u + p_wide * big_w) * down_slope).astype(BF)
    g_ffn = (gs_sum * u + w + mm_t(g_down, adapt_down) + mm_t(gq_low, j_q)).astype(BF)

    g_pre = (mm_t(g_ffn, w_out) * act_slope).astype(BF)
    g_norm1 = mm_t(g_pre, w_in) + g2
    g1 = norm_back(g_norm1, norm1_gain, xhat1, rstd1)

    g_ctx = mm_t(g1.astype(BF), w_o).astype(BF).reshape(mine, seq_len, HEADS, head_dim)
    g_probs = jnp.einsum("sqhe,skhe->shqk", g_ctx, v, preferred_element_type=F32)
    g_v = jnp.einsum("shqk,sqhe->skhe", probs_low, g_ctx, preferred_element_type=F32)
    g_scores = (probs * (g_probs - jnp.sum(g_probs * probs, axis=-1, keepdims=True))).astype(BF)
    g_q = jnp.einsum("shqk,skhe->sqhe", g_scores, k, preferred_element_type=F32) * scale
    g_k = jnp.einsum("shqk,sqhe->skhe", g_scores, q, preferred_element_type=F32) * scale
    total = g1
    for grad, weight in ((g_q, w_q), (g_k, w_k), (g_v, w_v)):
        total = total + mm_t(grad.astype(BF).reshape(rows, dim), weight)
    input_grad = total.astype(BF)

    def scatter(value):
        return lax.psum_scatter(value, ALL, scatter_dimension=0, tiled=True)

    return (
        layer_out.reshape(mine, seq_len, dim),
        input_grad.reshape(mine, seq_len, dim),
        scatter(d_jq), scatter(d_jk), scatter(d_jv), scatter(d_qb), scatter(d_vb),
    )


def solution(mesh):
    both = P(ALL, None)
    return jax.shard_map(
        shards,
        mesh=mesh,
        in_specs=(
            P("dp", None, None), P("dp"), P("dp"), P(ALL, None, None),
            P(None, "tensor"), P(None, "tensor"), P(None, "tensor"), P("tensor", None),
            P(), P(), P(None, "tensor"), P(), P("tensor", None), P(), P(), P(), P(),
            both, both, both, P(ALL), P(ALL),
        ),
        out_specs=(P(ALL, None, None), P(ALL, None, None), both, both, both, P(ALL), P(ALL)),
        check_vma=False,
    )
```

time: 1370 us -> 872 us (0.64)
  waiting for transfers between devices: 876 us -> 570 us
  matrix products: 231 us -> 101 us
  other arithmetic: 90.7 us -> 17 us
  local copies, waits for them, and re-layouts: 54.9 us -> 77 us
    reduce_scatter x9 -> x3, waiting for transfers between devices: 501 us -> 186 us  [scatter(): return lax.psum_scatter(value, ALL, scatter_dimension=0, tiled=True)]
    all_gather x7 -> x9, waiting for transfers between devices: 148 us -> 381 us  [the longest x6 259 us: gather(): lax.all_gather(part, ALL, axis=0, tiled=False)]
    psum x1 -> x0, waiting for transfers between devices: 225 us -> none  [shards(): attended = lax.psum(matmul(context_flat, att_out), 'tensor')]
    dot_general x60 -> x32, matrix products: 231 us -> 101 us  [the longest x11 40.7 us: mm_t(): lax.dot_general(left, right, (((1,), (1,)), ((), ())), preferred_element_...]
    reduce_sum x27 -> x10, other arithmetic: 59.8 us -> 7.61 us  [the longest x2 3.3 us: per_adapter(): return jnp.sum(values.reshape(rows, adapters, neck), axis=-1)]
    convert_element_type x12 -> x3, other arithmetic: 22.5 us -> 6.2 us  [the longest x1 6.19 us: shards(): (probs * (g_probs - jnp.sum(g_probs * probs, axis=-1, keepdims=True))).as...]
  transfers between devices with their start and end apart: 17 -> 12, of which waited for: 14 -> 11; matrix products, arithmetic and copies ran while one was open for 16% -> 20% of each run, Pallas kernels for 0% -> 0%
where the time goes in v1:
time: 872 us; the launch traced here: 862 us
  waiting for transfers between devices  570 us (65%)
  matrix products  101 us (12%)
  blocking collectives  81.4 us (9%)
  local copies, waits for them, and re-layouts  77 us (9%)
  other arithmetic  17 us (2%)
  between operations  15.4 us (2%)
    all_gather x6, waiting for transfers between devices, gather(): lax.all_gather(part, ALL, axis=0, tiled=False)  259 us
    reduce_scatter x3, waiting for transfers between devices, scatter(): return lax.psum_scatter(value, ALL, scatter_dimension=0, tiled=True)  186 us
    unnamed x2, blocking collectives  81.4 us
    all_gather x1, waiting for transfers between devices, shards(): j_k = lax.all_gather(joining_key, ALL, axis=0, tiled=True)  51 us
    dot_general x11, matrix products, mm_t(): lax.dot_general(left, right, (((1,), (1,)), ((), ())), preferred_element_...  40.7 us
    dot_general x12, matrix products, mm(): return jnp.dot(left, right, preferred_element_type=F32)  39.5 us
    all_gather x1, waiting for transfers between devices, shards(): j_v = lax.all_gather(joining_value, ALL, axis=0, tiled=True)  38 us
    all_gather x1, waiting for transfers between devices, shards(): j_q = lax.all_gather(joining_query, ALL, axis=0, tiled=True)  33.6 us
  transfers between devices with their start and end apart: 12, of which 11 were waited for; matrix products, arithmetic and copies ran while one was open for 20% of the time, Pallas kernels for 0%

profile of v1, /device:TPU:0, one launch (start us, length us, event | category | flops | bytes accessed | tf_op | source)
XLA Modules:
  0.0 861.8 jit_solution(7020450692323888402)
XLA Ops:
  22.0 42.1 %all-reduce.5 = (bf16[768]{0:T(1024)(128)(2,1)S(1)}, bf16[768]{0:T(1024)(128)(2,1)S(1)}) all-reduce(bf16[768]{0:T(1024)(128)(2,1)S(1)} %dynamic-update-slice, bf16[768]{0:T(1024)(128)(2,1)S(1)} %dynamic-update-slice.1), channel_id=1, replica_groups=mesh['dp'=8,'tensor'=4] {'dp','tensor'}, use_global_device_ids=true, to_apply=%add | all-reduce | flops 1536 | bytes 6144
  65.2 3.2 all-gather.28.cloned.1.call-done
  70.8 55.0 %all-gather.24.cloned.1.call-done = bf16[3072,192]{1,0:T(8,128)(2,1)} async-done(((bf16[96,192]{1,0:T(8,128)(2,1)}), bf16[3072,192]{1,0:T(8,128)(2,1)}) %all-gather.24.cloned.1.call-update) | async-done | bytes 1179664 | tf_op jit(solution)/shard_map/all_gather | solution.py:74
  130.0 53.2 %all-gather.26.cloned.1.call-done = bf16[3072,192]{1,0:T(8,128)(2,1)} async-done(((bf16[96,192]{1,0:T(8,128)(2,1)}), bf16[3072,192]{1,0:T(8,128)(2,1)}) %all-gather.26.cloned.1.call-update) | async-done | bytes 1179664 | tf_op jit(solution)/shard_map/all_gather | solution.py:74
  187.4 53.1 %all-gather.22.cloned.1.call-done = bf16[3072,192]{1,0:T(8,128)(2,1)} async-done(((bf16[96,192]{1,0:T(8,128)(2,1)}), bf16[3072,192]{1,0:T(8,128)(2,1)}) %all-gather.22.cloned.1.call-update) | async-done | bytes 1179664 | tf_op jit(solution)/shard_map/all_gather | solution.py:74
  253.1 3.1 convolution_convert_fusion.4
  267.3 38.3 %all-gather.30.cloned.1.call-done = bf16[3072,768]{1,0:T(8,128)(2,1)} async-done(((bf16[96,768]{1,0:T(8,128)(2,1)}), bf16[3072,768]{1,0:T(8,128)(2,1)}) %all-gather.30.cloned.1.call-update) | async-done | bytes 4718608 | tf_op jit(solution)/shard_map/all_gather | solution.py:74
  305.6 6.0 copy.118
  311.6 3.1 copy.146
  314.7 55.9 %all-gather.32.cloned.1.call-done = bf16[3072,768]{1,0:T(8,128)(2,1)} async-done(((bf16[96,768]{1,0:T(8,128)(2,1)}), bf16[3072,768]{1,0:T(8,128)(2,1)}) %all-gather.32.cloned.1.call-update) | async-done | bytes 4718608 | tf_op jit(solution)/shard_map/all_gather | solution.py:74
  379.8 13.0 %fusion.8 = f32[512,768]{1,0:T(8,128)S(1)} fusion(bf16[3072,768]{1,0:T(8,128)(2,1)S(1)} %bitcast.147, f32[512,3072]{1,0:T(8,128)S(1)} %fusion.40, f32[3072]{0:T(1024)S(1)} %copy-done.40), kind=kOutput, calls=%fused_computation.15 | convolution fusion | flops 2425356288 | bytes 12595200 | tf_op jit(solution)/shard_map/dot_general | solution.py:17
  392.8 33.6 %all-gather.16.cloned.1.call-done = bf16[768,768]{1,0:T(8,128)(2,1)} async-done(((bf16[24,768]{1,0:T(8,128)(2,1)}), bf16[768,768]{1,0:T(8,128)(2,1)}) %all-gather.16.cloned.1.call-update) | async-done | bytes 1179664 | tf_op jit(solution)/shard_map/all_gather | solution.py:88
  431.2 51.0 %all-gather.18.cloned.1.call-done = bf16[768,768]{1,0:T(8,128)(2,1)} async-done(((bf16[24,768]{1,0:T(8,128)(2,1)}), bf16[768,768]{1,0:T(8,128)(2,1)}) %all-gather.18.cloned.1.call-update) | async-done | bytes 1179664 | tf_op jit(solution)/shard_map/all_gather | solution.py:89
  496.8 3.3 add_convert_fusion.4
  500.1 38.0 %all-gather.20.cloned.1.call-done = bf16[768,768]{1,0:T(8,128)(2,1)} async-done(((bf16[24,768]{1,0:T(8,128)(2,1)}), bf16[768,768]{1,0:T(8,128)(2,1)}) %all-gather.20.cloned.1.call-update) | async-done | bytes 1179664 | tf_op jit(solution)/shard_map/all_gather | solution.py:90
  569.2 5.8 fusion.44
  576.4 4.2 add_convert_fusion.1
  580.6 13.1 %fusion.91 = (f32[512]{0:T(512)S(1)}, f32[512]{0:T(512)S(1)}, f32[512,768]{1,0:T(8,128)}) fusion(f32[512]{0:T(512)S(1)} %add_rsqrt_fusion.1, f32[512,768]{1,0:T(8,128)} %copy-done.16, f32[512]{0:T(512)S(1)} %broadcast_multiply_fusion.4, f32[768]{0:T(1024)S(1)} %copy-done.42, f32[512,768]{1,0:T(8,128)S(1)} %copy-done.4, bf16[768,3072]{1,0:T(8,128)(2,1)} %bitcast.145, ...), kind=kOutput, calls=%fused_computation.149 | convolution fusion | flops 4851891200 | bytes 21257216 | tf_op jit(solution)/shard_map/dot_general | solution.py:21
  600.4 6.6 multiply_reduce_fusion
  607.1 3.9 fusion.32
  610.9 39.3 %all-reduce.4 = (f32[768]{0:T(1024)S(1)}, f32[768]{0:T(1024)S(1)}) all-reduce(f32[768]{0:T(1024)S(1)} %get-tuple-element.37, f32[768]{0:T(1024)S(1)} %get-tuple-element.7), channel_id=11, replica_groups=mesh['dp'=8,'tensor'=4] {'dp','tensor'}, use_global_device_ids=true, to_apply=%region_24.25.clone | all-reduce | flops 1536 | bytes 12288
  652.4 6.2 multiply_convert_fusion
  668.6 82.2 %reduce-scatter.4.cloned.1.call-done = f32[24,768]{1,0:T(8,128)} async-done(((f32[768,768]{1,0:T(8,128)}), f32[24,768]{1,0:T(8,128)}) %reduce-scatter.4.cloned.1.call-update) | async-done | bytes 73744 | tf_op jit(solution)/shard_map/reduce_scatter | solution.py:184
  750.7 103.8 %reduce-scatter.6.cloned.1.call-done = f32[24,768]{1,0:T(8,128)} async-done(((f32[768,768]{1,0:T(8,128)}), f32[24,768]{1,0:T(8,128)}) %reduce-scatter.6.cloned.1.call-update) | async-done | bytes 73744 | tf_op jit(solution)/shard_map/reduce_scatter | solution.py:184
  (220 shorter events, 129.3 us)
Async XLA Ops:
  7.2 57.0 %copy-start = (bf16[8,256,768]{2,1,0:T(8,128)(2,1)S(1)}, bf16[8,256,768]{2,1,0:T(8,128)(2,1)}, u32[]{:S(2)}) copy-start(bf16[8,256,768]{2,1,0:T(8,128)(2,1)} %param.22) | copy-start | bytes 9437188
  7.2 12.7 %copy-start.43 = (s32[8]{0:T(128)S(1)}, s32[8]{0:T(128)}, u32[]{:S(2)}) copy-start(s32[8]{0:T(128)} %param.23) | copy-start | bytes 100
  7.2 12.8 %copy-start.44 = (s32[8]{0:T(128)S(1)}, s32[8]{0:T(128)}, u32[]{:S(2)}) copy-start(s32[8]{0:T(128)} %param.24) | copy-start | bytes 100
  7.2 12.9 %copy-start.38 = (f32[768]{0:T(1024)S(1)}, f32[768]{0:T(1024)}, u32[]{:S(2)}) copy-start(f32[768]{0:T(1024)} %param.37) | copy-start | bytes 9220
  7.2 14.3 %copy-start.45 = (bf16[24]{0:T(256)(128)(2,1)S(1)}, bf16[24]{0:T(256)(128)(2,1)}, u32[]{:S(2)}) copy-start(bf16[24]{0:T(256)(128)(2,1)} %param.42) | copy-start | bytes 148
  7.2 14.5 %copy-start.46 = (bf16[24]{0:T(256)(128)(2,1)S(1)}, bf16[24]{0:T(256)(128)(2,1)}, u32[]{:S(2)}) copy-start(bf16[24]{0:T(256)(128)(2,1)} %param.43) | copy-start | bytes 148
  7.2 61.2 %all-gather.28.cloned.1.call-start = ((), (), s32[]{:S(2)}) async-start(), calls=%async_computation.12 | async-start | bytes 1216512 | tf_op jit(solution)/shard_map/all_gather | solution.py:74
  8.9 116.9 %all-gather.24.cloned.1.call-start = ((), (), s32[]{:S(2)}) async-start(), calls=%async_computation.10 | async-start | bytes 1622016 | tf_op jit(solution)/shard_map/all_gather | solution.py:74
  10.6 172.5 %all-gather.26.cloned.1.call-start = ((), (), s32[]{:S(2)}) async-start(), calls=%async_computation.11 | async-start | bytes 1622016 | tf_op jit(solution)/shard_map/all_gather | solution.py:74
  12.4 228.0 %all-gather.22.cloned.1.call-start = ((), (), s32[]{:S(2)}) async-start(), calls=%async_computation.9 | async-start | bytes 1622016 | tf_op jit(solution)/shard_map/all_gather | solution.py:74
  14.2 291.4 %all-gather.30.cloned.1.call-start = ((), (), s32[]{:S(2)}) async-start(), calls=%async_computation.13 | async-start | bytes 4866048 | tf_op jit(solution)/shard_map/all_gather | solution.py:74
  15.9 354.7 %all-gather.32.cloned.1.call-start = ((), (), s32[]{:S(2)}) async-start(), calls=%async_computation.14 | async-start | bytes 4866048 | tf_op jit(solution)/shard_map/all_gather | solution.py:74
  17.6 408.8 %all-gather.16.cloned.1.call-start = ((), (), s32[]{:S(2)}) async-start(), calls=%async_computation.3 | async-start | bytes 1216512 | tf_op jit(solution)/shard_map/all_gather | solution.py:88
  18.3 463.9 %all-gather.18.cloned.1.call-start = ((), (), s32[]{:S(2)}) async-start(), calls=%async_computation.4 | async-start | bytes 1216512 | tf_op jit(solution)/shard_map/all_gather | solution.py:89
  19.1 519.1 %all-gather.20.cloned.1.call-start = ((), (), s32[]{:S(2)}) async-start(), calls=%async_computation.5 | async-start | bytes 1216512 | tf_op jit(solution)/shard_map/all_gather | solution.py:90
  19.8 648.8 %reduce-scatter.8.cloned.1.call-start = ((), (), s32[]{:S(2)}) async-start(), calls=%async_computation.8 | async-start | bytes 2433024 | tf_op jit(solution)/shard_map/reduce_scatter | solution.py:184
  247.1 10.7 %copy-start.14 = (bf16[2,256,12,64]{1,0,3,2:T(2,128)(2,1)}, bf16[2,256,12,64]{1,0,3,2:T(2,128)(2,1)S(1)}, u32[]{:S(2)}) copy-start(bf16[2,256,12,64]{1,0,3,2:T(2,128)(2,1)S(1)} %reshape.606) | copy-start | bytes 2359300
  266.9 106.6 %copy-start.16 = (f32[512,768]{1,0:T(8,128)}, f32[512,768]{1,0:T(8,128)S(1)}, u32[]{:S(2)}) copy-start(f32[512,768]{1,0:T(8,128)S(1)} %get-tuple-element.24) | copy-start | bytes 4718596
  392.8 36.5 %copy-start.26 = (bf16[768,768]{1,0:T(8,128)(2,1)S(1)}, bf16[768,768]{1,0:T(8,128)(2,1)}, u32[]{:S(2)}) copy-start(bf16[768,768]{1,0:T(8,128)(2,1)} %param.35) | copy-start | bytes 3538948
  431.2 53.6 %copy-start.2 = (bf16[16,48,768]{2,1,0:T(8,128)(2,1)S(1)}, bf16[16,48,768]{2,1,0:T(8,128)(2,1)}, u32[]{:S(2)}) copy-start(bf16[16,48,768]{2,1,0:T(8,128)(2,1)} %param.36) | copy-start | bytes 3538948
  547.9 202.8 %reduce-scatter.4.cloned.1.call-start = ((), (), s32[]{:S(2)}) async-start(), calls=%async_computation.6 | async-start | bytes 2433024 | tf_op jit(solution)/shard_map/reduce_scatter | solution.py:184
  575.0 279.5 %reduce-scatter.6.cloned.1.call-start = ((), (), s32[]{:S(2)}) async-start(), calls=%async_computation.7 | async-start | bytes 2433024 | tf_op jit(solution)/shard_map/reduce_scatter | solution.py:184
  580.6 13.1 %copy-start.17 = (f32[512,768]{1,0:T(8,128)S(1)}, f32[512,768]{1,0:T(8,128)}, u32[]{:S(2)}) copy-start(f32[512,768]{1,0:T(8,128)} %copy-done.16) | copy-start | bytes 4718596
  666.4 188.2 %copy-start.1 = (bf16[8,256,768]{2,1,0:T(8,128)(2,1)S(1)}, bf16[8,256,768]{2,1,0:T(8,128)(2,1)}, u32[]{:S(2)}) copy-start(bf16[8,256,768]{2,1,0:T(8,128)(2,1)} %param.22) | copy-start | bytes 9437188
  (36 other events, 97.5 us)
Sparse Core Ops, SparseCore 0:
  11.4 56.9 all-gather.27
  71.9 53.8 all-gather.23
  129.2 53.9 all-gather.25
  186.5 53.9 all-gather.21
  243.1 62.4 all-gather.29
  308.2 62.3 all-gather.31
  373.4 52.8 all-gather.15
  429.2 53.0 all-gather.17
  485.0 53.0 all-gather.19
  548.0 98.0 reduce-scatter.7
  652.8 97.8 reduce-scatter.3
  756.4 98.0 reduce-scatter.5

commit v2 on v1

--- a/solution.py
+++ b/solution.py
@@ -1,8 +1,11 @@
+from functools import partial
 import math
 
 import jax
 import jax.numpy as jnp
 from jax import lax
+from jax.experimental import pallas as pl
+from jax.experimental.pallas import tpu as pltpu
 from jax.sharding import PartitionSpec as P
 
 HEADS = 12
@@ -46,6 +49,120 @@
     cdf = 0.5 * (1.0 + lax.erf(pre * (1.0 / math.sqrt(2.0))))
     pdf = jnp.exp(-0.5 * pre * pre) * (1.0 / math.sqrt(2.0 * math.pi))
     return pre * cdf, cdf + pre * pdf
+
+
+CORE = [(i, i ^ 1) for i in range(8)]
+ALONG_X = [(i, i ^ 2) for i in range(8)]
+ALONG_Y = [(i, i ^ 4) for i in range(8)]
+SPLIT_XY = [(i, i ^ (4 if i & 1 else 2)) for i in range(8)]
+CROSS_XY = [(i, i ^ (3 if i & 1 else 5)) for i in range(8)]
+
+
+def send(array, pairs):
+    return lax.ppermute(array, "dp", pairs)
+
+
+def shift(array, by, groups):
+    return lax.ppermute(array, "tensor", [(i, (i + by) % groups) for i in range(groups)])
+
+
+def place_kernel(spots_ref, *refs, first_item, item_count, groups):
+    pieces, out, sems = refs[:-2], refs[-2], refs[-1]
+    copies = []
+    if first_item:
+        pieces, own = pieces[:-1], pieces[-1]
+        copies.append(pltpu.make_async_copy(own, out.at[spots_ref[8]], sems.at[0]))
+    for k, piece in enumerate(pieces):
+        for i in range(item_count):
+            plane = lax.rem(spots_ref[8] + (groups - first_item - i), groups)
+            copies.append(
+                pltpu.make_async_copy(piece.at[i], out.at[plane, spots_ref[k]], sems.at[len(copies)])
+            )
+    for copy in copies:
+        copy.start()
+    for copy in copies:
+        copy.wait()
+
+
+def place(pieces, own, spots, groups):
+    item_count = pieces[0].shape[0]
+    first_item = 0 if own is None else 1
+    arrays = list(pieces) + ([] if own is None else [own])
+    return pl.pallas_call(
+        partial(place_kernel, first_item=first_item, item_count=item_count, groups=groups),
+        out_shape=jax.ShapeDtypeStruct((groups, 8) + pieces[0].shape[1:], BF),
+        in_specs=[pl.BlockSpec(memory_space=pltpu.SMEM)] + [pl.BlockSpec(memory_space=pl.ANY)] * len(arrays),
+        out_specs=pl.BlockSpec(memory_space=pltpu.VMEM),
+        scratch_shapes=[pltpu.SemaphoreType.DMA((8 * item_count + first_item,))],
+        compiler_params=pltpu.CompilerParams(vmem_limit_bytes=32 * 2**20),
+    )(spots, *arrays)
+
+
+class Gather:
+    def __init__(self, dp_size, groups, my_d, my_z):
+        self.dp_size, self.groups, self.my_d, self.my_z = dp_size, groups, my_d, my_z
+        self.paired = dp_size == 8 and groups == 4
+        core = lax.rem(my_d, 2)
+        even = [0, 1, 2, 3, 7, 5, 4, 6]
+        odd = [0, 1, 4, 5, 7, 3, 2, 6]
+        flips = jnp.where(core == 0, jnp.array(even, jnp.int32), jnp.array(odd, jnp.int32))
+        self.spots = jnp.concatenate([jnp.bitwise_xor(my_d, flips), my_z[None]]).astype(jnp.int32)
+
+    def spread(self, items):
+        other = send(items, CORE)
+        near0, near1 = send(items, SPLIT_XY), send(other, SPLIT_XY)
+        far = send(near0, CROSS_XY)
+        return [items, other, near0, near1, far, send(near0, CORE), send(near1, CORE), send(far, CORE)]
+
+    def frozen(self, shard):
+        rows = shard.shape[0] // self.dp_size
+        part = lax.dynamic_slice_in_dim(shard, self.my_d * rows, rows, 0)
+        if not self.paired:
+            return lax.all_gather(part, ("dp", "tensor"), axis=0).reshape(
+                (self.dp_size, self.groups) + part.shape
+            ).transpose(1, 0, 2, 3)
+        items = jnp.stack([shift(part, i, self.groups) for i in range(1, self.groups)])
+        return place(self.spread(items), shard.reshape(self.dp_size, rows, -1), self.spots, self.groups)
+
+    def joining(self, part):
+        if not self.paired:
+            return lax.all_gather(part, ("dp", "tensor"), axis=0).reshape(
+                (self.dp_size, self.groups) + part.shape
+            ).transpose(1, 0, 2, 3)
+        items = jnp.stack([part] + [shift(part, i, self.groups) for i in range(1, self.groups)])
+        return place(self.spread(items), None, self.spots, self.groups)
+
+
+def reduce_grads(grads, dp_size, groups, my_d, my_z, own_rows):
+    part = own_rows * groups
+    dim = grads.shape[-1]
+    if dp_size == 8 and groups == 4:
+        core, quarter = lax.rem(my_d, 2), my_d // 2
+        by_core = grads.reshape(4, 2, *grads.shape[1:])
+        away = lax.dynamic_index_in_dim(by_core, 1 - core, 1, keepdims=False).astype(BF)
+        half = lax.dynamic_index_in_dim(by_core, core, 1, keepdims=False)
+        half = half + send(away, CORE).astype(F32)
+
+        def block(flip):
+            return lax.dynamic_index_in_dim(half, jnp.bitwise_xor(quarter, flip), 0, keepdims=False)
+
+        passed = send(block(3).astype(BF), SPLIT_XY).astype(F32)
+        to_x = block(1) + jnp.where(core == 1, passed, 0.0)
+        to_y = block(2) + jnp.where(core == 0, passed, 0.0)
+        total = block(0) + send(to_x.astype(BF), ALONG_X).astype(F32) + send(to_y.astype(BF), ALONG_Y).astype(F32)
+    else:
+        total = lax.psum_scatter(grads, "dp", scatter_dimension=0, tiled=False)
+    mats = total[: 3 * part].reshape(3, groups, own_rows, dim).transpose(1, 0, 2, 3).reshape(groups, 3 * own_rows, dim)
+    extra = jnp.pad(total[3 * part : 3 * part + groups][:, None, :], ((0, 0), (0, 7), (0, 0)))
+    blocks = jnp.concatenate([mats, extra], axis=1)
+    if dp_size == 8 and groups == 4:
+        mine = lax.dynamic_index_in_dim(blocks, my_z, 0, keepdims=False)
+        for i in range(1, groups):
+            goes = lax.dynamic_index_in_dim(blocks, lax.rem(my_z + i, groups), 0, keepdims=False)
+            mine = mine + shift(goes.astype(BF), i, groups).astype(F32)
+    else:
+        mine = lax.psum_scatter(blocks, "tensor", scatter_dimension=0, tiled=False)
+    return mine[: 3 * own_rows].reshape(3, own_rows, dim), mine[3 * own_rows]
 
 
 def shards(
@@ -66,30 +183,31 @@
     def my_slice(array):
         return lax.dynamic_slice_in_dim(array, t_rank * mine, mine, 0)
 
-    def my_part(weight):
-        part = weight.shape[0] // dp_size
-        return lax.dynamic_slice_in_dim(weight, d_rank * part, part, 0)
-
-    def gather(part):
-        return lax.all_gather(part, ALL, axis=0, tiled=False).reshape((dp_size, groups) + part.shape)
-
-    def cols_whole(weight):
-        g = gather(my_part(weight))
-        return g.transpose(0, 2, 1, 3).reshape(weight.shape[0], groups * weight.shape[1])
-
-    def rows_whole(weight):
-        g = gather(my_part(weight))
-        return g.transpose(1, 0, 2, 3).reshape(groups * weight.shape[0], weight.shape[1])
-
-    w_q, w_k, w_v = cols_whole(att_query), cols_whole(att_key), cols_whole(att_value)
-    w_o = rows_whole(att_out)
-    w_in = cols_whole(ffn_in)
-    w_out = rows_whole(ffn_out)
-    j_q = lax.all_gather(joining_query, ALL, axis=0, tiled=True)
-    j_k = lax.all_gather(joining_key, ALL, axis=0, tiled=True)
-    j_v = lax.all_gather(joining_value, ALL, axis=0, tiled=True)
-    j_qb = lax.all_gather(joining_qbias, ALL, axis=0, tiled=True).astype(F32)
-    j_vb = lax.all_gather(joining_vbias, ALL, axis=0, tiled=True).astype(F32)
+    my_z, my_d = t_rank, d_rank
+    att_pack = jnp.concatenate([att_query.T, att_key.T, att_value.T, att_out], axis=0)
+    gather = Gather(dp_size, groups, my_d, my_z)
+    att_all = gather.frozen(att_pack)
+    in_all = gather.frozen(ffn_in)
+    out_all = gather.frozen(ffn_out)
+    own_rows = joining_query.shape[0]
+    bias_row = jnp.zeros((8, dim), BF)
+    bias_row = bias_row.at[0, :own_rows].set(joining_qbias).at[0, own_rows : 2 * own_rows].set(joining_vbias)
+    join_all = gather.joining(jnp.concatenate([joining_query, joining_key, joining_value, bias_row], axis=0))
+
+    att_all = att_all.reshape(groups, 4, dim // groups, dim)
+    w_q, w_k, w_v, w_o = (att_all[:, i].reshape(dim, dim) for i in range(4))
+    w_q, w_k, w_v = w_q.T, w_k.T, w_v.T
+    w_in = in_all.reshape(groups, dim, -1).transpose(1, 0, 2).reshape(dim, -1)
+    w_out = out_all.reshape(-1, dim)
+    join_all = join_all.transpose(1, 0, 2, 3)
+
+    def joined(lo, hi):
+        return join_all[:, :, lo:hi].reshape(-1, dim)
+
+    j_q, j_k, j_v = (joined(i * own_rows, (i + 1) * own_rows) for i in range(3))
+    biases = join_all[:, :, 3 * own_rows, : 2 * own_rows].astype(F32)
+    j_qb = biases[:, :, :own_rows].reshape(-1)
+    j_vb = biases[:, :, own_rows:].reshape(-1)
 
     x_low = my_slice(tokens).reshape(rows, dim)
     x_mine = x_low.astype(F32)
@@ -180,13 +298,21 @@
         total = total + mm_t(grad.astype(BF).reshape(rows, dim), weight)
     input_grad = total.astype(BF)
 
-    def scatter(value):
-        return lax.psum_scatter(value, ALL, scatter_dimension=0, tiled=True)
-
+    part = dim // dp_size
+    bias_grads = jnp.stack([d_qb.reshape(dp_size, groups, own_rows), d_vb.reshape(dp_size, groups, own_rows)], axis=2)
+    bias_grads = jnp.pad(
+        bias_grads.reshape(dp_size, groups, 2 * own_rows), ((0, 0), (0, 16 - groups), (0, dim - 2 * own_rows))
+    )
+    grads = jnp.concatenate(
+        [d_jq.reshape(dp_size, part, dim), d_jk.reshape(dp_size, part, dim), d_jv.reshape(dp_size, part, dim), bias_grads],
+        axis=1,
+    )
+    mats, bias_sum = reduce_grads(grads, dp_size, groups, my_d, my_z, own_rows)
     return (
         layer_out.reshape(mine, seq_len, dim),
         input_grad.reshape(mine, seq_len, dim),
-        scatter(d_jq), scatter(d_jk), scatter(d_jv), scatter(d_qb), scatter(d_vb),
+        mats[0], mats[1], mats[2],
+        bias_sum[:own_rows], bias_sum[own_rows : 2 * own_rows],
     )
 
 

time: 872 us -> 298 us (0.34)
  waiting for transfers between devices: 570 us -> 58 us
  blocking collectives: 81.4 us -> 0 us
  starting transfers between devices: 0.7 us -> 50.9 us
  matrix products: 101 us -> 73.5 us
  Pallas kernels: 0 us -> 14.2 us
  between operations: 15.4 us -> 2.1 us
  local copies, waits for them, and re-layouts: 77 us -> 64.5 us
  other arithmetic: 17 us -> 29.3 us
    all_gather x9 -> x0, waiting for transfers between devices: 381 us -> none  [the longest x6 259 us: gather(): lax.all_gather(part, ALL, axis=0, tiled=False)]
    reduce_scatter x3 -> x0, waiting for transfers between devices: 186 us -> none  [scatter(): return lax.psum_scatter(value, ALL, scatter_dimension=0, tiled=True)]
    unnamed x2 -> x0, blocking collectives: 81.4 us -> none
    ppermute x0 -> x47, waiting for transfers between devices: none -> 58 us  [the longest x32 39.5 us: send(): return lax.ppermute(array, 'dp', pairs)]
    ppermute x0 -> x47, starting transfers between devices: none -> 50.9 us  [the longest x15 30.1 us: shift(): lax.ppermute(array, 'tensor', [(i, (i + by) % groups) for i in range(grou...]
    dot_general x12, matrix products: 39.5 us -> 21.8 us  [mm(): return jnp.dot(left, right, preferred_element_type=F32)]
    pallas_call x0 -> x4, Pallas kernels: none -> 14.2 us  [place(): pl.pallas_call(partial(place_kernel, first_item=first_item, item_count=it...]
    dot_general x11, matrix products: 40.7 us -> 29.7 us  [mm_t(): lax.dot_general(left, right, (((1,), (1,)), ((), ())), preferred_element_...]
  transfers between devices with their start and end apart: 12 -> 47, of which waited for: 11 -> 12; matrix products, arithmetic and copies ran while one was open for 20% -> 22% of each run, Pallas kernels for 0% -> 4%
where the time goes in v2:
time: 298 us; the launch traced here: 292 us
  matrix products  73.5 us (25%)
  local copies, waits for them, and re-layouts  64.5 us (22%)
  waiting for transfers between devices  58 us (19%)
  starting transfers between devices  50.9 us (17%)
  other arithmetic  29.3 us (10%)
  Pallas kernels  14.2 us (5%)
    ppermute x32, waiting for transfers between devices, send(): return lax.ppermute(array, 'dp', pairs)  39.5 us
    ppermute x15, starting transfers between devices, shift(): lax.ppermute(array, 'tensor', [(i, (i + by) % groups) for i in range(grou...  30.1 us
    dot_general x11, matrix products, mm_t(): lax.dot_general(left, right, (((1,), (1,)), ((), ())), preferred_element_...  29.7 us
    dot_general x12, matrix products, mm(): return jnp.dot(left, right, preferred_element_type=F32)  21.8 us
    ppermute x32, starting transfers between devices, send(): return lax.ppermute(array, 'dp', pairs)  20.8 us
    ppermute x15, waiting for transfers between devices, shift(): lax.ppermute(array, 'tensor', [(i, (i + by) % groups) for i in range(grou...  18.6 us
    unnamed x162, local copies, waits for them, and re-layouts  17.9 us
    pallas_call x4, Pallas kernels, place(): pl.pallas_call(partial(place_kernel, first_item=first_item, item_count=it...  14.2 us
  transfers between devices with their start and end apart: 47, of which 12 were waited for; matrix products, arithmetic and copies ran while one was open for 22% of the time, Pallas kernels for 4%

profile of v2, /device:TPU:0, one launch (start us, length us, event | category | flops | bytes accessed | tf_op | source)
XLA Modules:
  0.0 292.4 jit_solution(7394579276322438764)
XLA Ops:
  2.4 5.0 %collective-permute-start.22 = (bf16[96,768]{1,0:T(8,128)(2,1)}, bf16[96,768]{1,0:T(8,128)(2,1)}, u32[]{:S(2)}, u32[]{:S(2)}) collective-permute-start(bf16[96,768]{1,0:T(8,128)(2,1)} %constant_dynamic-slice_fusion), channel_id=1, source_target_pairs={{0,3},{1,0},{2,1},{3,2},{4,7},{5,4},{6,5},{7,6},{8,11},{9,8},{10,9... | collective-permute-start | bytes 442376 | tf_op jit(solution)/shard_map/ppermute | solution.py:66
  24.1 3.8 %collective-permute-start.2 = (bf16[96,768]{1,0:T(8,128)(2,1)}, bf16[96,768]{1,0:T(8,128)(2,1)S(1)}, u32[]{:S(2)}, u32[]{:S(2)}) collective-permute-start(bf16[96,768]{1,0:T(8,128)(2,1)} %constant_dynamic-slice_fusion.2), channel_id=1, source_target_pairs={{0,3},{1,0},{2,1},{3,2},{4,7},{5,4},{6,5},{7,6},{8,11},{9,8},{10,9... | collective-permute-start | bytes 442376 | tf_op jit(solution)/shard_map/ppermute | solution.py:66
  31.6 8.3 %collective-permute-done.11 = bf16[96,768]{1,0:T(8,128)(2,1)S(1)} collective-permute-done((bf16[96,768]{1,0:T(8,128)(2,1)}, bf16[96,768]{1,0:T(8,128)(2,1)S(1)}, u32[]{:S(2)}, u32[]{:S(2)}) %collective-permute-start.11) | collective-permute-done | bytes 147488 | tf_op jit(solution)/shard_map/ppermute | solution.py:66
  40.6 3.6 %collective-permute-start.31 = (bf16[80,768]{1,0:T(8,128)(2,1)S(1)}, bf16[80,768]{1,0:T(8,128)(2,1)S(1)}, u32[]{:S(2)}, u32[]{:S(2)}) collective-permute-start(bf16[80,768]{1,0:T(8,128)(2,1)S(1)} %get-tuple-element.59), channel_id=1, source_target_pairs={{0,2},{1,3},{2,0},{3,1},{4,6},{5,7},{6,4},{7,5},{8,10},{9,11},{10,... | collective-permute-start | bytes 368648 | tf_op jit(solution)/shard_map/ppermute | solution.py:66
  44.2 3.1 %collective-permute-done.32 = bf16[80,768]{1,0:T(8,128)(2,1)S(1)} collective-permute-done((bf16[80,768]{1,0:T(8,128)(2,1)S(1)}, bf16[80,768]{1,0:T(8,128)(2,1)S(1)}, u32[]{:S(2)}, u32[]{:S(2)}) %collective-permute-start.32) | collective-permute-done | bytes 122912 | tf_op jit(solution)/shard_map/ppermute | solution.py:66
  47.3 7.4 %collective-permute-start.30 = (bf16[80,768]{1,0:T(8,128)(2,1)S(1)}, bf16[80,768]{1,0:T(8,128)(2,1)S(1)}, u32[]{:S(2)}, u32[]{:S(2)}) collective-permute-start(bf16[80,768]{1,0:T(8,128)(2,1)S(1)} %get-tuple-element.59), channel_id=1, source_target_pairs={{0,1},{1,2},{2,3},{3,0},{4,5},{5,6},{6,7},{7,4},{8,9},{9,10},{10,1... | collective-permute-start | bytes 368648 | tf_op jit(solution)/shard_map/ppermute | solution.py:66
  71.2 11.6 %collective-permute-done.4.refs_2_ = bf16[3,96,768]{2,1,0:T(8,128)(2,1)} collective-permute-done((bf16[3,96,768]{2,1,0:T(8,128)(2,1)}, bf16[3,96,768]{2,1,0:T(8,128)(2,1)}, u32[]{:S(2)}, u32[]{:S(2)}) %collective-permute-start.4) | collective-permute-done | bytes 442400 | tf_op jit(solution)/shard_map/ppermute | solution.py:62
  88.2 8.6 %collective-permute-done.5.refs_3_ = bf16[3,96,768]{2,1,0:T(8,128)(2,1)} collective-permute-done((bf16[3,96,768]{2,1,0:T(8,128)(2,1)}, bf16[3,96,768]{2,1,0:T(8,128)(2,1)}, u32[]{:S(2)}, u32[]{:S(2)}) %collective-permute-start.5) | collective-permute-done | bytes 442400 | tf_op jit(solution)/shard_map/ppermute | solution.py:62
  101.4 3.5 %shard_map.280 = bf16[4,8,96,768]{3,2,1,0:T(8,128)(2,1)S(1)} custom-call(s32[9]{0:T(128)S(1)} %pad_add_fusion.spots_ref, bf16[3,96,768]{2,1,0:T(8,128)(2,1)S(1)} %copy-done.9, bf16[3,96,768]{2,1,0:T(8,128)(2,1)} %collective-permute-done.13.refs_1_, bf16[3,96,768]{2,1,0:T(8,128)(2,1)} %collective-permute-done.14.refs_2_, ...), custom_call_target="tpu_custom_call" | custom-call | tf_op jit(solution)/shard_map/pallas_call | solution.py:91
  107.1 6.7 %copy.92 = bf16[4,768,768]{1,2,0:T(8,128)(2,1)} copy(bf16[4,768,768]{2,1,0:T(8,128)(2,1)} %bitcast.186) | data formatting | bytes 9437184 | tf_op jit(solution)/shard_map/reshape | solution.py:200
  116.7 3.1 %shard_map.279 = bf16[4,8,96,768]{3,2,1,0:T(8,128)(2,1)S(1)} custom-call(s32[9]{0:T(128)S(1)} %pad_add_fusion.spots_ref, bf16[3,96,768]{2,1,0:T(8,128)(2,1)} %pad_maximum_fusion.3.refs_0_, bf16[3,96,768]{2,1,0:T(8,128)(2,1)} %collective-permute-done.3.refs_1_, bf16[3,96,768]{2,1,0:T(8,128)(2,1)} %collective-permute-done.4.refs_2_, ...), custom_call_target="tpu_custom_call" | custom-call | tf_op jit(solution)/shard_map/pallas_call | solution.py:91
  146.4 3.9 %shard_map.281 = bf16[4,8,96,768]{3,2,1,0:T(8,128)(2,1)S(1)} custom-call(s32[9]{0:T(128)S(1)} %pad_add_fusion.spots_ref, bf16[3,96,768]{2,1,0:T(8,128)(2,1)S(1)} %copy-done.7, bf16[3,96,768]{2,1,0:T(8,128)(2,1)S(1)} %copy-done.13, bf16[3,96,768]{2,1,0:T(8,128)(2,1)} %collective-permute-done.24.refs_2_, bf16[3,96,768]{2,1,0:T(8,128)(2,1)} %collective-permute-done.25.refs_3_, ...), custom_call_target="tpu_custom_call" | custom-call | tf_op jit(solution)/shard_map/pallas_call | solution.py:91
  150.4 3.1 %fusion.8 = f32[512,768]{1,0:T(8,128)S(1)} fusion(bf16[3072,768]{1,0:T(8,128)(2,1)S(1)} %bitcast.190, f32[512,3072]{1,0:T(8,128)S(1)} %fusion.46, f32[3072]{0:T(1024)S(1)} %copy-done.68), kind=kOutput, calls=%fused_computation.18 | convolution fusion | flops 2425356288 | bytes 12595200 | tf_op jit(solution)/shard_map/dot_general | solution.py:20
  155.5 3.6 %shard_map.282 = bf16[4,8,80,768]{3,2,1,0:T(8,128)(2,1)S(1)} custom-call(s32[9]{0:T(128)S(1)} %pad_add_fusion.spots_ref, bf16[4,80,768]{2,1,0:T(8,128)(2,1)} %pad_maximum_fusion.2.refs_0_, bf16[4,80,768]{2,1,0:T(8,128)(2,1)} %collective-permute-done.33.refs_1_, bf16[4,80,768]{2,1,0:T(8,128)(2,1)} %collective-permute-done.34.refs_2_, ...), custom_call_target="tpu_custom_call" | custom-call | tf_op jit(solution)/shard_map/pallas_call | solution.py:91
  171.1 3.1 %copy.96 = f32[512,768]{0,1:T(8,128)} copy(f32[512,768]{1,0:T(8,128)} %get-tuple-element.38) | data formatting | bytes 3145728 | tf_op jit(solution)/shard_map/mul | solution.py:257
  177.3 3.0 %copy.97 = f32[512,768]{1,0:T(8,128)} copy(f32[512,768]{0,1:T(8,128)} %bitcast.204) | data formatting | bytes 3145728 | tf_op jit(solution)/shard_map/reshape | solution.py:254
  200.2 3.1 %copy.101 = f32[512,768]{1,0:T(8,128)} copy(f32[512,768]{0,1:T(8,128)} %bitcast.203) | data formatting | bytes 3145728 | tf_op jit(solution)/shard_map/reshape | solution.py:254
  216.7 12.9 %fusion.108 = (f32[512]{0:T(512)S(1)}, f32[512]{0:T(512)S(1)}, f32[512,768]{1,0:T(8,128)}) fusion(f32[512]{0:T(512)S(1)} %add_rsqrt_fusion.1, f32[512,768]{1,0:T(8,128)} %copy-done.35, f32[512]{0:T(512)S(1)} %broadcast_multiply_fusion.4, f32[768]{0:T(1024)S(1)} %copy-done.70, f32[512,768]{1,0:T(8,128)S(1)} %copy-done.19, bf16[768,3072]{0,1:T(8,128)(2,1)} %bitcast.209, ...), kind=kOutput, calls=%fused_computation.190 | convolution fusion | flops 4851891200 | bytes 21257216 | tf_op jit(solution)/shard_map/dot_general | solution.py:24
  233.8 7.1 %multiply_reduce_fusion = (f32[2,12,256]{2,1,0:T(8,128)S(1)}, f32[2,12,256,256]{2,3,1,0:T(8,128)}) fusion(f32[2,12,256,256]{2,3,1,0:T(8,128)} %copy-done.39, f32[2,12,256]{2,1,0:T(8,128)S(1)} %get-tuple-element.64, bf16[2,256,12,64]{1,0,3,2:T(2,128)(2,1)S(1)} %copy-done.57, bf16[2,256,12,64]{1,0,3,2:T(2,128)(2,1)} %reshape.716), kind=kOutput, calls=%fused_computation.10 | convolution fusion | flops 206039040 | bytes 14204928 | tf_op jit(solution)/shard_map/sqhe,skhe->shqk/dot_general | solution.py:291
  245.7 4.4 %fusion.33 = bf16[2,256,12,64]{1,3,2,0:T(8,128)(2,1)S(1)} fusion(bf16[2,256,12,64]{1,0,3,2:T(2,128)(2,1)S(1)} %copy-done.60, f32[2,12,256,256]{2,3,1,0:T(8,128)} %copy-done.39, f32[2,12,256]{2,1,0:T(8,128)S(1)} %get-tuple-element.64), kind=kOutput, calls=%fused_computation.78 | convolution fusion | flops 204865536 | bytes 7888896 | tf_op jit(solution)/shard_map/shqk,sqhe->skhe/dot_general | solution.py:292
  250.1 4.3 %multiply_convert_fusion = bf16[2,12,256,256]{2,3,1,0:T(8,128)(2,1)S(1)} fusion(f32[2,12,256,256]{2,3,1,0:T(8,128)} %get-tuple-element.79, f32[2,12,256]{2,1,0:T(8,128)S(1)} %get-tuple-element.78, f32[2,12,256,256]{2,3,1,0:T(8,128)S(1)} %bitcast.206, f32[2,12,256]{2,1,0:T(8,128)S(1)} %get-tuple-element.64), kind=kLoop, calls=%fused_computation.9 | loop fusion | flops 6291456 | bytes 15777792 | tf_op jit(solution)/shard_map/convert_element_type | solution.py:293
  261.1 4.1 %collective-permute-done.41 = bf16[304,768]{1,0:T(8,128)(2,1)S(1)} collective-permute-done((bf16[304,768]{1,0:T(8,128)(2,1)S(1)}, bf16[304,768]{1,0:T(8,128)(2,1)S(1)}, u32[]{:S(2)}, u32[]{:S(2)}) %collective-permute-start.41) | collective-permute-done | bytes 466976 | tf_op jit(solution)/shard_map/ppermute | solution.py:62
  272.5 5.2 %collective-permute-done.43 = bf16[304,768]{1,0:T(8,128)(2,1)S(1)} collective-permute-done((bf16[304,768]{1,0:T(8,128)(2,1)S(1)}, bf16[304,768]{1,0:T(8,128)(2,1)S(1)}, u32[]{:S(2)}, u32[]{:S(2)}) %collective-permute-start.43) | collective-permute-done | bytes 466976 | tf_op jit(solution)/shard_map/ppermute | solution.py:62
  285.7 5.2 %collective-permute-done.45 = bf16[80,768]{1,0:T(8,128)(2,1)S(1)} collective-permute-done((bf16[80,768]{1,0:T(8,128)(2,1)S(1)}, bf16[80,768]{1,0:T(8,128)(2,1)S(1)}, u32[]{:S(2)}, u32[]{:S(2)}) %collective-permute-start.45) | collective-permute-done | bytes 122912 | tf_op jit(solution)/shard_map/ppermute | solution.py:66
  (364 shorter events, 162.4 us)
Async XLA Ops:
  2.4 20.8 %collective-permute-start.22 = (bf16[96,768]{1,0:T(8,128)(2,1)}, bf16[96,768]{1,0:T(8,128)(2,1)}, u32[]{:S(2)}, u32[]{:S(2)}) collective-permute-start(bf16[96,768]{1,0:T(8,128)(2,1)} %constant_dynamic-slice_fusion), channel_id=1, source_target_pairs={{0,3},{1,0},{2,1},{3,2},{4,7},{5,4},{6,5},{7,6},{8,11},{9,8},{10,9... | collective-permute-start | bytes 442376 | tf_op jit(solution)/shard_map/ppermute | solution.py:66
  7.5 16.6 %collective-permute-start.21 = (bf16[96,768]{1,0:T(8,128)(2,1)}, bf16[96,768]{1,0:T(8,128)(2,1)}, u32[]{:S(2)}, u32[]{:S(2)}) collective-permute-start(bf16[96,768]{1,0:T(8,128)(2,1)} %constant_dynamic-slice_fusion), channel_id=1, source_target_pairs={{0,2},{1,3},{2,0},{3,1},{4,6},{5,7},{6,4},{7,5},{8,10},{9,11},{10,... | collective-permute-start | bytes 442376 | tf_op jit(solution)/shard_map/ppermute | solution.py:66
  7.5 20.5 %collective-permute-start.20 = (bf16[96,768]{1,0:T(8,128)(2,1)}, bf16[96,768]{1,0:T(8,128)(2,1)}, u32[]{:S(2)}, u32[]{:S(2)}) collective-permute-start(bf16[96,768]{1,0:T(8,128)(2,1)} %constant_dynamic-slice_fusion), channel_id=1, source_target_pairs={{0,1},{1,2},{2,3},{3,0},{4,5},{5,6},{6,7},{7,4},{8,9},{9,10},{10,1... | collective-permute-start | bytes 442376 | tf_op jit(solution)/shard_map/ppermute | solution.py:66
  10.1 20.4 %collective-permute-start.12 = (bf16[96,768]{1,0:T(8,128)(2,1)}, bf16[96,768]{1,0:T(8,128)(2,1)S(1)}, u32[]{:S(2)}, u32[]{:S(2)}) collective-permute-start(bf16[96,768]{1,0:T(8,128)(2,1)} %constant_dynamic-slice_fusion.1), channel_id=1, source_target_pairs={{0,3},{1,0},{2,1},{3,2},{4,7},{5,4},{6,5},{7,6},{8,11},{9,8},{10,9... | collective-permute-start | bytes 442376 | tf_op jit(solution)/shard_map/ppermute | solution.py:66
  12.9 27.0 %collective-permute-start.11 = (bf16[96,768]{1,0:T(8,128)(2,1)}, bf16[96,768]{1,0:T(8,128)(2,1)S(1)}, u32[]{:S(2)}, u32[]{:S(2)}) collective-permute-start(bf16[96,768]{1,0:T(8,128)(2,1)} %constant_dynamic-slice_fusion.1), channel_id=1, source_target_pairs={{0,2},{1,3},{2,0},{3,1},{4,6},{5,7},{6,4},{7,5},{8,10},{9,11},{10,... | collective-permute-start | bytes 442376 | tf_op jit(solution)/shard_map/ppermute | solution.py:66
  23.2 17.3 %collective-permute-start.10 = (bf16[96,768]{1,0:T(8,128)(2,1)}, bf16[96,768]{1,0:T(8,128)(2,1)S(1)}, u32[]{:S(2)}, u32[]{:S(2)}) collective-permute-start(bf16[96,768]{1,0:T(8,128)(2,1)} %constant_dynamic-slice_fusion.1), channel_id=1, source_target_pairs={{0,1},{1,2},{2,3},{3,0},{4,5},{5,6},{6,7},{7,4},{8,9},{9,10},{10,1... | collective-permute-start | bytes 442376 | tf_op jit(solution)/shard_map/ppermute | solution.py:66
  24.1 30.6 %collective-permute-start.2 = (bf16[96,768]{1,0:T(8,128)(2,1)}, bf16[96,768]{1,0:T(8,128)(2,1)S(1)}, u32[]{:S(2)}, u32[]{:S(2)}) collective-permute-start(bf16[96,768]{1,0:T(8,128)(2,1)} %constant_dynamic-slice_fusion.2), channel_id=1, source_target_pairs={{0,3},{1,0},{2,1},{3,2},{4,7},{5,4},{6,5},{7,6},{8,11},{9,8},{10,9... | collective-permute-start | bytes 442376 | tf_op jit(solution)/shard_map/ppermute | solution.py:66
  28.0 26.8 %collective-permute-start.1 = (bf16[96,768]{1,0:T(8,128)(2,1)}, bf16[96,768]{1,0:T(8,128)(2,1)S(1)}, u32[]{:S(2)}, u32[]{:S(2)}) collective-permute-start(bf16[96,768]{1,0:T(8,128)(2,1)} %constant_dynamic-slice_fusion.2), channel_id=1, source_target_pairs={{0,2},{1,3},{2,0},{3,1},{4,6},{5,7},{6,4},{7,5},{8,10},{9,11},{10,... | collective-permute-start | bytes 442376 | tf_op jit(solution)/shard_map/ppermute | solution.py:66
  30.5 25.9 %collective-permute-start = (bf16[96,768]{1,0:T(8,128)(2,1)}, bf16[96,768]{1,0:T(8,128)(2,1)S(1)}, u32[]{:S(2)}, u32[]{:S(2)}) collective-permute-start(bf16[96,768]{1,0:T(8,128)(2,1)} %constant_dynamic-slice_fusion.2), channel_id=1, source_target_pairs={{0,1},{1,2},{2,3},{3,0},{4,5},{5,6},{6,7},{7,4},{8,9},{9,10},{10,1... | collective-permute-start | bytes 442376 | tf_op jit(solution)/shard_map/ppermute | solution.py:66
  40.6 16.8 %collective-permute-start.31 = (bf16[80,768]{1,0:T(8,128)(2,1)S(1)}, bf16[80,768]{1,0:T(8,128)(2,1)S(1)}, u32[]{:S(2)}, u32[]{:S(2)}) collective-permute-start(bf16[80,768]{1,0:T(8,128)(2,1)S(1)} %get-tuple-element.59), channel_id=1, source_target_pairs={{0,2},{1,3},{2,0},{3,1},{4,6},{5,7},{6,4},{7,5},{8,10},{9,11},{10,... | collective-permute-start | bytes 368648 | tf_op jit(solution)/shard_map/ppermute | solution.py:66
  59.8 23.0 %collective-permute-start.33 = (bf16[4,80,768]{2,1,0:T(8,128)(2,1)}, bf16[4,80,768]{2,1,0:T(8,128)(2,1)}, u32[]{:S(2)}, u32[]{:S(2)}) collective-permute-start(bf16[4,80,768]{2,1,0:T(8,128)(2,1)} %pad_maximum_fusion.2.refs_0_), channel_id=1, source_target_pairs={{0,4},{4,0},{8,12},{12,8},{16,20},{20,16},{24,28},{28,24},{1,5},{5... | collective-permute-start | bytes 1474568 | tf_op jit(solution)/shard_map/ppermute | solution.py:62
  63.3 21.0 %collective-permute-start.34 = (bf16[4,80,768]{2,1,0:T(8,128)(2,1)}, bf16[4,80,768]{2,1,0:T(8,128)(2,1)}, u32[]{:S(2)}, u32[]{:S(2)}) collective-permute-start(bf16[4,80,768]{2,1,0:T(8,128)(2,1)} %pad_maximum_fusion.2.refs_0_), channel_id=1, source_target_pairs={{0,8},{4,20},{8,0},{12,28},{16,24},{20,4},{24,16},{28,12},{1,9},{5... | collective-permute-start | bytes 1474568 | tf_op jit(solution)/shard_map/ppermute | solution.py:62
  64.8 18.0 %collective-permute-start.4 = (bf16[3,96,768]{2,1,0:T(8,128)(2,1)}, bf16[3,96,768]{2,1,0:T(8,128)(2,1)}, u32[]{:S(2)}, u32[]{:S(2)}) collective-permute-start(bf16[3,96,768]{2,1,0:T(8,128)(2,1)} %pad_maximum_fusion.3.refs_0_), channel_id=1, source_target_pairs={{0,8},{4,20},{8,0},{12,28},{16,24},{20,4},{24,16},{28,12},{1,9},{5... | collective-permute-start | bytes 1327112 | tf_op jit(solution)/shard_map/ppermute | solution.py:62
  68.0 19.5 %collective-permute-start.15 = (bf16[3,96,768]{2,1,0:T(8,128)(2,1)}, bf16[3,96,768]{2,1,0:T(8,128)(2,1)}, u32[]{:S(2)}, u32[]{:S(2)}) collective-permute-start(bf16[3,96,768]{2,1,0:T(8,128)(2,1)} %collective-permute-done.13.refs_1_), channel_id=1, source_target_pairs={{0,8},{4,20},{8,0},{12,28},{16,24},{20,4},{24,16},{28,12},{1,9},{5... | collective-permute-start | bytes 1327112 | tf_op jit(solution)/shard_map/ppermute | solution.py:62
  69.5 18.0 %collective-permute-start.16 = (bf16[3,96,768]{2,1,0:T(8,128)(2,1)}, bf16[3,96,768]{2,1,0:T(8,128)(2,1)}, u32[]{:S(2)}, u32[]{:S(2)}) collective-permute-start(bf16[3,96,768]{2,1,0:T(8,128)(2,1)} %collective-permute-done.14.refs_2_), channel_id=1, source_target_pairs={{0,20},{4,8},{8,28},{12,0},{16,4},{20,24},{24,12},{28,16},{1,21},{... | collective-permute-start | bytes 1327112 | tf_op jit(solution)/shard_map/ppermute | solution.py:62
  88.0 27.9 %collective-permute-start.7 = (bf16[3,96,768]{2,1,0:T(8,128)(2,1)}, bf16[3,96,768]{2,1,0:T(8,128)(2,1)}, u32[]{:S(2)}, u32[]{:S(2)}) collective-permute-start(bf16[3,96,768]{2,1,0:T(8,128)(2,1)} %collective-permute-done.4.refs_2_), channel_id=1, source_target_pairs={{0,4},{4,0},{8,12},{12,8},{16,20},{20,16},{24,28},{28,24},{1,5},{5... | collective-permute-start | bytes 1327112 | tf_op jit(solution)/shard_map/ppermute | solution.py:62
  96.8 17.0 %collective-permute-start.25 = (bf16[3,96,768]{2,1,0:T(8,128)(2,1)}, bf16[3,96,768]{2,1,0:T(8,128)(2,1)}, u32[]{:S(2)}, u32[]{:S(2)}) collective-permute-start(bf16[3,96,768]{2,1,0:T(8,128)(2,1)} %copy-done.12), channel_id=1, source_target_pairs={{0,8},{4,20},{8,0},{12,28},{16,24},{20,4},{24,16},{28,12},{1,9},{5... | collective-permute-start | bytes 1327112 | tf_op jit(solution)/shard_map/ppermute | solution.py:62
  98.5 17.6 %collective-permute-start.8 = (bf16[3,96,768]{2,1,0:T(8,128)(2,1)}, bf16[3,96,768]{2,1,0:T(8,128)(2,1)}, u32[]{:S(2)}, u32[]{:S(2)}) collective-permute-start(bf16[3,96,768]{2,1,0:T(8,128)(2,1)} %collective-permute-done.5.refs_3_), channel_id=1, source_target_pairs={{0,4},{4,0},{8,12},{12,8},{16,20},{20,16},{24,28},{28,24},{1,5},{5... | collective-permute-start | bytes 1327112 | tf_op jit(solution)/shard_map/ppermute | solution.py:62
  99.0 17.6 %collective-permute-start.9 = (bf16[3,96,768]{2,1,0:T(8,128)(2,1)}, bf16[3,96,768]{2,1,0:T(8,128)(2,1)}, u32[]{:S(2)}, u32[]{:S(2)}) collective-permute-start(bf16[3,96,768]{2,1,0:T(8,128)(2,1)} %collective-permute-done.6.refs_4_), channel_id=1, source_target_pairs={{0,4},{4,0},{8,12},{12,8},{16,20},{20,16},{24,28},{28,24},{1,5},{5... | collective-permute-start | bytes 1327112 | tf_op jit(solution)/shard_map/ppermute | solution.py:62
  113.8 31.5 %collective-permute-start.27 = (bf16[3,96,768]{2,1,0:T(8,128)(2,1)}, bf16[3,96,768]{2,1,0:T(8,128)(2,1)}, u32[]{:S(2)}, u32[]{:S(2)}) collective-permute-start(bf16[3,96,768]{2,1,0:T(8,128)(2,1)} %collective-permute-done.24.refs_2_), channel_id=1, source_target_pairs={{0,4},{4,0},{8,12},{12,8},{16,20},{20,16},{24,28},{28,24},{1,5},{5... | collective-permute-start | bytes 1327112 | tf_op jit(solution)/shard_map/ppermute | solution.py:62
  114.3 31.5 %collective-permute-start.35 = (bf16[4,80,768]{2,1,0:T(8,128)(2,1)}, bf16[4,80,768]{2,1,0:T(8,128)(2,1)}, u32[]{:S(2)}, u32[]{:S(2)}) collective-permute-start(bf16[4,80,768]{2,1,0:T(8,128)(2,1)} %collective-permute-done.33.refs_1_), channel_id=1, source_target_pairs={{0,8},{4,20},{8,0},{12,28},{16,24},{20,4},{24,16},{28,12},{1,9},{5... | collective-permute-start | bytes 1474568 | tf_op jit(solution)/shard_map/ppermute | solution.py:62
  115.9 30.0 %collective-permute-start.36 = (bf16[4,80,768]{2,1,0:T(8,128)(2,1)}, bf16[4,80,768]{2,1,0:T(8,128)(2,1)}, u32[]{:S(2)}, u32[]{:S(2)}) collective-permute-start(bf16[4,80,768]{2,1,0:T(8,128)(2,1)} %collective-permute-done.34.refs_2_), channel_id=1, source_target_pairs={{0,20},{4,8},{8,28},{12,0},{16,4},{20,24},{24,12},{28,16},{1,21},{... | collective-permute-start | bytes 1474568 | tf_op jit(solution)/shard_map/ppermute | solution.py:62
  116.1 30.3 %collective-permute-start.28 = (bf16[3,96,768]{2,1,0:T(8,128)(2,1)}, bf16[3,96,768]{2,1,0:T(8,128)(2,1)}, u32[]{:S(2)}, u32[]{:S(2)}) collective-permute-start(bf16[3,96,768]{2,1,0:T(8,128)(2,1)} %collective-permute-done.25.refs_3_), channel_id=1, source_target_pairs={{0,4},{4,0},{8,12},{12,8},{16,20},{20,16},{24,28},{28,24},{1,5},{5... | collective-permute-start | bytes 1327112 | tf_op jit(solution)/shard_map/ppermute | solution.py:62
  116.6 29.8 %collective-permute-start.29 = (bf16[3,96,768]{2,1,0:T(8,128)(2,1)}, bf16[3,96,768]{2,1,0:T(8,128)(2,1)}, u32[]{:S(2)}, u32[]{:S(2)}) collective-permute-start(bf16[3,96,768]{2,1,0:T(8,128)(2,1)} %collective-permute-done.26.refs_4_), channel_id=1, source_target_pairs={{0,4},{4,0},{8,12},{12,8},{16,20},{20,16},{24,28},{28,24},{1,5},{5... | collective-permute-start | bytes 1327112 | tf_op jit(solution)/shard_map/ppermute | solution.py:62
  (101 other events, 876.6 us)

commit v3 on v1

v3 whole, which is shorter than its diff:
```python
from functools import partial
import math

import jax
import jax.numpy as jnp
from jax import lax
from jax.experimental import pallas as pl
from jax.experimental.pallas import tpu as pltpu
from jax.sharding import PartitionSpec as P

HEADS = 12
EPS = 1e-05
MASKED = -1e30
ALL = ("dp", "tensor")
BF = jnp.bfloat16
F32 = jnp.float32


def mm(left, right):
    return jnp.dot(left, right, preferred_element_type=F32)


def mm_t(left, right):
    return lax.dot_general(left, right, (((1,), (1,)), ((), ())), preferred_element_type=F32)


def t_mm(left, right):
    return lax.dot_general(left, right, (((0,), (0,)), ((), ())), preferred_element_type=F32)


def norm_parts(values):
    average = jnp.mean(values, axis=-1, keepdims=True)
    centered = values - average
    variance = jnp.mean(centered * centered, axis=-1, keepdims=True)
    rstd = lax.rsqrt(variance + EPS)
    return centered * rstd, rstd


def norm_back(grad, gain, xhat, rstd):
    scaled = grad * gain
    return rstd * (
        scaled
        - jnp.mean(scaled, axis=-1, keepdims=True)
        - xhat * jnp.mean(scaled * xhat, axis=-1, keepdims=True)
    )


def gelu_parts(pre):
    cdf = 0.5 * (1.0 + lax.erf(pre * (1.0 / math.sqrt(2.0))))
    pdf = jnp.exp(-0.5 * pre * pre) * (1.0 / math.sqrt(2.0 * math.pi))
    return pre * cdf, cdf + pre * pdf


SMALL_PARAMS = pltpu.CompilerParams(vmem_limit_bytes=60 * 2**20)
VMEM = pl.BlockSpec(memory_space=pltpu.VMEM)
SMEM = pl.BlockSpec(memory_space=pltpu.SMEM)
LITTLE = pltpu.CompilerParams(vmem_limit_bytes=24 * 2**20)
FAR_XY = [(i, i ^ 6) for i in range(8)]
CORE = [(i, i ^ 1) for i in range(8)]
ALONG_X = [(i, i ^ 2) for i in range(8)]
ALONG_Y = [(i, i ^ 4) for i in range(8)]
SPLIT_XY = [(i, i ^ (4 if i & 1 else 2)) for i in range(8)]
CROSS_XY = [(i, i ^ (3 if i & 1 else 5)) for i in range(8)]


def send(array, pairs):
    return lax.ppermute(array, "dp", pairs)


def shift(array, by, groups):
    return lax.ppermute(array, "tensor", [(i, (i + by) % groups) for i in range(groups)])


def scoped(name, step, *args):
    with jax.named_scope(name):
        return step(*args)


def tie(array, *others):
    return lax.optimization_barrier((array,) + others)[0]


def order_kernel(spots_ref, *refs, groups):
    pieces, (join_ref, bias_ref, stage_ref, sems) = refs[:-4], refs[-4:]
    copies = []
    for k, piece in enumerate(pieces):
        for i in range(groups):
            plane = lax.rem(spots_ref[8] + (groups - i), groups)
            copies.append(
                pltpu.make_async_copy(piece.at[i], stage_ref.at[spots_ref[k] * groups + plane], sems.at[len(copies)])
            )
    for copy in copies:
        copy.start()
    for copy in copies:
        copy.wait()
    rows = join_ref.shape[1] // stage_ref.shape[0]
    for b in range(0, stage_ref.shape[0], 2):
        pair = [stage_ref[b + i].astype(F32) for i in range(2)]
        for m in range(3):
            both = jnp.concatenate([block[m * rows : (m + 1) * rows] for block in pair], axis=0)
            join_ref[m, b * rows : (b + 2) * rows, :] = both.astype(BF)
        for i in range(2):
            bias_ref[b + i] = pair[i][3 * rows :]


def order(pieces, spots, groups):
    height, dim = pieces[0].shape[1:]
    blocks = 8 * groups
    return pl.pallas_call(
        partial(order_kernel, groups=groups),
        out_shape=[jax.ShapeDtypeStruct((3, dim, dim), BF), jax.ShapeDtypeStruct((blocks, 8, dim), F32)],
        in_specs=[SMEM] + [ANY] * 8,
        out_specs=[VMEM] * 2,
        scratch_shapes=[pltpu.VMEM((blocks, height, dim), BF), pltpu.SemaphoreType.DMA((blocks,))],
        compiler_params=SMALL_PARAMS,
    )(spots, *pieces)


COPIES = 32


def fetch(spots_ref, sources, out_ref, sems, stacked=False):
    if len(sources) == 1:
        copies = [pltpu.make_async_copy(sources[0], out_ref, sems.at[0])]
    else:
        pieces, own = sources[:-1], sources[-1]
        groups, dim = out_ref.shape[0], out_ref.shape[1]
        rows, width = pieces[0].shape[1], dim // groups
        copies = []

        def add(source, target):
            copies.append(pltpu.make_async_copy(source, target, sems.at[len(copies)]))

        my_z = spots_ref[8]
        if stacked:
            for m in range(groups):
                add(own.at[pl.ds(m * width, width)], out_ref.at[m, pl.ds(pl.multiple_of(my_z * width, width), width)])
        else:
            add(own, out_ref.at[my_z])
        per = width // rows
        for k, piece in enumerate(pieces):
            e = spots_ref[k]
            for i in range(groups - 1):
                plane = lax.rem(my_z + (groups - 1 - i), groups)
                if stacked:
                    at = pl.multiple_of(plane * width + lax.rem(e, per) * rows, rows)
                    add(piece.at[i], out_ref.at[lax.div(e, per), pl.ds(at, rows)])
                else:
                    add(piece.at[i], out_ref.at[plane, pl.ds(pl.multiple_of(e * rows, rows), rows)])
    for copy in copies:
        copy.start()
    return copies


ANY = pl.BlockSpec(memory_space=pl.ANY)


class Gather:
    def __init__(self, dp_size, groups, my_d, my_z):
        self.dp_size, self.groups, self.my_d, self.my_z = dp_size, groups, my_d, my_z
        self.paired = dp_size == 8 and groups == 4
        core = lax.rem(my_d, 2)
        even = [0, 1, 2, 3, 7, 5, 4, 6]
        odd = [0, 1, 4, 5, 7, 3, 2, 6]
        flips = jnp.where(core == 0, jnp.array(even, jnp.int32), jnp.array(odd, jnp.int32))
        self.spots = jnp.concatenate([jnp.bitwise_xor(my_d, flips), my_z[None]]).astype(jnp.int32)

    def all_parts(self, part):
        whole = lax.all_gather(part, ("dp", "tensor"), axis=0)
        return whole.reshape((self.dp_size, self.groups) + part.shape).transpose(1, 0, 2, 3)

    def part_of(self, shard):
        rows = shard.shape[0] // self.dp_size
        return lax.dynamic_slice_in_dim(shard, self.my_d * rows, rows, 0)

    def all_rounds(self, parts, steps):
        count = len(parts)
        gathered, spread = [], []
        ahead, done = self.planes(parts[0][0], 0), []
        for r in range(count + 2):
            with jax.named_scope("round%d" % r):
                if r < count:
                    part, with_own = parts[r]
                    items = jnp.stack(([part] if with_own else []) + [ahead[i] for i in (1, 2, 3)])
                    items = tie(items, *done)
                    mark = [items]
                    other = scoped("other", send, items, CORE)
                    if r + 1 < count:
                        ahead = self.planes(tie(parts[r + 1][0], items), r + 1)
                else:
                    mark = done
                if 1 <= r <= count:
                    last = spread[r - 1]
                    last.append(scoped("far", send, tie(last[2], *mark), CROSS_XY))
                if r < count:
                    near0, near1 = scoped("near0", send, items, SPLIT_XY), scoped("near1", send, other, SPLIT_XY)
                if 1 <= r <= count:
                    last += [scoped("swap%d" % i, send, tie(last[2 + i], *mark), CORE) for i in range(2)]
                if r >= 2:
                    whole = spread[r - 2]
                    gathered.append(whole + [scoped("swap2", send, tie(whole[4], *mark), CORE)])
                if r < count:
                    spread.append([items, other, near0, near1])
                done = steps[r](gathered)
        return gathered

    def planes(self, part, g):
        with jax.named_scope("planes%d" % g):
            return {i: scoped("by%d" % i, shift, part, i, self.groups) for i in (1, 3, 2)}

    def whole(self, part, stacked=False):
        whole = self.all_parts(part)
        dim = part.shape[1]
        if stacked:
            whole = whole.reshape(self.groups, 4, -1, dim).transpose(1, 0, 2, 3)
        return [whole.reshape(4, -1, dim)]


def reduce_grads(gather, grads, own_rows):
    groups, spots = gather.groups, gather.spots
    if not gather.paired:
        mats, bias = grads
        mats = lax.psum_scatter(mats, ("dp", "tensor"), scatter_dimension=1, tiled=True)
        return mats[0], mats[1], mats[2], lax.psum(bias, ("dp", "tensor"))
    keep, away = grads
    rows, dim = keep.shape[1:]
    low = jax.ShapeDtypeStruct((rows, dim), BF)
    come = scoped("cores", send, away, CORE)
    own, bias, to_x, to_y, to_far = pl.pallas_call(
        add_cores_kernel,
        out_shape=[jax.ShapeDtypeStruct((rows - 16, dim), F32), jax.ShapeDtypeStruct((8, dim), F32), low, low, low],
        in_specs=[SMEM, VMEM, VMEM],
        out_specs=[VMEM] * 5,
        compiler_params=LITTLE,
    )(spots, keep, come)
    from_far = scoped("far", send, to_far, FAR_XY)
    from_x = scoped("x", send, to_x, ALONG_X)
    from_y = scoped("y", send, to_y, ALONG_Y)
    block = jax.ShapeDtypeStruct((3 * own_rows + 24, dim), BF)
    mine, *goes = pl.pallas_call(
        add_plane_kernel,
        out_shape=[jax.ShapeDtypeStruct((3 * own_rows + 8, dim), F32)] + [block] * (groups - 1),
        in_specs=[SMEM] + [VMEM] * 5,
        out_specs=[VMEM] * groups,
        scratch_shapes=[pltpu.VMEM((rows - 16, dim), F32)],
        compiler_params=LITTLE,
    )(spots, own, bias, from_x, from_y, from_far)
    comes = [scoped("stack%d" % i, shift, go, i + 1, groups) for i, go in enumerate(goes)]
    part = jax.ShapeDtypeStruct((own_rows, dim), F32)
    return pl.pallas_call(
        add_stack_kernel,
        out_shape=[part, part, part, jax.ShapeDtypeStruct((8, dim), F32)],
        in_specs=[VMEM] * groups,
        out_specs=[VMEM] * 4,
        compiler_params=LITTLE,
    )(mine, *comes)


def cost(flops, moved, exps=0):
    return pl.CostEstimate(flops=int(flops), bytes_accessed=int(moved), transcendentals=int(exps))


def head_masks():
    lane = lax.broadcasted_iota(jnp.int32, (1, 128), 1)
    first = (lane < 64).astype(F32)
    return [first.astype(BF), (1.0 - first).astype(BF)], lane < 64


def attention_kernel(spots_ref, len_ref, x_ref, gain_ref, bias_ref, *refs):
    sources = refs[:-10]
    q_ref, k_ref, v_ref, p_ref, low_ref, xhat_ref, rstd_ref, w_ref, ctx_ref, sems = refs[-10:]
    copies = fetch(spots_ref, sources, w_ref, sems, True)
    rows, dim = x_ref.shape
    for copy in copies:
        copy.wait()
    seq_len = p_ref.shape[1]
    x = x_ref[...]
    q_ref[...] = (mm_t(x, w_ref[0]).astype(BF).astype(F32) * (1.0 / math.sqrt(dim // HEADS))).astype(BF)
    k_ref[...] = mm_t(x, w_ref[1]).astype(BF)
    v_ref[...] = mm_t(x, w_ref[2]).astype(BF)
    masks, first = head_masks()
    key_at = lax.broadcasted_iota(jnp.int32, (seq_len, 1), 0)

    def one_seq(s, _):
        at = pl.ds(pl.multiple_of(s * seq_len, seq_len), seq_len)
        valid = key_at < len_ref[s]
        for j in range(HEADS // 2):
            cols = slice(128 * j, 128 * (j + 1))
            q, k, v = q_ref[at, cols], k_ref[at, cols], v_ref[at, cols]
            parts = []
            for h in range(2):
                scores = jnp.where(valid, mm_t(k, q * masks[h]), MASKED)
                exps = jnp.exp(scores - jnp.max(scores, axis=0, keepdims=True))
                probs = (exps * (1.0 / jnp.sum(exps, axis=0, keepdims=True))).astype(BF)
                p_ref[s * HEADS + 2 * j + h] = probs
                parts.append(t_mm(probs, v))
            ctx_ref[at, cols] = jnp.where(first, parts[0], parts[1]).astype(BF)
        return 0

    lax.fori_loop(0, rows // seq_len, one_seq, 0)
    xhat, rstd = norm_parts(x.astype(F32) + mm(ctx_ref[...], w_ref[3]))
    xhat_ref[...] = xhat
    rstd_ref[...] = rstd
    low_ref[...] = (xhat * gain_ref[...] + bias_ref[...]).astype(BF)


def attention_forward(spots, lengths, x, sources, gain, bias, seq_len):
    rows, dim = x.shape
    seqs = rows // seq_len
    low = jax.ShapeDtypeStruct((rows, dim), BF)
    return pl.pallas_call(
        attention_kernel,
        out_shape=[low, low, low,
                   jax.ShapeDtypeStruct((seqs * HEADS, seq_len, seq_len), BF), low,
                   jax.ShapeDtypeStruct((rows, dim), F32), jax.ShapeDtypeStruct((rows, 1), F32)],
        in_specs=[SMEM] * 2 + [VMEM] * 3 + [ANY] * len(sources),
        out_specs=[VMEM] * 7,
        scratch_shapes=[pltpu.VMEM((4, dim, dim), BF), pltpu.VMEM((rows, dim), BF), pltpu.SemaphoreType.DMA((COPIES,))],
        compiler_params=SMALL_PARAMS,
        cost_estimate=cost(2 * rows * dim * (4 * dim + 2 * seq_len), 2 * (4 * dim * dim + 8 * rows * dim), rows * seq_len * HEADS),
    )(spots, lengths, x, gain, bias, *sources)


def gelu_rows(pre_ref, act_ref, slope_ref, step=32):
    def some(i, _):
        at = pl.ds(pl.multiple_of(i * step, step), step)
        act, slope = gelu_parts(pre_ref[at, :])
        act_ref[at, :] = act.astype(act_ref.dtype)
        slope_ref[at, :] = slope.astype(slope_ref.dtype)
        return 0

    lax.fori_loop(0, pre_ref.shape[0] // step, some, 0)


def ffn_in_kernel(spots_ref, x_ref, bias_ref, *refs):
    sources = refs[:-5]
    act_ref, slope_ref, w_ref, pre_ref, sems = refs[-5:]
    for copy in fetch(spots_ref, sources, w_ref, sems):
        copy.wait()
    for p in range(w_ref.shape[0]):
        pre_ref[...] = mm(x_ref[...], w_ref[p]) + bias_ref[p]
        gelu_rows(pre_ref, act_ref.at[p], slope_ref.at[p])


def ffn_forward(spots, x, sources, bias, units):
    rows, dim = x.shape
    planes = bias.shape[0] // units
    out = jax.ShapeDtypeStruct((planes, rows, units), BF)
    return pl.pallas_call(
        ffn_in_kernel,
        out_shape=[out, out],
        in_specs=[SMEM] + [VMEM] * 2 + [ANY] * len(sources),
        out_specs=[VMEM] * 2,
        scratch_shapes=[
            pltpu.VMEM((planes, dim, units), BF), pltpu.VMEM((rows, units), F32), pltpu.SemaphoreType.DMA((COPIES,)),
        ],
        compiler_params=SMALL_PARAMS,
        cost_estimate=cost(2 * rows * dim * units * planes, 2 * planes * units * (dim + 2 * rows), 2 * rows * units * planes),
    )(spots, x, bias.reshape(planes, 1, units), *sources)


def two_pass(values, table):
    high = values.astype(BF)
    return mm(high, table) + mm((values - high.astype(F32)).astype(BF), table)


def put_rows(ref, mats, bias):
    at = 0
    for mat in mats:
        ref[at : at + mat.shape[0], :] = mat.astype(BF)
        at += mat.shape[0]
    high = bias.astype(BF).astype(F32)
    ref[at : at + 16, :] = jnp.concatenate([high, bias - high], axis=0).astype(BF)


def sum_rows(arrays):
    total = arrays[0].astype(F32)
    for array in arrays[1:]:
        total = total + array.astype(F32)
    rows = total.shape[0] - 16
    return total[:rows], total[rows : rows + 8] + total[rows + 8 :]


def add_cores_kernel(spots_ref, keep_ref, come_ref, own_ref, bias_ref, x_ref, y_ref, far_ref):
    quarter = lax.div(spots_ref[0], 2)
    own_ref[...], bias_ref[...] = sum_rows([keep_ref[quarter], come_ref[quarter]])
    for flip, ref in ((1, x_ref), (2, y_ref), (3, far_ref)):
        q = jnp.bitwise_xor(quarter, flip)
        mats, bias = sum_rows([keep_ref[q], come_ref[q]])
        put_rows(ref, [mats], bias)


def add_plane_kernel(spots_ref, own_ref, bias_ref, x_ref, y_ref, far_ref, mine_ref, *refs):
    go_refs, total_ref = refs[:-1], refs[-1]
    mats, bias = sum_rows([x_ref[...], y_ref[...], far_ref[...]])
    total_ref[...] = own_ref[...] + mats
    bias = bias + bias_ref[...]
    groups = len(go_refs) + 1
    width = total_ref.shape[0] // 3
    rows = width // groups

    def block(plane):
        at = [pl.multiple_of(i * width + plane * rows, 8) for i in range(3)]
        return jnp.concatenate([total_ref[pl.ds(a, rows), :] for a in at], axis=0)

    my_z = spots_ref[8]
    mine_ref[...] = jnp.concatenate([block(my_z), bias], axis=0)
    high = bias.astype(BF).astype(F32)
    for i, ref in enumerate(go_refs):
        there = block(lax.rem(my_z + i + 1, groups))
        ref[...] = jnp.concatenate([there, high, bias - high, jnp.zeros_like(bias)], axis=0).astype(BF)


def add_stack_kernel(mine_ref, *refs):
    come_refs, (q_ref, k_ref, v_ref, bias_ref) = refs[:-4], refs[-4:]
    total = mine_ref[...]
    rows = q_ref.shape[0]
    for ref in come_refs:
        come = ref[...].astype(F32)
        bias = come[3 * rows : 3 * rows + 8] + come[3 * rows + 8 : 3 * rows + 16]
        total = total + jnp.concatenate([come[: 3 * rows], bias], axis=0)
    q_ref[...], k_ref[...], v_ref[...] = (total[i * rows : (i + 1) * rows] for i in range(3))
    bias_ref[...] = total[3 * rows :]


def joining_kernel(
    spots_ref, act_ref, member_ref, member_t_ref, qb_ref, vb_ref, avail_ref,
    xhat1_ref, gain1_ref, bias1_ref, cot_ref, gain2_ref, bias2_ref, *refs, halves
):
    *refs, w_out_ref, down_ref, up_ref, join_ref, pre_ref, down_act_ref, slope_ref, sums_ref, bias_sums_ref, out_sems, sems = refs
    *sources, down_hbm, up_hbm, join_hbm, out_ref, g2_ref, g_ffn_ref, grad_ref0, grad_ref1 = refs
    grad_refs = [grad_ref0, grad_ref1]
    s = pl.program_id(0)
    loads = [
        pltpu.make_async_copy(source, target, sems.at[i])
        for i, (source, target) in enumerate(((down_hbm, down_ref), (join_hbm, join_ref), (up_hbm, up_ref)))
    ]

    @pl.when(s == 0)
    def _():
        copies = fetch(spots_ref, sources, w_out_ref, out_sems)
        for load in loads:
            load.start()
        for copy in copies:
            copy.wait()

    dim = out_ref.shape[-1]
    fscale = 1.0 / math.sqrt(dim)
    member, member_t = member_ref[...], member_t_ref[...]
    ffn = mm(act_ref[0], w_out_ref[0])
    for p in range(1, act_ref.shape[0]):
        ffn = ffn + mm(act_ref[p], w_out_ref[p])
    x_low = ffn.astype(BF)

    @pl.when(s == 0)
    def _():
        for load in loads:
            load.wait()

    up = up_ref[...]
    pre_ref[...] = mm(x_low, down_ref[...])
    gelu_rows(pre_ref, down_act_ref, slope_ref)
    q_low = (mm(x_low, join_ref[0]) + qb_ref[...]).astype(BF)
    u = mm_t(q_low, join_ref[1])
    big_u = mm_t(u.astype(BF), up)
    down = down_act_ref[...].astype(F32)
    fscores = (two_pass(down * big_u, member) + jnp.sum(ffn * u, axis=-1, keepdims=True)) * fscale
    fscores = jnp.where(avail_ref[0] > 0, fscores, MASKED)
    fexp = jnp.exp(fscores - jnp.max(fscores, axis=-1, keepdims=True))
    fprobs = fexp / jnp.sum(fexp, axis=-1, keepdims=True)
    p_wide = two_pass(fprobs, member_t)
    mixed_low = (ffn + mm((p_wide * down).astype(BF), up)).astype(BF)
    normed1 = xhat1_ref[...] * gain1_ref[...] + bias1_ref[...]
    xhat2, rstd2 = norm_parts(normed1 + mm(mixed_low, join_ref[2]) + vb_ref[...])
    out_ref[...] = (xhat2 * gain2_ref[...] + bias2_ref[...]).astype(BF)

    g2 = norm_back(cot_ref[...].astype(F32), gain2_ref[...], xhat2, rstd2)
    g2_ref[...] = g2
    g2_low = g2.astype(BF)
    w = mm_t(g2_low, join_ref[2])
    big_w = mm_t(w.astype(BF), up)
    gvals = two_pass(down * big_w, member) + jnp.sum(ffn * w, axis=-1, keepdims=True) + jnp.sum(g2 * vb_ref[...], axis=-1, keepdims=True)
    gs = fprobs * (gvals - jnp.sum(gvals * fprobs, axis=-1, keepdims=True)) * fscale
    gs_sum = jnp.sum(gs, axis=-1, keepdims=True)
    gs_wide = two_pass(gs, member_t)
    t_low = (mm((gs_wide * down).astype(BF), up) + gs_sum * ffn).astype(BF)
    gq_low = mm(t_low, join_ref[1]).astype(BF)
    g_down = ((gs_wide * big_u + p_wide * big_w) * slope_ref[...]).astype(BF)
    g_ffn = gs_sum * u + w + mm_t(g_down, down_ref[...]) + mm_t(gq_low, join_ref[0])
    g_ffn_ref[...] = g_ffn.astype(BF)

    first, last = s == 0, s == pl.num_programs(0) - 1
    pairs = ((x_low, gq_low), (t_low, q_low), (mixed_low, g2_low))
    d_qb = jnp.sum(gq_low.astype(F32), axis=0, keepdims=True)
    d_vb = jnp.sum(g2, axis=0, keepdims=True)
    row = lax.broadcasted_iota(jnp.int32, (8, 1), 0)
    d_bias = jnp.where(row == 0, d_qb, jnp.where(row == 1, d_vb, 0.0))

    @pl.when(first)
    def _():
        bias_sums_ref[...] = d_bias
        for i, (left, right) in enumerate(pairs):
            sums_ref[i] = t_mm(left, right)

    @pl.when(jnp.logical_not(first))
    def _():
        bias_sums_ref[...] += d_bias
        for i, (left, right) in enumerate(pairs):
            sums_ref[i] += t_mm(left, right)

    @pl.when(last)
    def _():
        if not halves:
            grad_refs[0][...] = sums_ref[...]
            grad_refs[1][...] = bias_sums_ref[...]
            return
        core = lax.rem(spots_ref[0], 2)
        part = dim // 8
        for ref, side in zip(grad_refs, (core, 1 - core)):
            for q in range(4):
                at = pl.ds(pl.multiple_of((2 * q + side) * part, part), part)
                put_rows(ref.at[q], [sums_ref[i, at, :] for i in range(3)], bias_sums_ref[...])


def joining(spots, halves, act, sources, adapt_down, up, join, qb, vb, avail, xhat1, gain1, bias1, cot, gain2, bias2, seq_len, neck):
    planes, rows, units = act.shape
    dim = xhat1.shape[1]
    seqs = rows // seq_len
    owner = jnp.arange(up.shape[0], dtype=jnp.int32) // neck
    member = (owner[:, None] == jnp.arange(128, dtype=jnp.int32)[None, :]).astype(BF)
    row_block = pl.BlockSpec((seq_len, dim), lambda s: (s, 0))

    def whole(array):
        return pl.BlockSpec(array.shape, lambda s: (0,) * array.ndim, pipeline_mode=pl.Buffered(1))

    member_t = member.T
    if halves:
        grads = [jax.ShapeDtypeStruct((4, 3 * dim // 8 + 16, dim), BF)] * 2
    else:
        grads = [jax.ShapeDtypeStruct((3, dim, dim), F32), jax.ShapeDtypeStruct((8, dim), F32)]
    return pl.pallas_call(
        partial(joining_kernel, halves=halves),
        grid=(seqs,),
        out_shape=[
            jax.ShapeDtypeStruct((rows, dim), BF),
            jax.ShapeDtypeStruct((rows, dim), F32),
            jax.ShapeDtypeStruct((rows, dim), BF),
        ] + grads,
        in_specs=[
            SMEM, pl.BlockSpec((planes, seq_len, units), lambda s: (0, s, 0)),
            whole(member), whole(member_t), whole(qb), whole(vb),
            pl.BlockSpec((1, 1, 128), lambda s: (s, 0, 0)),
            row_block, whole(gain1), whole(bias1), row_block, whole(gain2), whole(bias2),
        ] + [ANY] * (len(sources) + 3),
        out_specs=[row_block, row_block, row_block] + [whole(grad) for grad in grads],
        scratch_shapes=[
            pltpu.VMEM((planes, units, dim), BF),
            pltpu.VMEM(adapt_down.shape, BF),
            pltpu.VMEM(up.shape, BF),
            pltpu.VMEM(join.shape, BF),
            pltpu.VMEM((seq_len, dim), F32),
            pltpu.VMEM((seq_len, dim), BF),
            pltpu.VMEM((seq_len, dim), F32),
            pltpu.VMEM((3, dim, dim), F32),
            pltpu.VMEM((8, dim), F32),
            pltpu.SemaphoreType.DMA((COPIES,)),
            pltpu.SemaphoreType.DMA((3,)),
        ],
        compiler_params=SMALL_PARAMS,
        cost_estimate=cost(2 * rows * dim * (15 * dim + planes * units), 2 * dim * (8 * dim + 10 * rows), 2 * rows * dim),
    )(spots, act, member, member_t, qb, vb, avail, xhat1, gain1, bias1, cot, gain2, bias2, *sources, adapt_down, up, join)


def ffn_back_kernel(spots_ref, g_ref, rstd_ref, gain_ref, *refs, count):
    out_sources, in_sources = refs[:count], refs[count : 2 * count]
    slope_hbm, g2_hbm, xhat_hbm, g1_ref = refs[2 * count : 2 * count + 4]
    w_out_ref, w_in_ref, slope_ref, g2_ref, xhat_ref, pre_ref, out_sems, in_sems, sems = refs[2 * count + 4 :]
    out_copies = fetch(spots_ref, out_sources, w_out_ref, out_sems)
    loads = [
        pltpu.make_async_copy(source, target, sems.at[i])
        for i, (source, target) in enumerate(((slope_hbm, slope_ref), (g2_hbm, g2_ref), (xhat_hbm, xhat_ref)))
    ]
    loads[0].start()
    in_copies = fetch(spots_ref, in_sources, w_in_ref, in_sems)
    loads[1].start()
    loads[2].start()
    for copy in out_copies:
        copy.wait()
    loads[0].wait()
    planes = slope_ref.shape[0]
    for p in range(planes):
        pre_ref[p] = (mm_t(g_ref[...], w_out_ref[p]) * slope_ref[p].astype(F32)).astype(BF)
    for copy in in_copies:
        copy.wait()
    total = mm_t(pre_ref[0], w_in_ref[0])
    for p in range(1, planes):
        total = total + mm_t(pre_ref[p], w_in_ref[p])
    loads[1].wait()
    loads[2].wait()
    g1_ref[...] = norm_back(total + g2_ref[...], gain_ref[...], xhat_ref[...], rstd_ref[...])


def ffn_backward(spots, g_ffn, slope, out_sources, in_sources, g2, xhat, rstd, gain):
    planes, rows, units = slope.shape
    dim = xhat.shape[1]
    return pl.pallas_call(
        partial(ffn_back_kernel, count=len(out_sources)),
        out_shape=jax.ShapeDtypeStruct((rows, dim), F32),
        in_specs=[SMEM] + [VMEM] * 3 + [ANY] * (2 * len(out_sources) + 3),
        out_specs=VMEM,
        scratch_shapes=[
            pltpu.VMEM((planes, units, dim), BF), pltpu.VMEM((planes, dim, units), BF), pltpu.VMEM((planes, rows, units), BF),
            pltpu.VMEM((rows, dim), F32), pltpu.VMEM((rows, dim), F32), pltpu.VMEM((planes, rows, units), BF),
            pltpu.SemaphoreType.DMA((COPIES,)), pltpu.SemaphoreType.DMA((COPIES,)), pltpu.SemaphoreType.DMA((3,)),
        ],
        compiler_params=SMALL_PARAMS,
        cost_estimate=cost(4 * rows * dim * units * planes, 2 * planes * units * (2 * dim + rows)),
    )(spots, g_ffn, rstd, gain, *out_sources, *in_sources, slope, g2, xhat)


def attention_back_kernel(spots_ref, g1_ref, *refs):
    *refs, out_ref, w_ref, q_ref, k_ref, v_ref, p_ref, ctx_ref, dq_ref, dk_ref, dv_ref, w_sems, sems = refs
    *sources, q_hbm, k_hbm, v_hbm, p_hbm = refs
    copies = fetch(spots_ref, sources, w_ref, w_sems, True)
    loads = [
        pltpu.make_async_copy(source, target, sems.at[i])
        for i, (source, target) in enumerate(((q_hbm, q_ref), (k_hbm, k_ref), (v_hbm, v_ref), (p_hbm, p_ref)))
    ]
    for load in loads:
        load.start()
    for copy in copies:
        copy.wait()
    rows, dim = g1_ref.shape
    seq_len = p_ref.shape[1]
    scale = 1.0 / math.sqrt(dim // HEADS)
    ctx_ref[...] = mm_t(g1_ref[...].astype(BF), w_ref[3]).astype(BF)
    for load in loads:
        load.wait()
    masks, first = head_masks()

    def one_seq(s, _):
        at = pl.ds(pl.multiple_of(s * seq_len, seq_len), seq_len)
        for j in range(HEADS // 2):
            cols = slice(128 * j, 128 * (j + 1))
            q, k, v, g = q_ref[at, cols], k_ref[at, cols], v_ref[at, cols], ctx_ref[at, cols]
            dq, dk, dv = [], [], []
            for h in range(2):
                probs_low = p_ref[s * HEADS + 2 * j + h]
                probs = probs_low.astype(F32)
                g_probs = mm_t(v, g * masks[h])
                g_scores = (probs * (g_probs - jnp.sum(g_probs * probs, axis=0, keepdims=True))).astype(BF)
                dv.append(mm(probs_low, g))
                dk.append(mm(g_scores, q))
                dq.append(t_mm(g_scores, k))
            dq_ref[at, cols] = (jnp.where(first, dq[0], dq[1]) * scale).astype(BF)
            dk_ref[at, cols] = jnp.where(first, dk[0], dk[1]).astype(BF)
            dv_ref[at, cols] = jnp.where(first, dv[0], dv[1]).astype(BF)
        return 0

    lax.fori_loop(0, rows // seq_len, one_seq, 0)
    total = g1_ref[...] + mm(dq_ref[...], w_ref[0])
    total = total + mm(dk_ref[...], w_ref[1])
    out_ref[...] = (total + mm(dv_ref[...], w_ref[2])).astype(BF)


def attention_backward(spots, g1, sources, q, k, v, probs):
    rows, dim = g1.shape
    seq_len = probs.shape[1]
    low = pltpu.VMEM((rows, dim), BF)
    return pl.pallas_call(
        attention_back_kernel,
        out_shape=jax.ShapeDtypeStruct((rows, dim), BF),
        in_specs=[SMEM, VMEM] + [ANY] * (len(sources) + 4),
        out_specs=VMEM,
        scratch_shapes=[pltpu.VMEM((4, dim, dim), BF), low, low, low, pltpu.VMEM(probs.shape, BF), low, low, low, low,
                        pltpu.SemaphoreType.DMA((COPIES,)), pltpu.SemaphoreType.DMA((4,))],
        compiler_params=SMALL_PARAMS,
        cost_estimate=cost(2 * rows * dim * (4 * dim + 4 * seq_len), 2 * (4 * dim * dim + 8 * rows * dim)),
    )(spots, g1, *sources, q, k, v, probs)


def shards(
    tokens, lengths, adapter_mask, cotangent, att_query, att_key, att_value, att_out,
    norm1_gain, norm1_bias, ffn_in, ffn_bias, ffn_out, adapt_down, adapt_up, norm2_gain,
    norm2_bias, joining_query, joining_key, joining_value, joining_qbias, joining_vbias,
):
    groups = lax.axis_size("tensor")
    dp_size = lax.axis_size("dp")
    my_z = lax.axis_index("tensor")
    my_d = lax.axis_index("dp")
    seq_local, seq_len, dim = tokens.shape
    mine = seq_local // groups
    rows = mine * seq_len
    adapters, neck = adapt_up.shape[0], adapt_up.shape[1]
    own_rows = joining_query.shape[0]

    gather = Gather(dp_size, groups, my_d, my_z)
    spots = gather.spots
    biases = jnp.pad(jnp.stack([joining_qbias, joining_vbias]), ((0, 6), (0, dim - own_rows)))
    att_pack = jnp.concatenate([att_query.T, att_key.T, att_value.T, att_out], axis=0)
    join_part = jnp.concatenate([joining_query, joining_key, joining_value, biases], axis=0)
    parts = [gather.part_of(att_pack), gather.part_of(ffn_in), join_part, gather.part_of(ffn_out)]

    def my_slice(array):
        return lax.dynamic_slice_in_dim(array, my_z * mine, mine, 0)

    x = my_slice(tokens).reshape(rows, dim)
    shifts = jnp.arange(128, dtype=jnp.int32)
    bits = jnp.right_shift(my_slice(adapter_mask)[:, None], jnp.minimum(shifts, adapters)[None, :]) % 2
    avail = jnp.where(shifts[None, :] < adapters, bits, 0)[:, None, :]
    gain1, bias1, gain2, bias2 = (v.reshape(1, dim) for v in (norm1_gain, norm1_bias, norm2_gain, norm2_bias))
    kept = {}

    def attend(sources):
        kept["att"] = attention_forward(spots, my_slice(lengths), x, sources, gain1, bias1, seq_len)
        return [kept["att"][4]]

    def feed(sources):
        kept["ffn"] = ffn_forward(spots, kept["att"][4], sources, ffn_bias, ffn_in.shape[1])
        return [kept["ffn"][0]]

    def join_of(join, rows_of_bias):
        kept["join"] = join
        kept["bias"] = [rows_of_bias[:, i, :own_rows].reshape(1, dim) for i in range(2)]
        return [join] + kept["bias"]

    if gather.paired:
        own = [att_pack, ffn_in, None, ffn_out]
        steps = [
            lambda got: [],
            lambda got: [],
            lambda got: attend(got[0] + own[:1]),
            lambda got: feed(got[1] + own[1:2]),
            lambda got: join_of(*order(got[2], spots, groups)),
            lambda got: [],
        ]
        got = gather.all_rounds([(part, shard is None) for part, shard in zip(parts, own)], steps)
        att_sources, in_sources, out_sources = (got[i] + [own[i]] for i in (0, 1, 3))
    else:
        att_sources, in_sources, out_sources = (gather.whole(parts[i], i == 0) for i in (0, 1, 3))
        attend(att_sources)
        feed(in_sources)
        join_all = gather.all_parts(parts[2]).transpose(1, 0, 2, 3)
        mats = [join_all[:, :, i * own_rows : (i + 1) * own_rows].reshape(dim, dim) for i in range(3)]
        join_of(jnp.stack(mats), join_all[:, :, 3 * own_rows :].reshape(-1, 8, dim).astype(F32))
    q, k, v, probs, low1, xhat1, rstd1 = kept["att"]
    act, slope = kept["ffn"]
    up = adapt_up.reshape(adapters * neck, dim)
    layer_out, g2, g_ffn, *grads = joining(
        spots, gather.paired, act, out_sources, adapt_down, up, kept["join"], *kept["bias"], avail, xhat1, gain1, bias1,
        cotangent.reshape(rows, dim), gain2, bias2, seq_len, neck,
    )
    g1 = ffn_backward(spots, g_ffn, slope, out_sources, in_sources, g2, xhat1, rstd1, gain1)
    input_grad = attention_backward(spots, g1, att_sources, q, k, v, probs)
    d_q, d_k, d_v, d_bias = reduce_grads(gather, grads, own_rows)
    d_bias = lax.dynamic_slice_in_dim(d_bias[:2], (my_d * groups + my_z) * own_rows, own_rows, 1)
    return (
        layer_out.reshape(mine, seq_len, dim),
        input_grad.reshape(mine, seq_len, dim),
        d_q, d_k, d_v, d_bias[0], d_bias[1],
    )


def solution(mesh):
    both = P(ALL, None)
    return jax.shard_map(
        shards,
        mesh=mesh,
        in_specs=(
            P("dp", None, None), P("dp"), P("dp"), P(ALL, None, None),
            P(None, "tensor"), P(None, "tensor"), P(None, "tensor"), P("tensor", None),
            P(), P(), P(None, "tensor"), P(), P("tensor", None), P(), P(), P(), P(),
            both, both, both, P(ALL), P(ALL),
        ),
        out_specs=(P(ALL, None, None), P(ALL, None, None), both, both, both, P(ALL), P(ALL)),
        check_vma=False,
    )
```

time: 872 us -> 220 us (0.25); the launches traced: 862 us -> 220 us
  waiting for transfers between devices: 570 us -> 59.9 us
  matrix products: 101 us -> 0 us
  Pallas kernels: 0 us -> 97.1 us
  blocking collectives: 81.4 us -> 0 us
  local copies, waits for them, and re-layouts: 77 us -> 14.5 us
  starting transfers between devices: 0.7 us -> 40 us
  between operations: 15.4 us -> 1.07 us
  other arithmetic: 17 us -> 7.1 us
    all_gather x9 -> x0, waiting for transfers between devices: 381 us -> none  [the longest x6 259 us: gather(): lax.all_gather(part, ALL, axis=0, tiled=False)]
    reduce_scatter x3 -> x0, waiting for transfers between devices: 186 us -> none  [scatter(): return lax.psum_scatter(value, ALL, scatter_dimension=0, tiled=True)]
    dot_general x32 -> x0, matrix products: 101 us -> none  [the longest x11 40.7 us: mm_t(): lax.dot_general(left, right, (((1,), (1,)), ((), ())), preferred_element_...]
    pallas_call x0 -> x9, Pallas kernels: none -> 97.1 us  [the longest x1 29.8 us: joining(): pl.pallas_call(partial(joining_kernel, halves=halves), grid=(seqs,), out_...]
    unnamed x2 -> x0, blocking collectives: 81.4 us -> none
    ppermute x0 -> x47, waiting for transfers between devices: none -> 59.9 us  [the longest x15 39.3 us: shift(): lax.ppermute(array, 'tensor', [(i, (i + by) % groups) for i in range(grou...]
    ppermute x0 -> x47, starting transfers between devices: none -> 40 us  [the longest x15 20.4 us: shift(): lax.ppermute(array, 'tensor', [(i, (i + by) % groups) for i in range(grou...]
    reshape x13 -> x4, local copies, waits for them, and re-layouts: 26.6 us -> 2.34 us  [shards(): v.reshape(1, dim)]
  transfers between devices with their start and end apart: 12 -> 47, of which waited for: 11 -> 11; matrix products, arithmetic and copies ran while one was open for 20% -> 6% of each run, Pallas kernels for 0% -> 28%
where the time goes in v3:
time: 220 us
  Pallas kernels  97.1 us (44%)
  waiting for transfers between devices  59.9 us (27%)
  starting transfers between devices  40 us (18%)
  local copies, waits for them, and re-layouts  14.5 us (7%)
  other arithmetic  7.1 us (3%)
    ppermute x15, waiting for transfers between devices, shift(): lax.ppermute(array, 'tensor', [(i, (i + by) % groups) for i in range(grou...  39.3 us
    pallas_call x1, Pallas kernels, joining(): pl.pallas_call(partial(joining_kernel, halves=halves), grid=(seqs,), out_...  29.8 us
    ppermute x32, waiting for transfers between devices, send(): return lax.ppermute(array, 'dp', pairs)  20.5 us
    ppermute x15, starting transfers between devices, shift(): lax.ppermute(array, 'tensor', [(i, (i + by) % groups) for i in range(grou...  20.4 us
    ppermute x32, starting transfers between devices, send(): return lax.ppermute(array, 'dp', pairs)  19.6 us
    pallas_call x1, Pallas kernels, attention_backward(): pl.pallas_call(attention_back_kernel, out_shape=jax.ShapeDtypeStruct((row...  15.6 us
    pallas_call x1, Pallas kernels, ffn_backward(): pl.pallas_call(partial(ffn_back_kernel, count=len(out_sources)), out_shap...  15.1 us
    pallas_call x1, Pallas kernels, ffn_forward(): pl.pallas_call(ffn_in_kernel, out_shape=[out, out], in_specs=[SMEM] + [VM...  13.8 us
  transfers between devices with their start and end apart: 47, of which 11 were waited for; matrix products, arithmetic and copies ran while one was open for 6% of the time, Pallas kernels for 28%

profile of v3, /device:TPU:0, one launch (start us, length us, event | category | flops | bytes accessed | tf_op | source)
XLA Modules:
  0.0 219.6 jit_solution(13256540754924266874)
XLA Ops:
  2.2 5.1 %collective-permute-start.2 = (bf16[96,768]{1,0:T(8,128)(2,1)S(1)}, bf16[96,768]{1,0:T(8,128)(2,1)S(1)}, u32[]{:S(2)}, u32[]{:S(2)}) collective-permute-start(bf16[96,768]{1,0:T(8,128)(2,1)S(1)} %constant_dynamic-slice_fusion.3), channel_id=1, source_target_pairs={{0,3},{1,0},{2,1},{3,2},{4,7},{5,4},{6,5},{7,6},{8,11},{9,8},{10,9... | collective-permute-start | bytes 442376 | tf_op jit(solution)/shard_map/planes0/by3/ppermute | solution.py:71
  8.3 1.7 constant_dynamic-slice_fusion.1
  10.0 1.6 collective-permute-done.2
  11.6 8.2 %collective-permute-done.1 = bf16[96,768]{1,0:T(8,128)(2,1)S(1)} collective-permute-done((bf16[96,768]{1,0:T(8,128)(2,1)S(1)}, bf16[96,768]{1,0:T(8,128)(2,1)S(1)}, u32[]{:S(2)}, u32[]{:S(2)}) %collective-permute-start.1) | collective-permute-done | bytes 147488 | tf_op jit(solution)/shard_map/planes0/by2/ppermute | solution.py:71
  22.8 1.9 collective-permute-start.6
  26.4 9.0 %collective-permute-done.7 = bf16[96,768]{1,0:T(8,128)(2,1)S(1)} collective-permute-done((bf16[96,768]{1,0:T(8,128)(2,1)S(1)}, bf16[96,768]{1,0:T(8,128)(2,1)S(1)}, u32[]{:S(2)}, u32[]{:S(2)}) %collective-permute-start.7) | collective-permute-done | bytes 147488 | tf_op jit(solution)/shard_map/round0/planes1/by2/ppermute | solution.py:71
  37.4 2.0 collective-permute-start.12
  39.4 2.3 %collective-permute-done.14 = bf16[80,768]{1,0:T(8,128)(2,1)S(1)} collective-permute-done((bf16[80,768]{1,0:T(8,128)(2,1)S(1)}, bf16[80,768]{1,0:T(8,128)(2,1)S(1)}, u32[]{:S(2)}, u32[]{:S(2)}) %collective-permute-start.14) | collective-permute-done | bytes 122912 | tf_op jit(solution)/shard_map/round1/planes2/by3/ppermute | solution.py:71
  43.2 5.6 %collective-permute-done.13 = bf16[80,768]{1,0:T(8,128)(2,1)S(1)} collective-permute-done((bf16[80,768]{1,0:T(8,128)(2,1)S(1)}, bf16[80,768]{1,0:T(8,128)(2,1)S(1)}, u32[]{:S(2)}, u32[]{:S(2)}) %collective-permute-start.13) | collective-permute-done | bytes 122912 | tf_op jit(solution)/shard_map/round1/planes2/by2/ppermute | solution.py:71
  51.2 5.3 %collective-permute-done.24 = bf16[96,768]{1,0:T(8,128)(2,1)S(1)} collective-permute-done((bf16[96,768]{1,0:T(8,128)(2,1)}, bf16[96,768]{1,0:T(8,128)(2,1)S(1)}, u32[]{:S(2)}, u32[]{:S(2)}) %collective-permute-start.24) | collective-permute-done | bytes 147488 | tf_op jit(solution)/shard_map/round2/planes3/by3/ppermute | solution.py:71
  58.1 1.8 collective-permute-start.22
  62.3 7.3 %collective-permute-done.23 = bf16[96,768]{1,0:T(8,128)(2,1)} collective-permute-done((bf16[96,768]{1,0:T(8,128)(2,1)}, bf16[96,768]{1,0:T(8,128)(2,1)}, u32[]{:S(2)}, u32[]{:S(2)}) %collective-permute-start.23) | collective-permute-done | bytes 147488 | tf_op jit(solution)/shard_map/round2/planes3/by2/ppermute | solution.py:71
  77.6 12.4 %round2.1 = (bf16[512,768]{1,0:T(8,128)(2,1)}, bf16[512,768]{1,0:T(8,128)(2,1)}, bf16[512,768]{1,0:T(8,128)(2,1)}, bf16[24,256,256]{2,1,0:T(8,128)(2,1)}, bf16[5...) custom-call(s32[9]{0:T(128)} %pad_add_fusion.spots_ref, s32[2]{0:T(128)} %dynamic_slice.21.len_ref, ...), custom_call_target="tpu_custom_call" | custom-call | flops 2818572288 | bytes 11010048 | tf_op jit(solution)/shard_map/round2/pallas_call | solution.py:311
  93.3 13.8 %round3.1 = (bf16[4,512,768]{2,1,0:T(8,128)(2,1)}, bf16[4,512,768]{2,1,0:T(8,128)(2,1)}) custom-call(s32[9]{0:T(128)} %pad_add_fusion.spots_ref, bf16[512,768]{1,0:T(8,128)(2,1)} %get-tuple-element.57.x_ref, f32[4,1,768]{2,1,0:T(1,128)} %bitcast.49, bf16[3,96,768]{2,1,0:T(8,128)(2,1)} %pad_maximum_fusion.3.refs_0_.refs_9_, bf16[3,96,768]{2,1,0:T(8,128)(2,1)} %copy-done.11, ...), custom_call_target="tpu_custom_call" | custom-call | flops 2415919104 | bytes 11010048 | tf_op jit(solution)/shard_map/round3/pallas_call | solution.py:349
  111.0 10.9 %collective-permute-done.35.refs_3_ = bf16[3,96,768]{2,1,0:T(8,128)(2,1)} collective-permute-done((bf16[3,96,768]{2,1,0:T(8,128)(2,1)}, bf16[3,96,768]{2,1,0:T(8,128)(2,1)}, u32[]{:S(2)}, u32[]{:S(2)}) %collective-permute-start.35) | collective-permute-done | bytes 442400 | tf_op jit(solution)/shard_map/round3/near1/ppermute | solution.py:67
  122.5 5.4 %round4.1 = (bf16[3,768,768]{2,1,0:T(8,128)(2,1)}, f32[32,8,768]{2,1,0:T(8,128)}) custom-call(s32[9]{0:T(128)} %pad_add_fusion.spots_ref, bf16[4,80,768]{2,1,0:T(8,128)(2,1)} %pad_maximum_fusion.1.refs_0_, bf16[4,80,768]{2,1,0:T(8,128)(2,1)} %collective-permute-done.26.refs_1_, bf16[4,80,768]{2,1,0:T(8,128)(2,1)} %collective-permute-done.27.refs_2_, ...), custom_call_target="tpu_custom_call" | custom-call | tf_op jit(solution)/shard_map/round4/pallas_call | solution.py:109
  133.2 29.8 %shard_map.279 = (bf16[512,768]{1,0:T(8,128)(2,1)}, f32[512,768]{1,0:T(8,128)}, bf16[512,768]{1,0:T(8,128)(2,1)}, bf16[4,304,768]{2,1,0:T(8,128)(2,1)}, bf16[4,304,768]{2,1,0:T(8,128)(2,1)}) custom-call(s32[9]{0:T(128)} %pad_add_fusion.spots_ref, bf16[4,512,768]{2,1,0:T(8,128)(2,1)} %get-tuple-element.63.act_ref, bf16[768,128]{1,0:T(8,128)(2,1)} %fusion.member_ref, ...), custom_call_target="tpu_custom_call" | custom-call | flops 11475615744 | bytes 17301504 | tf_op jit(solution)/shard_map/pallas_call | solution.py:541
  163.1 3.9 %collective-permute-done.40.come_ref = bf16[4,304,768]{2,1,0:T(8,128)(2,1)S(1)} collective-permute-done((bf16[4,304,768]{2,1,0:T(8,128)(2,1)}, bf16[4,304,768]{2,1,0:T(8,128)(2,1)S(1)}, u32[]{:S(2)}, u32[]{:S(2)}) %collective-permute-start.40) | collective-permute-done | bytes 1867808 | tf_op jit(solution)/shard_map/cores/ppermute | solution.py:67
  168.5 1.9 shard_map.282
  174.8 15.1 %shard_map.280.g1_ref = f32[512,768]{1,0:T(8,128)} custom-call(s32[9]{0:T(128)} %pad_add_fusion.spots_ref, bf16[512,768]{1,0:T(8,128)(2,1)} %get-tuple-element.74.g_ref, f32[512,1]{1,0:T(8,128)} %get-tuple-element.75.rstd_ref, f32[1,768]{1,0:T(1,128)} %reshape.160.gain_ref.gain1_ref, bf16[3,96,768]{2,1,0:T(8,128)(2,1)} %copy-done.8, ...), custom_call_target="tpu_custom_call" | custom-call | flops 4831838208 | bytes 12582912 | tf_op jit(solution)/shard_map/pallas_call | solution.py:606
  189.9 5.1 %collective-permute-done.42.y_ref = bf16[304,768]{1,0:T(8,128)(2,1)} collective-permute-done((bf16[304,768]{1,0:T(8,128)(2,1)}, bf16[304,768]{1,0:T(8,128)(2,1)}, u32[]{:S(2)}, u32[]{:S(2)}) %collective-permute-start.42) | collective-permute-done | bytes 466976 | tf_op jit(solution)/shard_map/y/ppermute | solution.py:67
  196.2 2.5 %shard_map.283 = (f32[80,768]{1,0:T(8,128)S(1)}, bf16[96,768]{1,0:T(8,128)(2,1)}, bf16[96,768]{1,0:T(8,128)(2,1)}, bf16[96,768]{1,0:T(8,128)(2,1)S(1)}) custom-call(s32[9]{0:T(128)S(1)} %copy-done.5, f32[288,768]{1,0:T(8,128)S(1)} %copy-done.3, f32[8,768]{1,0:T(8,128)S(1)} %get-tuple-element.85.bias_ref, bf16[304,768]{1,0:T(8,128)(2,1)} %collective-permute-done.41.x_ref, ...), custom_call_target="tpu_custom_call" | custom-call | tf_op jit(solution)/shard_map/pallas_call | solution.py:240
  199.8 2.9 %collective-permute-start.46 = (bf16[96,768]{1,0:T(8,128)(2,1)S(1)}, bf16[96,768]{1,0:T(8,128)(2,1)S(1)}, u32[]{:S(2)}, u32[]{:S(2)}) collective-permute-start(bf16[96,768]{1,0:T(8,128)(2,1)S(1)} %get-tuple-element.92), channel_id=1, source_target_pairs={{0,3},{1,0},{2,1},{3,2},{4,7},{5,4},{6,5},{7,6},{8,11},{9,8},{10,9... | collective-permute-start | bytes 442376 | tf_op jit(solution)/shard_map/stack2/ppermute | solution.py:71
  202.7 15.6 %shard_map.281 = bf16[512,768]{1,0:T(8,128)(2,1)} custom-call(s32[9]{0:T(128)} %pad_add_fusion.spots_ref, f32[512,768]{1,0:T(8,128)} %shard_map.280.g1_ref, bf16[3,96,768]{2,1,0:T(8,128)(2,1)} %copy-done.7, bf16[3,96,768]{2,1,0:T(8,128)(2,1)} %collective-permute-done.3.refs_1_, bf16[3,96,768]{2,1,0:T(8,128)(2,1)} %copy-done.9, ...), custom_call_target="tpu_custom_call" | custom-call | flops 3221225472 | bytes 11010048 | tf_op jit(solution)/shard_map/pallas_call | solution.py:670
  (167 shorter events, 47.5 us)
Async XLA Ops:
  24.7 14.7 %collective-permute-start.4 = (bf16[3,96,768]{2,1,0:T(8,128)(2,1)S(1)}, bf16[3,96,768]{2,1,0:T(8,128)(2,1)S(1)}, u32[]{:S(2)}, u32[]{:S(2)}) collective-permute-start(bf16[3,96,768]{2,1,0:T(8,128)(2,1)S(1)} %pad_maximum_fusion.2.refs_0_), channel_id=1, source_target_pairs={{0,8},{4,20},{8,0},{12,28},{16,24},{20,4},{24,16},{28,12},{1,9},{5... | collective-permute-start | bytes 1327112 | tf_op jit(solution)/shard_map/round0/near0/ppermute | solution.py:67
  26.2 15.5 %collective-permute-start.3 = (bf16[3,96,768]{2,1,0:T(8,128)(2,1)S(1)}, bf16[3,96,768]{2,1,0:T(8,128)(2,1)}, u32[]{:S(2)}, u32[]{:S(2)}) collective-permute-start(bf16[3,96,768]{2,1,0:T(8,128)(2,1)S(1)} %pad_maximum_fusion.2.refs_0_), channel_id=1, source_target_pairs={{0,4},{4,0},{8,12},{12,8},{16,20},{20,16},{24,28},{28,24},{1,5},{5... | collective-permute-start | bytes 1327112 | tf_op jit(solution)/shard_map/round0/other/ppermute | solution.py:67
  39.4 17.1 %collective-permute-start.16 = (bf16[3,96,768]{2,1,0:T(8,128)(2,1)}, bf16[3,96,768]{2,1,0:T(8,128)(2,1)S(1)}, u32[]{:S(2)}, u32[]{:S(2)}) collective-permute-start(bf16[3,96,768]{2,1,0:T(8,128)(2,1)} %pad_maximum_fusion.3.refs_0_.refs_9_), channel_id=1, source_target_pairs={{0,4},{4,0},{8,12},{12,8},{16,20},{20,16},{24,28},{28,24},{1,5},{5... | collective-permute-start | bytes 1327112 | tf_op jit(solution)/shard_map/round1/other/ppermute | solution.py:67
  41.7 15.3 %collective-permute-start.9 = (bf16[3,96,768]{2,1,0:T(8,128)(2,1)S(1)}, bf16[3,96,768]{2,1,0:T(8,128)(2,1)S(1)}, u32[]{:S(2)}, u32[]{:S(2)}) collective-permute-start(bf16[3,96,768]{2,1,0:T(8,128)(2,1)S(1)} %collective-permute-done.4.refs_2_), channel_id=1, source_target_pairs={{0,20},{4,8},{8,28},{12,0},{16,4},{20,24},{24,12},{28,16},{1,21},{... | collective-permute-start | bytes 1327112 | tf_op jit(solution)/shard_map/round1/far/ppermute | solution.py:67
  41.7 18.2 %collective-permute-start.5 = (bf16[3,96,768]{2,1,0:T(8,128)(2,1)}, bf16[3,96,768]{2,1,0:T(8,128)(2,1)}, u32[]{:S(2)}, u32[]{:S(2)}) collective-permute-start(bf16[3,96,768]{2,1,0:T(8,128)(2,1)} %collective-permute-done.3.refs_1_), channel_id=1, source_target_pairs={{0,8},{4,20},{8,0},{12,28},{16,24},{20,4},{24,16},{28,12},{1,9},{5... | collective-permute-start | bytes 1327112 | tf_op jit(solution)/shard_map/round0/near1/ppermute | solution.py:67
  48.8 21.3 %collective-permute-start.17 = (bf16[3,96,768]{2,1,0:T(8,128)(2,1)}, bf16[3,96,768]{2,1,0:T(8,128)(2,1)}, u32[]{:S(2)}, u32[]{:S(2)}) collective-permute-start(bf16[3,96,768]{2,1,0:T(8,128)(2,1)} %pad_maximum_fusion.3.refs_0_.refs_9_), channel_id=1, source_target_pairs={{0,8},{4,20},{8,0},{12,28},{16,24},{20,4},{24,16},{28,12},{1,9},{5... | collective-permute-start | bytes 1327112 | tf_op jit(solution)/shard_map/round1/near0/ppermute | solution.py:67
  70.2 19.8 %collective-permute-start.19 = (bf16[3,96,768]{2,1,0:T(8,128)(2,1)}, bf16[3,96,768]{2,1,0:T(8,128)(2,1)}, u32[]{:S(2)}, u32[]{:S(2)}) collective-permute-start(bf16[3,96,768]{2,1,0:T(8,128)(2,1)} %collective-permute-done.17.refs_2_.refs_11_), channel_id=1, source_target_pairs={{0,20},{4,8},{8,28},{12,0},{16,4},{20,24},{24,12},{28,16},{1,21},{... | collective-permute-start | bytes 1327112 | tf_op jit(solution)/shard_map/round2/far/ppermute | solution.py:67
  74.0 16.3 %collective-permute-start.27 = (bf16[4,80,768]{2,1,0:T(8,128)(2,1)}, bf16[4,80,768]{2,1,0:T(8,128)(2,1)}, u32[]{:S(2)}, u32[]{:S(2)}) collective-permute-start(bf16[4,80,768]{2,1,0:T(8,128)(2,1)} %pad_maximum_fusion.1.refs_0_), channel_id=1, source_target_pairs={{0,8},{4,20},{8,0},{12,28},{16,24},{20,4},{24,16},{28,12},{1,9},{5... | collective-permute-start | bytes 1474568 | tf_op jit(solution)/shard_map/round2/near0/ppermute | solution.py:67
  76.2 15.3 %collective-permute-start.20 = (bf16[3,96,768]{2,1,0:T(8,128)(2,1)}, bf16[3,96,768]{2,1,0:T(8,128)(2,1)}, u32[]{:S(2)}, u32[]{:S(2)}) collective-permute-start(bf16[3,96,768]{2,1,0:T(8,128)(2,1)} %collective-permute-done.17.refs_2_.refs_11_), channel_id=1, source_target_pairs={{0,4},{4,0},{8,12},{12,8},{16,20},{20,16},{24,28},{28,24},{1,5},{5... | collective-permute-start | bytes 1327112 | tf_op jit(solution)/shard_map/round2/swap0/ppermute | solution.py:67
  76.2 14.9 %collective-permute-start.28 = (bf16[4,80,768]{2,1,0:T(8,128)(2,1)}, bf16[4,80,768]{2,1,0:T(8,128)(2,1)}, u32[]{:S(2)}, u32[]{:S(2)}) collective-permute-start(bf16[4,80,768]{2,1,0:T(8,128)(2,1)} %collective-permute-done.26.refs_1_), channel_id=1, source_target_pairs={{0,8},{4,20},{8,0},{12,28},{16,24},{20,4},{24,16},{28,12},{1,9},{5... | collective-permute-start | bytes 1474568 | tf_op jit(solution)/shard_map/round2/near1/ppermute | solution.py:67
  77.4 15.2 %collective-permute-start.21 = (bf16[3,96,768]{2,1,0:T(8,128)(2,1)}, bf16[3,96,768]{2,1,0:T(8,128)(2,1)}, u32[]{:S(2)}, u32[]{:S(2)}) collective-permute-start(bf16[3,96,768]{2,1,0:T(8,128)(2,1)} %collective-permute-done.18.refs_3_.refs_12_), channel_id=1, source_target_pairs={{0,4},{4,0},{8,12},{12,8},{16,20},{20,16},{24,28},{28,24},{1,5},{5... | collective-permute-start | bytes 1327112 | tf_op jit(solution)/shard_map/round2/swap1/ppermute | solution.py:67
  90.4 16.7 %collective-permute-start.29 = (bf16[4,80,768]{2,1,0:T(8,128)(2,1)}, bf16[4,80,768]{2,1,0:T(8,128)(2,1)}, u32[]{:S(2)}, u32[]{:S(2)}) collective-permute-start(bf16[4,80,768]{2,1,0:T(8,128)(2,1)} %collective-permute-done.27.refs_2_), channel_id=1, source_target_pairs={{0,20},{4,8},{8,28},{12,0},{16,4},{20,24},{24,12},{28,16},{1,21},{... | collective-permute-start | bytes 1474568 | tf_op jit(solution)/shard_map/round3/far/ppermute | solution.py:67
  91.1 17.8 %collective-permute-start.33 = (bf16[3,96,768]{2,1,0:T(8,128)(2,1)S(1)}, bf16[3,96,768]{2,1,0:T(8,128)(2,1)}, u32[]{:S(2)}, u32[]{:S(2)}) collective-permute-start(bf16[3,96,768]{2,1,0:T(8,128)(2,1)S(1)} %pad_maximum_fusion.4.refs_0_), channel_id=1, source_target_pairs={{0,4},{4,0},{8,12},{12,8},{16,20},{20,16},{24,28},{28,24},{1,5},{5... | collective-permute-start | bytes 1327112 | tf_op jit(solution)/shard_map/round3/other/ppermute | solution.py:67
  91.5 18.4 %collective-permute-start.34 = (bf16[3,96,768]{2,1,0:T(8,128)(2,1)S(1)}, bf16[3,96,768]{2,1,0:T(8,128)(2,1)}, u32[]{:S(2)}, u32[]{:S(2)}) collective-permute-start(bf16[3,96,768]{2,1,0:T(8,128)(2,1)S(1)} %pad_maximum_fusion.4.refs_0_), channel_id=1, source_target_pairs={{0,8},{4,20},{8,0},{12,28},{16,24},{20,4},{24,16},{28,12},{1,9},{5... | collective-permute-start | bytes 1327112 | tf_op jit(solution)/shard_map/round3/near0/ppermute | solution.py:67
  92.5 29.4 %collective-permute-start.30 = (bf16[4,80,768]{2,1,0:T(8,128)(2,1)}, bf16[4,80,768]{2,1,0:T(8,128)(2,1)}, u32[]{:S(2)}, u32[]{:S(2)}) collective-permute-start(bf16[4,80,768]{2,1,0:T(8,128)(2,1)} %collective-permute-done.27.refs_2_), channel_id=1, source_target_pairs={{0,4},{4,0},{8,12},{12,8},{16,20},{20,16},{24,28},{28,24},{1,5},{5... | collective-permute-start | bytes 1474568 | tf_op jit(solution)/shard_map/round3/swap0/ppermute | solution.py:67
  92.5 29.9 %collective-permute-start.31 = (bf16[4,80,768]{2,1,0:T(8,128)(2,1)}, bf16[4,80,768]{2,1,0:T(8,128)(2,1)}, u32[]{:S(2)}, u32[]{:S(2)}) collective-permute-start(bf16[4,80,768]{2,1,0:T(8,128)(2,1)} %collective-permute-done.28.refs_3_), channel_id=1, source_target_pairs={{0,4},{4,0},{8,12},{12,8},{16,20},{20,16},{24,28},{28,24},{1,5},{5... | collective-permute-start | bytes 1474568 | tf_op jit(solution)/shard_map/round3/swap1/ppermute | solution.py:67
  107.1 15.4 %collective-permute-start.32 = (bf16[4,80,768]{2,1,0:T(8,128)(2,1)}, bf16[4,80,768]{2,1,0:T(8,128)(2,1)}, u32[]{:S(2)}, u32[]{:S(2)}) collective-permute-start(bf16[4,80,768]{2,1,0:T(8,128)(2,1)} %collective-permute-done.29.refs_4_), channel_id=1, source_target_pairs={{0,4},{4,0},{8,12},{12,8},{16,20},{20,16},{24,28},{28,24},{1,5},{5... | collective-permute-start | bytes 1474568 | tf_op jit(solution)/shard_map/round4/swap2/ppermute | solution.py:67
  109.9 20.4 %collective-permute-start.36 = (bf16[3,96,768]{2,1,0:T(8,128)(2,1)}, bf16[3,96,768]{2,1,0:T(8,128)(2,1)}, u32[]{:S(2)}, u32[]{:S(2)}) collective-permute-start(bf16[3,96,768]{2,1,0:T(8,128)(2,1)} %collective-permute-done.34.refs_2_), channel_id=1, source_target_pairs={{0,20},{4,8},{8,28},{12,0},{16,4},{20,24},{24,12},{28,16},{1,21},{... | collective-permute-start | bytes 1327112 | tf_op jit(solution)/shard_map/round4/far/ppermute | solution.py:67
  171.3 18.6 %collective-permute-start.41 = (bf16[304,768]{1,0:T(8,128)(2,1)}, bf16[304,768]{1,0:T(8,128)(2,1)}, u32[]{:S(2)}, u32[]{:S(2)}) collective-permute-start(bf16[304,768]{1,0:T(8,128)(2,1)} %get-tuple-element.86), channel_id=1, source_target_pairs={{0,8},{4,12},{8,0},{12,4},{16,24},{20,28},{24,16},{28,20},{1,9},{5... | collective-permute-start | bytes 1400840 | tf_op jit(solution)/shard_map/x/ppermute | solution.py:67
  172.3 22.8 %collective-permute-start.42 = (bf16[304,768]{1,0:T(8,128)(2,1)}, bf16[304,768]{1,0:T(8,128)(2,1)}, u32[]{:S(2)}, u32[]{:S(2)}) collective-permute-start(bf16[304,768]{1,0:T(8,128)(2,1)} %get-tuple-element.87), channel_id=1, source_target_pairs={{0,16},{4,20},{8,24},{12,28},{16,0},{20,4},{24,8},{28,12},{1,17},{... | collective-permute-start | bytes 1400840 | tf_op jit(solution)/shard_map/y/ppermute | solution.py:67
  173.7 21.3 %collective-permute-start.43 = (bf16[304,768]{1,0:T(8,128)(2,1)}, bf16[304,768]{1,0:T(8,128)(2,1)}, u32[]{:S(2)}, u32[]{:S(2)}) collective-permute-start(bf16[304,768]{1,0:T(8,128)(2,1)} %get-tuple-element.88), channel_id=1, source_target_pairs={{0,24},{4,28},{8,16},{12,20},{16,8},{20,12},{24,0},{28,4},{1,25},{... | collective-permute-start | bytes 1400840 | tf_op jit(solution)/shard_map/far/ppermute | solution.py:67
  198.7 19.6 %collective-permute-start.44 = (bf16[96,768]{1,0:T(8,128)(2,1)}, bf16[96,768]{1,0:T(8,128)(2,1)S(1)}, u32[]{:S(2)}, u32[]{:S(2)}) collective-permute-start(bf16[96,768]{1,0:T(8,128)(2,1)} %get-tuple-element.90), channel_id=1, source_target_pairs={{0,1},{1,2},{2,3},{3,0},{4,5},{5,6},{6,7},{7,4},{8,9},{9,10},{10,1... | collective-permute-start | bytes 442376 | tf_op jit(solution)/shard_map/stack0/ppermute | solution.py:71
  198.7 19.6 %collective-permute-start.45 = (bf16[96,768]{1,0:T(8,128)(2,1)}, bf16[96,768]{1,0:T(8,128)(2,1)S(1)}, u32[]{:S(2)}, u32[]{:S(2)}) collective-permute-start(bf16[96,768]{1,0:T(8,128)(2,1)} %get-tuple-element.91), channel_id=1, source_target_pairs={{0,2},{1,3},{2,0},{3,1},{4,6},{5,7},{6,4},{7,5},{8,10},{9,11},{10,... | collective-permute-start | bytes 442376 | tf_op jit(solution)/shard_map/stack1/ppermute | solution.py:71
  199.8 18.5 %collective-permute-start.46 = (bf16[96,768]{1,0:T(8,128)(2,1)S(1)}, bf16[96,768]{1,0:T(8,128)(2,1)S(1)}, u32[]{:S(2)}, u32[]{:S(2)}) collective-permute-start(bf16[96,768]{1,0:T(8,128)(2,1)S(1)} %get-tuple-element.92), channel_id=1, source_target_pairs={{0,3},{1,0},{2,1},{3,2},{4,7},{5,4},{6,5},{7,6},{8,11},{9,8},{10,9... | collective-permute-start | bytes 442376 | tf_op jit(solution)/shard_map/stack2/ppermute | solution.py:71
  (52 other events, 848.3 us)

commit v4 on v3

v4 whole, which is shorter than its diff:
```python
from functools import partial
import math

import jax
import jax.numpy as jnp
from jax import lax
from jax.experimental import pallas as pl
from jax.experimental.pallas import tpu as pltpu
from jax.sharding import PartitionSpec as P

HEADS = 12
EPS = 1e-05
MASKED = -1e30
ALL = ("dp", "tensor")
BF = jnp.bfloat16
F32 = jnp.float32


def mm(left, right):
    return jnp.dot(left, right, preferred_element_type=F32)


def mm_t(left, right):
    return lax.dot_general(left, right, (((1,), (1,)), ((), ())), preferred_element_type=F32)


def t_mm(left, right):
    return lax.dot_general(left, right, (((0,), (0,)), ((), ())), preferred_element_type=F32)


def norm_parts(values):
    average = jnp.mean(values, axis=-1, keepdims=True)
    centered = values - average
    variance = jnp.mean(centered * centered, axis=-1, keepdims=True)
    rstd = lax.rsqrt(variance + EPS)
    return centered * rstd, rstd


def norm_back(grad, gain, xhat, rstd):
    scaled = grad * gain
    return rstd * (
        scaled
        - jnp.mean(scaled, axis=-1, keepdims=True)
        - xhat * jnp.mean(scaled * xhat, axis=-1, keepdims=True)
    )


def gelu_parts(pre):
    cdf = 0.5 * (1.0 + lax.erf(pre * (1.0 / math.sqrt(2.0))))
    pdf = jnp.exp(-0.5 * pre * pre) * (1.0 / math.sqrt(2.0 * math.pi))
    return pre * cdf, cdf + pre * pdf


def limit(mebibytes):
    return pltpu.CompilerParams(vmem_limit_bytes=mebibytes * 2**20)


VMEM = pl.BlockSpec(memory_space=pltpu.VMEM)
SMEM = pl.BlockSpec(memory_space=pltpu.SMEM)
LITTLE = limit(24)
FAR_XY = [(i, i ^ 6) for i in range(8)]
CORE = [(i, i ^ 1) for i in range(8)]
ALONG_X = [(i, i ^ 2) for i in range(8)]
ALONG_Y = [(i, i ^ 4) for i in range(8)]
SPLIT_XY = [(i, i ^ (4 if i & 1 else 2)) for i in range(8)]
CROSS_XY = [(i, i ^ (3 if i & 1 else 5)) for i in range(8)]


def send(array, pairs):
    return lax.ppermute(array, "dp", pairs)


def shift(array, by, groups):
    return lax.ppermute(array, "tensor", [(i, (i + by) % groups) for i in range(groups)])


def scoped(name, step, *args):
    with jax.named_scope(name):
        return step(*args)


def tie(array, *others):
    return lax.optimization_barrier((array,) + others)[0]


def fetch_blocks(spots_ref, sources, stage_ref, sem):
    if len(sources) == 1:
        pltpu.make_async_copy(sources[0], stage_ref, sem).start()
        return
    planes = planes_in_order(spots_ref)
    for k, (ref, first) in enumerate(views(sources)):
        for i, plane in enumerate(planes[1:] + planes[:1]):
            pltpu.make_async_copy(ref.at[first + i], stage_ref.at[spots_ref[k] * len(planes) + plane], sem).start()


def order_rows(stage_ref, join_ref, biases_ref):
    blocks = stage_ref.shape[0]
    rows = join_ref.shape[1] // blocks
    total = 0.0
    for b in range(0, blocks, 2):
        pair = [stage_ref[b + i].astype(F32) for i in range(2)]
        for m in range(3):
            both = jnp.concatenate([block[m * rows : (m + 1) * rows] for block in pair], axis=0)
            join_ref[m, b * rows : (b + 2) * rows, :] = both.astype(BF)
        total = total + pair[0][3 * rows :] + pair[1][3 * rows :]
    biases_ref[...] = total


def fetch(spots_ref, sources, out_ref, sems, stacked=False):
    groups, dim = out_ref.shape[0], out_ref.shape[1]

    def copy(source, index, target):
        pltpu.make_async_copy(source, target, sems.at[index]).start()

    if len(sources) == 1:
        for m in range(groups):
            copy(sources[0].at[m], m, out_ref.at[m])
        return
    pieces, own = views(sources[:-1]), sources[-1]
    rows, width = sources[0].shape[1], dim // groups
    my_z = spots_ref[8]
    if stacked:
        for m in range(groups):
            copy(own.at[pl.ds(m * width, width)], m, out_ref.at[m, pl.ds(pl.multiple_of(my_z * width, width), width)])
    else:
        copy(own, my_z, out_ref.at[my_z])
    per = width // rows
    for i, plane in enumerate(planes_in_order(spots_ref)[1:]):
        for k, (ref, first) in enumerate(pieces):
            e = spots_ref[k]
            if stacked:
                at = pl.multiple_of(plane * width + lax.rem(e, per) * rows, rows)
                copy(ref.at[first + i], lax.div(e, per), out_ref.at[lax.div(e, per), pl.ds(at, rows)])
            else:
                copy(ref.at[first + i], plane, out_ref.at[plane, pl.ds(pl.multiple_of(e * rows, rows), rows)])


def views(sources):
    if len(sources) == 8:
        return [(source, 0) for source in sources]
    both, near, far, swapped, swapped_far = sources
    count = far.shape[0]
    return [(both, 0), (both, count), (near, 0), (near, count), (far, 0), (swapped, 0), (swapped, count), (swapped_far, 0)]


def merge_kernel(spots_ref, *refs, count):
    beside, across, beside2, across2, *own = refs[:count]
    outs = refs[count:]
    core = lax.rem(spots_ref[0], 2)
    rows = across.shape[0]
    blocks = 3 + len(own) // 2
    sides = [outs[0], outs[1]] if len(outs) == 2 else [outs[0].at[pl.ds(i * blocks, blocks)] for i in range(2)]
    parts = [pl.ds(pl.multiple_of(at * rows, rows), rows) for at in (core, 1 - core)]
    for side, at, last, mine in zip(sides, parts, (across, across2), own or (None, None)):
        side[core] = beside[at, :]
        side[1 - core] = beside2[at, :]
        side[2] = last[...]
        if mine is not None:
            side[3] = mine[...]


def merge(spots, arrays, split):
    rows, dim = arrays[1].shape
    blocks = 3 + (len(arrays) - 4) // 2
    outs = [blocks, blocks] if split else [2 * blocks]
    return pl.pallas_call(
        partial(merge_kernel, count=len(arrays)),
        out_shape=[jax.ShapeDtypeStruct((out, rows, dim), BF) for out in outs],
        in_specs=[SMEM] + [VMEM] * len(arrays),
        out_specs=[VMEM] * len(outs),
        compiler_params=limit(8),
    )(spots, *arrays)


def arrive(out_ref, sems, m):
    pltpu.make_async_copy(out_ref.at[m], out_ref.at[m], sems.at[m]).wait()


def planes_in_order(spots_ref, groups=4):
    return [lax.rem(spots_ref[8] + step, groups) for step in (0, 1, groups - 1, 2)]


def begin(pairs, sems):
    copies = [pltpu.make_async_copy(source, target, sems.at[i]) for i, (source, target) in enumerate(pairs)]
    for one in copies:
        one.start()
    return copies


WEIGHT_SEMS = pltpu.SemaphoreType.DMA((4,))
ANY = pl.BlockSpec(memory_space=pltpu.HBM)


class Gather:
    def __init__(self, dp_size, groups, my_d, my_z, seqs):
        self.dp_size, self.groups, self.my_d, self.my_z = dp_size, groups, my_d, my_z
        self.paired = dp_size == 8 and groups == 4 and seqs == 2
        core = lax.rem(my_d, 2)
        even = [0, 1, 2, 3, 7, 5, 4, 6]
        odd = [0, 1, 4, 5, 7, 3, 2, 6]
        flips = jnp.where(core == 0, jnp.array(even, jnp.int32), jnp.array(odd, jnp.int32))
        self.spots = jnp.concatenate([jnp.bitwise_xor(my_d, flips), my_z[None]]).astype(jnp.int32)

    def all_parts(self, part):
        whole = lax.all_gather(part, ("dp", "tensor"), axis=0)
        return whole.reshape((self.dp_size, self.groups) + part.shape).transpose(1, 0, 2, 3)

    def part_of(self, shard):
        rows = shard.shape[0] // self.dp_size
        return lax.dynamic_slice_in_dim(shard, self.my_d * rows, rows, 0)

    def all_rounds(self, parts, steps):
        count = len(parts)
        gathered, spread = [], []
        ahead, done = self.planes(parts[0], 0), [rows for part in parts[1:] for rows in part[:2]]
        for r in range(count + 2):
            with jax.named_scope("round%d" % r):
                ready = list(lax.optimization_barrier((*ahead, *done)))
                ahead = ready[: len(ahead)]
                if r >= 1:
                    at = len(ahead)
                    if r <= count:
                        last = spread[r - 1]
                        last[1] = ready[at : at + len(last[1])]
                        at += len(last[1])
                    if r >= 2:
                        spread[r - 2][2] = ready[at]
                done = []
                if 1 <= r <= count:
                    near_half = last[1][0] if len(last[1]) == 2 else last[1][0][: last[1][0].shape[0] // 2]
                    last.append(scoped("far", send, near_half, CROSS_XY))
                if r < count:
                    beside, across = ahead
                    others = [scoped("others", send, beside, CORE), scoped("others", send, across, CORE)]
                    both = merge(self.spots, [beside, across, *others, *parts[r][2:]], r == count - 1)
                    near = [scoped("near", send, side, SPLIT_XY) for side in both]
                    spread.append([both, near])
                    done += near
                    ahead = []
                    if r + 1 < count:
                        ahead = self.planes([tie(rows, both[0]) for rows in parts[r + 1]], r + 1)
                else:
                    ahead = []
                if 1 <= r <= count:
                    last.append([scoped("swap", send, array, CORE) for array in last[1]])
                    done += last[2:3] + last[3]
                if r >= 2:
                    whole = spread[r - 2]
                    gathered.append([*whole[0], *whole[1], whole[2], *whole[3], scoped("swapfar", send, whole[2], CORE)])
                done += steps[r](gathered)
        return gathered

    def planes(self, part, r):
        with jax.named_scope("planes%d" % r):
            groups = self.groups
            pairs = [
                (d * groups + z, d * groups + (z + (1 if d & 1 else groups - 1)) % groups)
                for d in range(self.dp_size)
                for z in range(groups)
            ]
            beside = scoped("beside", lax.ppermute, part[1], ("dp", "tensor"), pairs)
            return beside, scoped("across", shift, part[0], 2, groups)

    def half_of(self, quarter):
        rows = quarter.shape[0] // 2
        return jnp.where(lax.rem(self.my_d, 2) == 0, quarter[:rows], quarter[rows:])

    def quarter_of(self, shard):
        rows = 2 * shard.shape[0] // self.dp_size
        return lax.dynamic_slice_in_dim(shard, self.my_d // 2 * rows, rows, 0)

    def whole(self, part, stacked=False):
        whole = self.all_parts(part)
        dim = part.shape[1]
        if stacked:
            whole = whole.reshape(self.groups, 4, -1, dim).transpose(1, 0, 2, 3)
        return [whole.reshape(4, -1, dim)]


def reduce_grads(gather, grads, own_rows):
    groups, spots = gather.groups, gather.spots
    if not gather.paired:
        mats, bias = grads
        mats = lax.psum_scatter(mats, ("dp", "tensor"), scatter_dimension=1, tiled=True)
        return mats[0], mats[1], mats[2], lax.psum(bias, ("dp", "tensor"))
    keep, away = grads
    rows, dim = keep.shape[1:]
    low = jax.ShapeDtypeStruct((rows, dim), BF)
    come = scoped("cores", send, away, CORE)
    own, bias, to_x, to_y, to_far = pl.pallas_call(
        add_cores_kernel,
        out_shape=[jax.ShapeDtypeStruct((rows - 16, dim), F32), jax.ShapeDtypeStruct((8, dim), F32), low, low, low],
        in_specs=[SMEM, VMEM, VMEM],
        out_specs=[VMEM] * 5,
        compiler_params=LITTLE,
    )(spots, keep, come)
    from_far = scoped("far", send, to_far, FAR_XY)
    from_x = scoped("x", send, to_x, ALONG_X)
    from_y = scoped("y", send, to_y, ALONG_Y)
    block = jax.ShapeDtypeStruct((3 * own_rows + 24, dim), BF)
    mine, *goes = pl.pallas_call(
        add_plane_kernel,
        out_shape=[jax.ShapeDtypeStruct((3 * own_rows + 8, dim), F32)] + [block] * (groups - 1),
        in_specs=[SMEM] + [VMEM] * 5,
        out_specs=[VMEM] * groups,
        scratch_shapes=[pltpu.VMEM((rows - 16, dim), F32)],
        compiler_params=LITTLE,
    )(spots, own, bias, from_x, from_y, from_far)
    comes = [scoped("stack%d" % i, shift, go, i + 1, groups) for i, go in enumerate(goes)]
    part = jax.ShapeDtypeStruct((own_rows, dim), F32)
    return pl.pallas_call(
        add_stack_kernel,
        out_shape=[part, part, part, jax.ShapeDtypeStruct((8, dim), F32)],
        in_specs=[VMEM] * groups,
        out_specs=[VMEM] * 4,
        compiler_params=LITTLE,
    )(mine, *comes)


def cost(flops, moved, exps=0):
    return pl.CostEstimate(flops=int(flops), bytes_accessed=int(moved), transcendentals=int(exps))


def head_masks():
    lane = lax.broadcasted_iota(jnp.int32, (1, 128), 1)
    first = (lane < 64).astype(F32)
    return [first.astype(BF), (1.0 - first).astype(BF)], lane < 64


def attention_kernel(spots_ref, len_ref, x_ref, norms_ref, *refs):
    *sources, q_hbm, k_hbm, v_hbm, p_hbm, low_ref, xhat_hbm, rstd_ref, w_ref, ctx_ref, q_ref, k_ref, v_ref, p_ref, xhat_ref, sems, store_sems = refs
    fetch(spots_ref, sources, w_ref, sems, True)
    rows, dim = x_ref.shape
    for m in range(4):
        arrive(w_ref, sems, m)
    seq_len = p_ref.shape[1]
    x = x_ref[...]
    q_ref[...] = (mm_t(x, w_ref[0]).astype(BF).astype(F32) * (1.0 / math.sqrt(dim // HEADS))).astype(BF)
    k_ref[...] = mm_t(x, w_ref[1]).astype(BF)
    v_ref[...] = mm_t(x, w_ref[2]).astype(BF)
    masks, first = head_masks()
    key_at = lax.broadcasted_iota(jnp.int32, (seq_len, 1), 0)

    def one_seq(s, _):
        at = pl.ds(pl.multiple_of(s * seq_len, seq_len), seq_len)
        valid = key_at < len_ref[s]
        for j in range(HEADS // 2):
            cols = slice(128 * j, 128 * (j + 1))
            q, k, v = q_ref[at, cols], k_ref[at, cols], v_ref[at, cols]
            parts = []
            for h in range(2):
                scores = jnp.where(valid, mm_t(k, q * masks[h]), MASKED)
                exps = jnp.exp(scores - jnp.max(scores, axis=0, keepdims=True))
                probs = (exps * (1.0 / jnp.sum(exps, axis=0, keepdims=True))).astype(BF)
                p_ref[s * HEADS + 2 * j + h] = probs
                parts.append(t_mm(probs, v))
            ctx_ref[at, cols] = jnp.where(first, parts[0], parts[1]).astype(BF)
        return 0

    lax.fori_loop(0, rows // seq_len, one_seq, 0)
    stores = begin(((q_ref, q_hbm), (k_ref, k_hbm), (v_ref, v_hbm), (p_ref, p_hbm)), store_sems)
    xhat, rstd = norm_parts(x.astype(F32) + mm(ctx_ref[...], w_ref[3]))
    xhat_ref[...] = xhat
    stores += begin(((xhat_ref, xhat_hbm),), store_sems.at[pl.ds(4, 1)])
    rstd_ref[...] = rstd
    low_ref[...] = (xhat * norms_ref[0:1, :] + norms_ref[1:2, :]).astype(BF)
    for store in stores:
        store.wait()


def attention_forward(spots, lengths, x, sources, norms, seq_len):
    rows, dim = x.shape
    seqs = rows // seq_len
    low = jax.ShapeDtypeStruct((rows, dim), BF)
    return pl.pallas_call(
        attention_kernel,
        out_shape=[low, low, low,
                   jax.ShapeDtypeStruct((seqs * HEADS, seq_len, seq_len), BF), low,
                   jax.ShapeDtypeStruct((rows, dim), F32), jax.ShapeDtypeStruct((rows, 1), F32)],
        in_specs=[SMEM] * 2 + [VMEM] * 2 + [ANY] * len(sources),
        out_specs=[ANY] * 4 + [VMEM, ANY, VMEM],
        scratch_shapes=[pltpu.VMEM((4, dim, dim), BF)] + [pltpu.VMEM((rows, dim), BF)] * 4 + [
            pltpu.VMEM((seqs * HEADS, seq_len, seq_len), BF), pltpu.VMEM((rows, dim), F32),
            WEIGHT_SEMS, pltpu.SemaphoreType.DMA((5,)),
        ],
        compiler_params=limit(60),
        cost_estimate=cost(2 * rows * dim * (4 * dim + 2 * seq_len), 2 * (4 * dim * dim + 8 * rows * dim), rows * seq_len * HEADS),
    )(spots, lengths, x, norms, *sources)


def by_rows(rows, step, work, unroll=1):
    work(slice(0, rows))


def ffn_in_kernel(spots_ref, x_ref, bias_ref, *refs):
    *sources, act_hbm, slope_hbm, act_ref, slope_ref, w_ref, pre_ref, sems, store_sems = refs
    fetch(spots_ref, sources, w_ref, sems)
    units = pre_ref.shape[1]
    stores = []
    for i, p in enumerate(planes_in_order(spots_ref, w_ref.shape[0])):
        arrive(w_ref, sems, p)
        pre_ref[...] = mm(x_ref[...], w_ref[p])
        cols = pl.ds(pl.multiple_of(p * units, units), units)
        act, slope = gelu_parts(pre_ref[...] + bias_ref[p])
        act_ref[:, cols] = act.astype(BF)
        slope_ref[:, cols] = slope.astype(BF)
        pairs = [(act_ref, act_hbm), (slope_ref, slope_hbm)]
        stores += begin([(ref.at[:, cols], hbm.at[:, cols]) for ref, hbm in pairs], store_sems.at[pl.ds(2 * i, 2)])
    for store in stores:
        store.wait()


def ffn_forward(spots, x, sources, bias, units):
    rows, dim = x.shape
    planes = bias.shape[0] // units
    out = jax.ShapeDtypeStruct((rows, planes * units), BF)
    return pl.pallas_call(
        ffn_in_kernel,
        out_shape=[out, out],
        in_specs=[SMEM] + [VMEM] * 2 + [ANY] * len(sources),
        out_specs=[ANY] * 2,
        scratch_shapes=[
            pltpu.VMEM((rows, planes * units), BF), pltpu.VMEM((rows, planes * units), BF),
            pltpu.VMEM((planes, dim, units), BF), pltpu.VMEM((rows, units), F32), WEIGHT_SEMS, pltpu.SemaphoreType.DMA((8,)),
        ],
        compiler_params=limit(60),
        cost_estimate=cost(2 * rows * dim * units * planes, 2 * planes * units * (dim + 2 * rows), 2 * rows * units * planes),
    )(spots, x, bias.reshape(planes, 1, units), *sources)


def two_pass(values, table):
    high = values.astype(BF)
    return mm(high, table) + mm((values - high.astype(F32)).astype(BF), table)


def put_rows(ref, mats, bias):
    at = 0
    for mat in mats:
        ref[at : at + mat.shape[0], :] = mat.astype(BF)
        at += mat.shape[0]
    high = bias.astype(BF).astype(F32)
    ref[at : at + 16, :] = jnp.concatenate([high, bias - high], axis=0).astype(BF)


def sum_rows(arrays):
    total = arrays[0].astype(F32)
    for array in arrays[1:]:
        total = total + array.astype(F32)
    rows = total.shape[0] - 16
    return total[:rows], total[rows : rows + 8] + total[rows + 8 :]


def add_cores_kernel(spots_ref, keep_ref, come_ref, own_ref, bias_ref, x_ref, y_ref, far_ref):
    quarter = lax.div(spots_ref[0], 2)
    own_ref[...], bias_ref[...] = sum_rows([keep_ref[quarter], come_ref[quarter]])
    for flip, ref in ((1, x_ref), (2, y_ref), (3, far_ref)):
        q = jnp.bitwise_xor(quarter, flip)
        mats, bias = sum_rows([keep_ref[q], come_ref[q]])
        put_rows(ref, [mats], bias)


def add_plane_kernel(spots_ref, own_ref, bias_ref, x_ref, y_ref, far_ref, mine_ref, *refs):
    go_refs, total_ref = refs[:-1], refs[-1]
    mats, bias = sum_rows([x_ref[...], y_ref[...], far_ref[...]])
    total_ref[...] = own_ref[...] + mats
    bias = bias + bias_ref[...]
    groups = len(go_refs) + 1
    width = total_ref.shape[0] // 3
    rows = width // groups

    def block(plane):
        at = [pl.multiple_of(i * width + plane * rows, 8) for i in range(3)]
        return jnp.concatenate([total_ref[pl.ds(a, rows), :] for a in at], axis=0)

    my_z = spots_ref[8]
    mine_ref[...] = jnp.concatenate([block(my_z), bias], axis=0)
    high = bias.astype(BF).astype(F32)
    for i, ref in enumerate(go_refs):
        there = block(lax.rem(my_z + i + 1, groups))
        ref[...] = jnp.concatenate([there, high, bias - high, jnp.zeros_like(bias)], axis=0).astype(BF)


def add_stack_kernel(mine_ref, *refs):
    come_refs, (q_ref, k_ref, v_ref, bias_ref) = refs[:-4], refs[-4:]
    total = mine_ref[...]
    rows = q_ref.shape[0]
    for ref in come_refs:
        come = ref[...].astype(F32)
        bias = come[3 * rows : 3 * rows + 8] + come[3 * rows + 8 : 3 * rows + 16]
        total = total + jnp.concatenate([come[: 3 * rows], bias], axis=0)
    q_ref[...], k_ref[...], v_ref[...] = (total[i * rows : (i + 1) * rows] for i in range(3))
    bias_ref[...] = total[3 * rows :]


def joining_kernel(
    spots_ref, member_ref, member_t_ref, avail_ref, norms_ref, act_hbm, xhat1_hbm, cot_hbm, *refs, halves, count
):
    gain1, bias1, gain2, bias2 = (norms_ref[i : i + 1, :] for i in range(4))
    down_hbm, up_hbm, *refs = refs
    join_sources, sources, refs = refs[:count], refs[count:-43], refs[-43:]
    stage_ref, biases_ref, stage_sem, refs = refs[-3], refs[-2], refs[-1], refs[:-3]
    out_hbm, g2_hbm, g_ffn_ref, grad_hbm0, grad_hbm1 = refs[:5]
    act_ref, w_out_ref, down_ref, up_ref, join_ref, xhat1_ref, cot_ref, act_sems, out_sems, sems, store_sems = refs[5:16]
    ffn_ref, tmp_ref, u_ref, w_ref, big_u_ref, big_w_ref, p_wide_ref = refs[16:23]
    x_ref, act2_ref, slope_ref, q_ref, high_ref, low_ref, mixed_ref, t_ref = refs[23:31]
    sums_ref, bias_sums_ref, dot_ref, dot2_ref, out_ref, g2_ref, grad_ref0, grad_ref1, bias_ref = refs[31:40]
    rows, dim = out_ref.shape
    planes, units = w_out_ref.shape[:2]
    fetch(spots_ref, sources, w_out_ref, out_sems)
    act_loads = []
    for i, p in enumerate(planes_in_order(spots_ref, planes)):
        cols = pl.ds(pl.multiple_of(p * units, units), units)
        act_loads.append((p, cols, pltpu.make_async_copy(act_hbm.at[:, cols], act_ref.at[:, cols], act_sems.at[i])))
        act_loads[-1][2].start()
    fetch_blocks(spots_ref, join_sources, stage_ref, stage_sem)
    loads = begin(((down_hbm, down_ref), (up_hbm, up_ref), (xhat1_hbm, xhat1_ref), (cot_hbm, cot_ref)), sems)
    seqs = avail_ref.shape[0]
    fscale = 1.0 / math.sqrt(dim)
    member, member_t = member_ref[...], member_t_ref[...]
    for i, (p, cols, load) in enumerate(act_loads):
        load.wait()
        arrive(w_out_ref, out_sems, p)
        term = mm(act_ref[:, cols], w_out_ref[p])
        ffn_ref[...] = term if i == 0 else ffn_ref[...] + term

    def lower_ffn(at):
        x_ref[at, :] = ffn_ref[at, :].astype(BF)

    by_rows(rows, 64, lower_ffn)
    loads[0].wait()
    big_w_ref[...] = mm(x_ref[...], down_ref[...])

    def gelu(at):
        act, slope = gelu_parts(big_w_ref[at, :])
        act2_ref[at, :] = act.astype(BF)
        slope_ref[at, :] = slope.astype(BF)

    pltpu.make_async_copy(stage_ref, stage_ref, stage_sem).wait()
    order_rows(stage_ref, join_ref, biases_ref)
    qb, vb = biases_ref[0:1, :], biases_ref[1:2, :]
    tmp_ref[...] = mm(x_ref[...], join_ref[0])

    def lower_q(at):
        q_ref[at, :] = (tmp_ref[at, :] + qb).astype(BF)

    by_rows(rows, 64, lower_q)
    u_ref[...] = mm_t(q_ref[...], join_ref[1])

    def lower_u(at):
        u = u_ref[at, :]
        high_ref[at, :] = u.astype(BF)
        dot_ref[at, :] = jnp.sum(ffn_ref[at, :] * u, axis=-1, keepdims=True)

    by_rows(rows, 64, lower_u)
    loads[1].wait()
    big_u_ref[...] = mm_t(high_ref[...], up_ref[...])
    by_rows(rows, 32, gelu)

    def product(source_ref):
        def work(at):
            both = act2_ref[at, :].astype(F32) * source_ref[at, :]
            high = both.astype(BF)
            high_ref[at, :] = high
            low_ref[at, :] = (both - high.astype(F32)).astype(BF)

        by_rows(rows, 64, work)
        return mm(high_ref[...], member) + mm(low_ref[...], member)

    avail = jnp.concatenate([jnp.broadcast_to(avail_ref[i], (rows // seqs, 128)) for i in range(seqs)], axis=0)
    fscores = (product(big_u_ref) + dot_ref[...]) * fscale
    fscores = jnp.where(avail > 0, fscores, MASKED)
    fexp = jnp.exp(fscores - jnp.max(fscores, axis=-1, keepdims=True))
    fprobs = fexp / jnp.sum(fexp, axis=-1, keepdims=True)
    p_wide_ref[...] = two_pass(fprobs, member_t)

    def weigh_p(at):
        high_ref[at, :] = (p_wide_ref[at, :] * act2_ref[at, :].astype(F32)).astype(BF)

    by_rows(rows, 64, weigh_p)
    tmp_ref[...] = mm(high_ref[...], up_ref[...])

    def mix(at):
        mixed_ref[at, :] = (ffn_ref[at, :] + tmp_ref[at, :]).astype(BF)

    by_rows(rows, 64, mix)
    tmp_ref[...] = mm(mixed_ref[...], join_ref[2])
    bias_sums_ref[...] = jnp.zeros_like(bias_sums_ref)
    loads[2].wait()
    loads[3].wait()

    def norm(at):
        normed1 = xhat1_ref[at, :] * gain1 + bias1
        xhat2, rstd2 = norm_parts(normed1 + tmp_ref[at, :] + vb)
        out_ref[at, :] = (xhat2 * gain2 + bias2).astype(BF)
        g2 = norm_back(cot_ref[at, :].astype(F32), gain2, xhat2, rstd2)
        g2_ref[at, :] = g2
        low_ref[at, :] = g2.astype(BF)
        dot2_ref[at, :] = jnp.sum(g2 * vb, axis=-1, keepdims=True)
        bias_sums_ref[1] += jnp.sum(g2.reshape(-1, 8, dim), axis=0)

    by_rows(rows, 32, norm)
    stores = begin(((out_ref, out_hbm), (g2_ref, g2_hbm)), store_sems)
    sums_ref[2] = t_mm(mixed_ref[...], low_ref[...])
    w_ref[...] = mm_t(low_ref[...], join_ref[2])

    def lower_w(at):
        w = w_ref[at, :]
        high_ref[at, :] = w.astype(BF)
        dot2_ref[at, :] += jnp.sum(ffn_ref[at, :] * w, axis=-1, keepdims=True)

    by_rows(rows, 64, lower_w)
    big_w_ref[...] = mm_t(high_ref[...], up_ref[...])
    gvals = product(big_w_ref) + dot2_ref[...]
    gs = fprobs * (gvals - jnp.sum(gvals * fprobs, axis=-1, keepdims=True)) * fscale
    dot_ref[...] = jnp.sum(gs, axis=-1, keepdims=True)
    tmp_ref[...] = two_pass(gs, member_t)

    def weigh_gs(at):
        wide = tmp_ref[at, :]
        high_ref[at, :] = (wide * act2_ref[at, :].astype(F32)).astype(BF)
        grad = wide * big_u_ref[at, :] + p_wide_ref[at, :] * big_w_ref[at, :]
        slope_ref[at, :] = (grad * slope_ref[at, :].astype(F32)).astype(BF)

    by_rows(rows, 64, weigh_gs)
    tmp_ref[...] = mm(high_ref[...], up_ref[...])

    def lower_t(at):
        t_ref[at, :] = (tmp_ref[at, :] + dot_ref[at, :] * ffn_ref[at, :]).astype(BF)

    by_rows(rows, 64, lower_t)
    tmp_ref[...] = mm(t_ref[...], join_ref[1])

    def lower_gq(at):
        gq = tmp_ref[at, :].astype(BF)
        high_ref[at, :] = gq
        bias_sums_ref[0] += jnp.sum(gq.astype(F32).reshape(-1, 8, dim), axis=0)

    by_rows(rows, 64, lower_gq)
    sums_ref[0] = t_mm(x_ref[...], high_ref[...])
    sums_ref[1] = t_mm(t_ref[...], q_ref[...])
    row = lax.broadcasted_iota(jnp.int32, (8, 1), 0)
    d_bias = [jnp.sum(bias_sums_ref[i], axis=0, keepdims=True) for i in range(2)]
    bias_ref[...] = jnp.where(row == 0, d_bias[0], jnp.where(row == 1, d_bias[1], 0.0))
    if halves:
        core = lax.rem(spots_ref[0], 2)
        part = dim // 8
        for i, (ref, side) in enumerate(((grad_ref1, 1 - core), (grad_ref0, core))):
            for q in range(4):
                at = pl.ds(pl.multiple_of((2 * q + side) * part, part), part)
                put_rows(ref.at[q], [sums_ref[i, at, :] for i in range(3)], bias_ref[...])
            hbm = grad_hbm0 if i else grad_hbm1
            stores += begin(((ref, hbm),), store_sems.at[pl.ds(2 + i, 1)])
    else:
        stores += begin(((sums_ref, grad_hbm0), (bias_ref, grad_hbm1)), store_sems.at[pl.ds(2, 2)])
    tmp_ref[...] = mm_t(slope_ref[...], down_ref[...]) + mm_t(high_ref[...], join_ref[0])

    def add_ffn(at):
        g_ffn_ref[at, :] = (dot_ref[at, :] * u_ref[at, :] + w_ref[at, :] + tmp_ref[at, :]).astype(BF)

    by_rows(rows, 64, add_ffn)
    for store in stores:
        store.wait()


def joining(spots, halves, act, sources, adapt_down, up, join_sources, member, member_t, avail, xhat1, norms, cot):
    rows, dim = xhat1.shape
    if halves:
        grads = [jax.ShapeDtypeStruct((4, 3 * dim // 8 + 16, dim), BF)] * 2
    else:
        grads = [jax.ShapeDtypeStruct((3, dim, dim), F32), jax.ShapeDtypeStruct((8, dim), F32)]
    wide, low = pltpu.VMEM((rows, dim), F32), pltpu.VMEM((rows, dim), BF)
    height, blocks = join_sources[-1].shape[-2:][0], 32
    stage_shape = join_sources[0].shape if len(join_sources) == 1 else (blocks, height, dim)
    return pl.pallas_call(
        partial(joining_kernel, halves=halves, count=len(join_sources)),
        out_shape=[
            jax.ShapeDtypeStruct((rows, dim), BF),
            jax.ShapeDtypeStruct((rows, dim), F32),
            jax.ShapeDtypeStruct((rows, dim), BF),
        ] + grads,
        in_specs=[SMEM] + [VMEM] * 4 + [ANY] * (len(sources) + len(join_sources) + 5),
        out_specs=[ANY, ANY, VMEM, ANY, ANY],
        scratch_shapes=[
            pltpu.VMEM(act.shape, BF),
            pltpu.VMEM((4, act.shape[1] // 4, dim), BF),
            pltpu.VMEM(adapt_down.shape, BF),
            pltpu.VMEM(up.shape, BF),
            pltpu.VMEM((3, dim, dim), BF),
            wide,
            low,
            WEIGHT_SEMS,
            WEIGHT_SEMS,
            pltpu.SemaphoreType.DMA((4,)),
            pltpu.SemaphoreType.DMA((4,)),
        ] + [wide] * 7 + [low] * 8 + [
            pltpu.VMEM((3, dim, dim), F32),
            pltpu.VMEM((2, 8, dim), F32),
            pltpu.VMEM((rows, 1), F32),
            pltpu.VMEM((rows, 1), F32),
            low,
            wide,
            pltpu.VMEM(grads[0].shape if halves else (8, 128), BF),
            pltpu.VMEM(grads[1].shape if halves else (8, 128), BF),
            pltpu.VMEM((8, dim), F32),
            pltpu.VMEM(stage_shape, BF),
            pltpu.VMEM((8, dim), F32),
            pltpu.SemaphoreType.DMA,
        ],
        compiler_params=limit(60),
        cost_estimate=cost(2 * rows * dim * (15 * dim + act.shape[1]), 2 * dim * (8 * dim + 10 * rows), 2 * rows * dim),
    )(spots, member, member_t, avail, norms, act, xhat1, cot, adapt_down, up, *join_sources, *sources)


def ffn_back_kernel(spots_ref, g_ref, rstd_ref, norms_ref, slope_hbm, g2_hbm, xhat_hbm, *refs, count):
    refs, (out_sources, in_sources) = refs[sum(count) :], (refs[: count[0]], refs[count[0] : sum(count)])
    g1_ref, slope_ref, g2_ref, xhat_ref, w_out_ref, w_in_ref, pre_ref, out_sems, in_sems, slope_sems, sems = refs
    planes, units = w_out_ref.shape[:2]
    fetch(spots_ref, out_sources, w_out_ref, out_sems)
    slopes = []
    for i, p in enumerate(planes_in_order(spots_ref, planes)):
        cols = pl.ds(pl.multiple_of(p * units, units), units)
        slopes.append((p, cols, pltpu.make_async_copy(slope_hbm.at[:, cols], slope_ref.at[:, cols], slope_sems.at[i])))
        slopes[-1][2].start()
    fetch(spots_ref, in_sources, w_in_ref, in_sems)
    loads = begin(((g2_hbm, g2_ref), (xhat_hbm, xhat_ref)), sems)
    for p, cols, load in slopes:
        arrive(w_out_ref, out_sems, p)
        load.wait()
        pre_ref[p] = (mm_t(g_ref[...], w_out_ref[p]) * slope_ref[:, cols].astype(F32)).astype(BF)
    total = None
    for p, _, _ in slopes:
        arrive(w_in_ref, in_sems, p)
        term = mm_t(pre_ref[p], w_in_ref[p])
        total = term if total is None else total + term
    for load in loads:
        load.wait()
    g1_ref[...] = norm_back(total + g2_ref[...], norms_ref[0:1, :], xhat_ref[...], rstd_ref[...])


def ffn_backward(spots, g_ffn, slope, out_sources, in_sources, g2, xhat, rstd, norms):
    rows, dim = xhat.shape
    planes = 4
    units = slope.shape[1] // planes
    return pl.pallas_call(
        partial(ffn_back_kernel, count=(len(out_sources), len(in_sources))),
        out_shape=jax.ShapeDtypeStruct((rows, dim), F32),
        in_specs=[SMEM] + [VMEM] * 3 + [ANY] * (len(out_sources) + len(in_sources) + 3),
        out_specs=VMEM,
        scratch_shapes=[
            pltpu.VMEM(slope.shape, BF), pltpu.VMEM((rows, dim), F32), pltpu.VMEM((rows, dim), F32),
            pltpu.VMEM((planes, units, dim), BF), pltpu.VMEM((planes, dim, units), BF), pltpu.VMEM((planes, rows, units), BF),
            WEIGHT_SEMS, WEIGHT_SEMS, WEIGHT_SEMS, pltpu.SemaphoreType.DMA((2,)),
        ],
        compiler_params=limit(60),
        cost_estimate=cost(4 * rows * dim * units * planes, 2 * planes * units * (2 * dim + rows)),
    )(spots, g_ffn, rstd, norms, slope, g2, xhat, *out_sources, *in_sources)


def attention_back_kernel(spots_ref, g1_ref, *refs):
    *refs, out_ref, w_ref, q_ref, k_ref, v_ref, p_ref, ctx_ref, dq_ref, dk_ref, dv_ref, w_sems, sems = refs
    *sources, q_hbm, k_hbm, v_hbm, p_hbm = refs
    rows, dim = g1_ref.shape
    seq_len = p_ref.shape[1]
    scale = 1.0 / math.sqrt(dim // HEADS)
    fetch(spots_ref, sources, w_ref, w_sems, True)
    half = p_ref.shape[0] // 2
    halves = [(p_hbm.at[pl.ds(i * half, half)], p_ref.at[pl.ds(i * half, half)]) for i in range(2)]
    loads = begin(((v_hbm, v_ref), (q_hbm, q_ref), (k_hbm, k_ref), *halves), sems)
    arrive(w_ref, w_sems, 3)
    ctx_ref[...] = mm_t(g1_ref[...].astype(BF), w_ref[3]).astype(BF)
    for load in loads:
        load.wait()
    masks, first = head_masks()

    def one_seq(s, _):
        at = pl.ds(pl.multiple_of(s * seq_len, seq_len), seq_len)
        for j in range(HEADS // 2):
            cols = slice(128 * j, 128 * (j + 1))
            q, k, v, g = q_ref[at, cols], k_ref[at, cols], v_ref[at, cols], ctx_ref[at, cols]
            dq, dk, dv = [], [], []
            for h in range(2):
                probs_low = p_ref[s * HEADS + 2 * j + h]
                probs = probs_low.astype(F32)
                g_probs = mm_t(v, g * masks[h])
                g_scores = (probs * (g_probs - jnp.sum(g_probs * probs, axis=0, keepdims=True))).astype(BF)
                dv.append(mm(probs_low, g))
                dk.append(mm(g_scores, q))
                dq.append(t_mm(g_scores, k))
            dq_ref[at, cols] = (jnp.where(first, dq[0], dq[1]) * scale).astype(BF)
            dk_ref[at, cols] = jnp.where(first, dk[0], dk[1]).astype(BF)
            dv_ref[at, cols] = jnp.where(first, dv[0], dv[1]).astype(BF)
        return 0

    lax.fori_loop(0, rows // seq_len, one_seq, 0)
    for m in range(3):
        arrive(w_ref, w_sems, m)
    total = g1_ref[...] + mm(dq_ref[...], w_ref[0])
    total = total + mm(dk_ref[...], w_ref[1])
    out_ref[...] = (total + mm(dv_ref[...], w_ref[2])).astype(BF)


def attention_backward(spots, g1, sources, q, k, v, probs):
    rows, dim = g1.shape
    seq_len = probs.shape[1]
    low = pltpu.VMEM((rows, dim), BF)
    return pl.pallas_call(
        attention_back_kernel,
        out_shape=jax.ShapeDtypeStruct((rows, dim), BF),
        in_specs=[SMEM, VMEM] + [ANY] * (len(sources) + 4),
        out_specs=VMEM,
        scratch_shapes=[pltpu.VMEM((4, dim, dim), BF), low, low, low, pltpu.VMEM(probs.shape, BF), low, low, low, low,
                        WEIGHT_SEMS, pltpu.SemaphoreType.DMA((5,))],
        compiler_params=limit(60),
        cost_estimate=cost(2 * rows * dim * (4 * dim + 4 * seq_len), 2 * (4 * dim * dim + 8 * rows * dim)),
    )(spots, g1, *sources, q, k, v, probs)


def shards(
    tokens, lengths, adapter_mask, cotangent, att_query, att_key, att_value, att_out,
    norm1_gain, norm1_bias, ffn_in, ffn_bias, ffn_out, adapt_down, adapt_up, norm2_gain,
    norm2_bias, joining_query, joining_key, joining_value, joining_qbias, joining_vbias,
):
    groups = lax.axis_size("tensor")
    dp_size = lax.axis_size("dp")
    my_z = lax.axis_index("tensor")
    my_d = lax.axis_index("dp")
    seq_local, seq_len, dim = tokens.shape
    mine = seq_local // groups
    rows = mine * seq_len
    adapters, neck = adapt_up.shape[0], adapt_up.shape[1]
    own_rows = joining_query.shape[0]

    gather = Gather(dp_size, groups, my_d, my_z, mine)
    spots = gather.spots
    biases = lax.dynamic_update_slice(
        jnp.zeros((8, dim), BF), jnp.stack([joining_qbias, joining_vbias]), (0, (my_d * groups + my_z) * own_rows)
    )
    att_mats = [att_query.T, att_key.T, att_value.T, att_out]
    att_pack = jnp.concatenate(att_mats, axis=0)
    join_part = jnp.concatenate([joining_query, joining_key, joining_value, biases], axis=0)
    parts = [gather.part_of(att_pack), gather.part_of(ffn_in), join_part, gather.part_of(ffn_out)]

    def my_slice(array):
        return lax.dynamic_slice_in_dim(array, my_z * mine, mine, 0)

    x = my_slice(tokens).reshape(rows, dim)
    shifts = jnp.arange(128, dtype=jnp.int32)
    bits = jnp.right_shift(my_slice(adapter_mask)[:, None], jnp.minimum(shifts, adapters)[None, :]) % 2
    avail = jnp.where(shifts[None, :] < adapters, bits, 0)[:, None, :]
    norms = jnp.stack([norm1_gain, norm1_bias, norm2_gain, norm2_bias])
    lens = my_slice(lengths)
    owner = jnp.arange(adapters * neck, dtype=jnp.int32) // neck
    member = (owner[:, None] == shifts[None, :]).astype(BF)
    member_t = (shifts[:, None] == owner[None, :]).astype(BF)
    kept = {}

    def attend(sources):
        kept["att"] = attention_forward(spots, lens, x, sources, norms, seq_len)
        return [kept["att"][4]]

    def feed(sources):
        kept["ffn"] = ffn_forward(spots, kept["att"][4], sources, ffn_bias, ffn_in.shape[1])
        return [kept["ffn"][0]]

    if gather.paired:
        own = [att_pack, ffn_in, None, ffn_out]
        steps = [
            lambda got: [x, norms, lens, avail, member, member_t, spots],
            lambda got: [],
            lambda got: attend(got[0] + own[:1]),
            lambda got: feed(got[1] + own[1:2]),
            lambda got: [],
            lambda got: [],
        ]
        quarter = att_mats[3]
        for i in range(3):
            quarter = jnp.where(my_d // 2 == i, att_mats[i], quarter)
        rounds = [(gather.half_of(quarter), quarter)]
        for shard in (ffn_in, ffn_out):
            shard = tie(shard, *rounds[0])
            rounds.append((gather.part_of(shard), gather.quarter_of(shard)))
        join_part = tie(join_part, *rounds[0])
        theirs = send(join_part, CORE)
        even = lax.rem(my_d, 2) == 0
        pair = jnp.concatenate([jnp.where(even, join_part, theirs), jnp.where(even, theirs, join_part)], axis=0)
        rounds.insert(2, (join_part, pair, join_part, theirs))
        got = gather.all_rounds(rounds, steps)
        att_sources, in_sources, out_sources = (got[i] + [own[i]] for i in (0, 1, 3))
        join_sources = got[2]
    else:
        att_sources, in_sources, out_sources = (gather.whole(parts[i], i == 0) for i in (0, 1, 3))
        join_sources = [lax.all_gather(parts[2], ("dp", "tensor"), axis=0)]
    up = adapt_up.reshape(adapters * neck, dim)
    cot = cotangent.reshape(rows, dim)

    def rest(att, ffn, avail, cot):
        q, k, v, probs, low1, xhat1, rstd1 = att
        act, slope = ffn
        layer_out, g2, g_ffn, *grads = joining(
            spots, gather.paired, act, out_sources, adapt_down, up, join_sources, member, member_t, avail, xhat1, norms, cot
        )
        g1 = ffn_backward(spots, g_ffn, slope, out_sources, in_sources, g2, xhat1, rstd1, norms)
        return layer_out, attention_backward(spots, g1, att_sources, q, k, v, probs), grads

    if gather.paired:
        layer_out, input_grad, grads = rest(kept["att"], kept["ffn"], avail, cot)
    else:
        step = 2 - mine % 2
        outs = []
        for first in range(0, mine, step):
            at = slice(first * seq_len, (first + step) * seq_len)
            att = attention_forward(spots, lens[first : first + step], x[at], att_sources, norms, seq_len)
            ffn = ffn_forward(spots, att[4], in_sources, ffn_bias, ffn_in.shape[1])
            outs.append(rest(att, ffn, avail[first : first + step], cot[at]))
        layer_out, input_grad = (jnp.concatenate([out[i] for out in outs]) for i in range(2))
        grads = [sum(out[2][i] for out in outs) for i in range(2)]
    d_q, d_k, d_v, d_bias = reduce_grads(gather, grads, own_rows)
    d_bias = lax.dynamic_slice_in_dim(d_bias[:2], (my_d * groups + my_z) * own_rows, own_rows, 1)
    return (
        layer_out.reshape(mine, seq_len, dim),
        input_grad.reshape(mine, seq_len, dim),
        d_q, d_k, d_v, d_bias[0], d_bias[1],
    )


def solution(mesh):
    both = P(ALL, None)
    return jax.shard_map(
        shards,
        mesh=mesh,
        in_specs=(
            P("dp", None, None), P("dp"), P("dp"), P(ALL, None, None),
            P(None, "tensor"), P(None, "tensor"), P(None, "tensor"), P("tensor", None),
            P(), P(), P(None, "tensor"), P(), P("tensor", None), P(), P(), P(), P(),
            both, both, both, P(ALL), P(ALL),
        ),
        out_specs=(P(ALL, None, None), P(ALL, None, None), both, both, both, P(ALL), P(ALL)),
        check_vma=False,
    )
```

time: 220 us -> 217 us (0.986); the launches traced: 220 us -> 214 us
  waiting for transfers between devices: 59.9 us -> 49.8 us
  local copies, waits for them, and re-layouts: 14.5 us -> 19.5 us
  starting transfers between devices: 40 us -> 35.1 us
  other arithmetic: 7.1 us -> 10.2 us
    ppermute x15 -> x7, waiting for transfers between devices: 39.3 us -> 23.4 us  [shift(): lax.ppermute(array, 'tensor', [(i, (i + by) % groups) for i in range(grou...]
    ppermute x15 -> x7, starting transfers between devices: 20.4 us -> 6.03 us  [shift(): lax.ppermute(array, 'tensor', [(i, (i + by) % groups) for i in range(grou...]
    ppermute x0 -> x4, starting transfers between devices: none -> 10.1 us  [scoped(): return step(*args)]
    ppermute x32 -> x31, waiting for transfers between devices: 20.5 us -> 26.4 us  [send(): return lax.ppermute(array, 'dp', pairs)]
    pallas_call x3 -> x6, Pallas kernels: 50.3 us -> 55.8 us  [the longest x1 35.9 us: joining(): pl.pallas_call(partial(joining_kernel, halves=halves, count=len(join_sour...]
    pallas_call x1, Pallas kernels: 13.8 us -> 8.72 us  [ffn_forward(): pl.pallas_call(ffn_in_kernel, out_shape=[out, out], in_specs=[SMEM] + [VM...]
    select_n x1 -> x4, other arithmetic: 0.01 us -> 3.75 us  [the longest x1 2.07 us: shards(): quarter = jnp.where(my_d // 2 == i, att_mats[i], quarter)]
    dynamic_slice x0 -> x2, local copies, waits for them, and re-layouts: none -> 3.38 us  [quarter_of(): return lax.dynamic_slice_in_dim(shard, self.my_d // 2 * rows, rows, 0)]
  transfers between devices with their start and end apart: 47 -> 42, of which waited for: 11 -> 14; matrix products, arithmetic and copies ran while one was open for 6% -> 10% of each run, Pallas kernels for 28% -> 25%
where the time goes in v4:
time: 217 us; the launch traced here: 214 us
  Pallas kernels  97.8 us (45%)
  waiting for transfers between devices  49.8 us (23%)
  starting transfers between devices  35.1 us (16%)
  local copies, waits for them, and re-layouts  19.5 us (9%)
  other arithmetic  10.2 us (5%)
    pallas_call x1, Pallas kernels, joining(): pl.pallas_call(partial(joining_kernel, halves=halves, count=len(join_sour...  35.9 us
    ppermute x31, waiting for transfers between devices, send(): return lax.ppermute(array, 'dp', pairs)  26.4 us
    ppermute x7, waiting for transfers between devices, shift(): lax.ppermute(array, 'tensor', [(i, (i + by) % groups) for i in range(grou...  23.4 us
    ppermute x31, starting transfers between devices, send(): return lax.ppermute(array, 'dp', pairs)  19 us
    pallas_call x1, Pallas kernels, attention_backward(): pl.pallas_call(attention_back_kernel, out_shape=jax.ShapeDtypeStruct((row...  15.6 us
    pallas_call x1, Pallas kernels, ffn_backward(): pl.pallas_call(partial(ffn_back_kernel, count=(len(out_sources), len(in_s...  15.2 us
    pallas_call x1, Pallas kernels, attention_forward(): pl.pallas_call(attention_kernel, out_shape=[low, low, low, jax.ShapeDtype...  12.8 us
    ppermute x4, starting transfers between devices, scoped(): return step(*args)  10.1 us
  transfers between devices with their start and end apart: 42, of which 14 were waited for; matrix products, arithmetic and copies ran while one was open for 10% of the time, Pallas kernels for 25%

profile of v4, /device:TPU:0, one launch (start us, length us, event | category | flops | bytes accessed | tf_op | source)
XLA Modules:
  0.0 213.8 jit_solution(12469592503947907290)
XLA Ops:
  0.7 2.1 select_select_fusion
  2.8 5.0 %collective-permute-start = (bf16[192,768]{1,0:T(8,128)(2,1)}, bf16[192,768]{1,0:T(8,128)(2,1)}, u32[]{:S(2)}, u32[]{:S(2)}) collective-permute-start(bf16[192,768]{1,0:T(8,128)(2,1)} %select_select_fusion), channel_id=1, source_target_pairs={{0,3},{1,0},{2,1},{3,2},{4,5},{5,6},{6,7},{7,4},{8,11},{9,8},{10,9... | collective-permute-start | bytes 884744 | tf_op jit(solution)/shard_map/planes0/beside/ppermute | solution.py:79
  13.2 1.7 constant_dynamic-slice_fusion.3
  17.9 3.5 %collective-permute-done.1.refs_1_ = bf16[96,768]{1,0:T(8,128)(2,1)S(1)} collective-permute-done((bf16[96,768]{1,0:T(8,128)(2,1)}, bf16[96,768]{1,0:T(8,128)(2,1)S(1)}, u32[]{:S(2)}, u32[]{:S(2)}) %collective-permute-start.1) | collective-permute-done | bytes 147488 | tf_op jit(solution)/shard_map/planes0/across/ppermute | solution.py:74
  33.8 8.8 %collective-permute-done.6.refs_1_ = bf16[96,768]{1,0:T(8,128)(2,1)S(1)} collective-permute-done((bf16[96,768]{1,0:T(8,128)(2,1)S(1)}, bf16[96,768]{1,0:T(8,128)(2,1)S(1)}, u32[]{:S(2)}, u32[]{:S(2)}) %collective-permute-start.6) | collective-permute-done | bytes 147488 | tf_op jit(solution)/shard_map/round0/planes1/across/ppermute | solution.py:74
  46.9 1.8 collective-permute-start.10
  48.7 11.0 %collective-permute-done.11.refs_1_ = bf16[80,768]{1,0:T(8,128)(2,1)S(1)} collective-permute-done((bf16[80,768]{1,0:T(8,128)(2,1)S(1)}, bf16[80,768]{1,0:T(8,128)(2,1)S(1)}, u32[]{:S(2)}, u32[]{:S(2)}) %collective-permute-start.11) | collective-permute-done | bytes 122912 | tf_op jit(solution)/shard_map/round1/planes2/across/ppermute | solution.py:74
  59.7 3.4 %collective-permute-done.12.refs_1_.refs_10_ = bf16[6,96,768]{2,1,0:T(8,128)(2,1)} collective-permute-done((bf16[6,96,768]{2,1,0:T(8,128)(2,1)S(1)}, bf16[6,96,768]{2,1,0:T(8,128)(2,1)}, u32[]{:S(2)}, u32[]{:S(2)}) %collective-permute-start.12) | collective-permute-done | bytes 884768 | tf_op jit(solution)/shard_map/round1/near/ppermute | solution.py:70
  73.3 12.8 %round2.2 = (bf16[512,768]{1,0:T(8,128)(2,1)}, bf16[512,768]{1,0:T(8,128)(2,1)}, bf16[512,768]{1,0:T(8,128)(2,1)}, bf16[24,256,256]{2,1,0:T(8,128)(2,1)}, bf16[5...) custom-call(s32[9]{0:T(128)} %copy-done.9, s32[2]{0:T(128)} %dynamic_slice.25.len_ref, ...), custom_call_target="tpu_custom_call" | custom-call | flops 2818572288 | bytes 11010048 | tf_op jit(solution)/shard_map/round2/pallas_call | solution.py:375
  87.2 1.8 slice.28
  89.1 1.9 collective-permute-start.28
  95.3 8.7 %round3.2 = (bf16[512,3072]{1,0:T(8,128)(2,1)}, bf16[512,3072]{1,0:T(8,128)(2,1)}) custom-call(s32[9]{0:T(128)} %copy-done.9, bf16[512,768]{1,0:T(8,128)(2,1)} %get-tuple-element.75.x_ref, f32[4,1,768]{2,1,0:T(1,128)} %bitcast.26, bf16[6,96,768]{2,1,0:T(8,128)(2,1)} %copy-done.2, bf16[6,96,768]{2,1,0:T(8,128)(2,1)} %collective-permute-done.12.refs_1_.refs_10_, ...), custom_call_target="tpu_custom_call" | custom-call | flops 2415919104 | bytes 11010048 | tf_op jit(solution)/shard_map/round3/pallas_call | solution.py:417
  104.1 3.2 %collective-permute-done.27.refs_10_.refs_3_ = bf16[3,96,768]{2,1,0:T(8,128)(2,1)} collective-permute-done((bf16[3,96,768]{2,1,0:T(8,128)(2,1)}, bf16[3,96,768]{2,1,0:T(8,128)(2,1)}, u32[]{:S(2)}, u32[]{:S(2)}) %collective-permute-start.27) | collective-permute-done | bytes 442400 | tf_op jit(solution)/shard_map/round3/near/ppermute | solution.py:70
  110.0 5.8 %collective-permute-done.31.refs_11_.refs_4_ = bf16[3,96,768]{2,1,0:T(8,128)(2,1)S(1)} collective-permute-done((bf16[3,96,768]{2,1,0:T(8,128)(2,1)}, bf16[3,96,768]{2,1,0:T(8,128)(2,1)S(1)}, u32[]{:S(2)}, u32[]{:S(2)}) %collective-permute-start.31) | collective-permute-done | bytes 442400 | tf_op jit(solution)/shard_map/round4/far/ppermute | solution.py:70
  118.4 35.9 %shard_map.279 = (bf16[512,768]{1,0:T(8,128)(2,1)}, f32[512,768]{1,0:T(8,128)}, bf16[512,768]{1,0:T(8,128)(2,1)}, bf16[4,304,768]{2,1,0:T(8,128)(2,1)}, bf16[4,304,768]{2,1,0:T(8,128)(2,1)}) custom-call(s32[9]{0:T(128)} %copy-done.9, bf16[768,128]{1,0:T(8,128)(2,1)} %fusion.member_ref, bf16[128,768]{1,0:T(8,128)(2,1)} %fusion.1.member_t_ref, ...), custom_call_target="tpu_custom_call" | custom-call | flops 11475615744 | bytes 17301504 | tf_op jit(solution)/shard_map/pallas_call | solution.py:674
  154.9 3.7 %collective-permute-done.35.come_ref = bf16[4,304,768]{2,1,0:T(8,128)(2,1)S(1)} collective-permute-done((bf16[4,304,768]{2,1,0:T(8,128)(2,1)}, bf16[4,304,768]{2,1,0:T(8,128)(2,1)S(1)}, u32[]{:S(2)}, u32[]{:S(2)}) %collective-permute-start.35) | collective-permute-done | bytes 1867808 | tf_op jit(solution)/shard_map/cores/ppermute | solution.py:70
  160.0 1.8 shard_map.282
  166.3 15.2 %shard_map.280.g1_ref = f32[512,768]{1,0:T(8,128)} custom-call(s32[9]{0:T(128)} %copy-done.9, bf16[512,768]{1,0:T(8,128)(2,1)} %get-tuple-element.94.g_ref, f32[512,1]{1,0:T(8,128)} %get-tuple-element.95.rstd_ref, f32[4,768]{1,0:T(4,128)} %pad_maximum_fusion.3.norms_ref, bf16[512,3072]{1,0:T(8,128)(2,1)} %get-tuple-element.96.slope_hbm, ...), custom_call_target="tpu_custom_call" | custom-call | flops 4831838208 | bytes 12582912 | tf_op jit(solution)/shard_map/pallas_call | solution.py:744
  181.5 4.0 %collective-permute-done.37.y_ref = bf16[304,768]{1,0:T(8,128)(2,1)} collective-permute-done((bf16[304,768]{1,0:T(8,128)(2,1)}, bf16[304,768]{1,0:T(8,128)(2,1)}, u32[]{:S(2)}, u32[]{:S(2)}) %collective-permute-start.37) | collective-permute-done | bytes 466976 | tf_op jit(solution)/shard_map/y/ppermute | solution.py:70
  185.5 1.7 collective-permute-done.38.far_ref
  188.4 2.3 %shard_map.283 = (f32[80,768]{1,0:T(8,128)S(1)}, bf16[96,768]{1,0:T(8,128)(2,1)}, bf16[96,768]{1,0:T(8,128)(2,1)}, bf16[96,768]{1,0:T(8,128)(2,1)S(1)}) custom-call(s32[9]{0:T(128)S(1)} %copy-done.12, f32[288,768]{1,0:T(8,128)S(1)} %copy-done.5, f32[8,768]{1,0:T(8,128)S(1)} %get-tuple-element.105.bias_ref, ...), custom_call_target="tpu_custom_call" | custom-call | tf_op jit(solution)/shard_map/pallas_call | solution.py:301
  190.7 2.1 collective-permute-start.39
  193.8 2.8 %collective-permute-start.41 = (bf16[96,768]{1,0:T(8,128)(2,1)S(1)}, bf16[96,768]{1,0:T(8,128)(2,1)S(1)}, u32[]{:S(2)}, u32[]{:S(2)}) collective-permute-start(bf16[96,768]{1,0:T(8,128)(2,1)S(1)} %get-tuple-element.112), channel_id=1, source_target_pairs={{0,3},{1,0},{2,1},{3,2},{4,7},{5,4},{6,5},{7,6},{8,11},{9,8},{10,9... | collective-permute-start | bytes 442376 | tf_op jit(solution)/shard_map/stack2/ppermute | solution.py:74
  196.6 15.6 %shard_map.281 = bf16[512,768]{1,0:T(8,128)(2,1)} custom-call(s32[9]{0:T(128)} %copy-done.9, f32[512,768]{1,0:T(8,128)} %shard_map.280.g1_ref, bf16[6,96,768]{2,1,0:T(8,128)(2,1)} %copy-done.1, bf16[6,96,768]{2,1,0:T(8,128)(2,1)} %copy-done.13, bf16[3,96,768]{2,1,0:T(8,128)(2,1)} %copy-done.19, bf16[6,96,768]{2,1,0:T(8,128)(2,1)} %copy-done.18, ...), custom_call_target="tpu_custom_call" | custom-call | flops 3221225472 | bytes 11010048 | tf_op jit(solution)/shard_map/pallas_call | solution.py:806
  (189 shorter events, 55.6 us)
Async XLA Ops:
  2.8 18.6 %collective-permute-start = (bf16[192,768]{1,0:T(8,128)(2,1)}, bf16[192,768]{1,0:T(8,128)(2,1)}, u32[]{:S(2)}, u32[]{:S(2)}) collective-permute-start(bf16[192,768]{1,0:T(8,128)(2,1)} %select_select_fusion), channel_id=1, source_target_pairs={{0,3},{1,0},{2,1},{3,2},{4,5},{5,6},{6,7},{7,4},{8,11},{9,8},{10,9... | collective-permute-start | bytes 884744 | tf_op jit(solution)/shard_map/planes0/beside/ppermute | solution.py:79
  9.5 11.9 %collective-permute-start.1 = (bf16[96,768]{1,0:T(8,128)(2,1)}, bf16[96,768]{1,0:T(8,128)(2,1)S(1)}, u32[]{:S(2)}, u32[]{:S(2)}) collective-permute-start(bf16[96,768]{1,0:T(8,128)(2,1)} %slice_select_fusion), channel_id=1, source_target_pairs={{0,2},{1,3},{2,0},{3,1},{4,6},{5,7},{6,4},{7,5},{8,10},{9,11},{10,... | collective-permute-start | bytes 442376 | tf_op jit(solution)/shard_map/planes0/across/ppermute | solution.py:74
  24.8 17.9 %collective-permute-start.7 = (bf16[6,96,768]{2,1,0:T(8,128)(2,1)S(1)}, bf16[6,96,768]{2,1,0:T(8,128)(2,1)S(1)}, u32[]{:S(2)}, u32[]{:S(2)}) collective-permute-start(bf16[6,96,768]{2,1,0:T(8,128)(2,1)S(1)} %round0.1.refs_0_), channel_id=1, source_target_pairs={{0,8},{4,20},{8,0},{12,28},{16,24},{20,4},{24,16},{28,12},{1,9},{5... | collective-permute-start | bytes 2654216 | tf_op jit(solution)/shard_map/round0/near/ppermute | solution.py:70
  28.0 14.7 %collective-permute-start.5 = (bf16[192,768]{1,0:T(8,128)(2,1)S(1)}, bf16[192,768]{1,0:T(8,128)(2,1)S(1)}, u32[]{:S(2)}, u32[]{:S(2)}) collective-permute-start(bf16[192,768]{1,0:T(8,128)(2,1)S(1)} %copy-done.25), channel_id=1, source_target_pairs={{0,3},{1,0},{2,1},{3,2},{4,5},{5,6},{6,7},{7,4},{8,11},{9,8},{10,9... | collective-permute-start | bytes 884744 | tf_op jit(solution)/shard_map/round0/planes1/beside/ppermute | solution.py:79
  31.0 11.7 %collective-permute-start.6 = (bf16[96,768]{1,0:T(8,128)(2,1)S(1)}, bf16[96,768]{1,0:T(8,128)(2,1)S(1)}, u32[]{:S(2)}, u32[]{:S(2)}) collective-permute-start(bf16[96,768]{1,0:T(8,128)(2,1)S(1)} %copy-done.27), channel_id=1, source_target_pairs={{0,2},{1,3},{2,0},{3,1},{4,6},{5,7},{6,4},{7,5},{8,10},{9,11},{10,... | collective-permute-start | bytes 442376 | tf_op jit(solution)/shard_map/round0/planes1/across/ppermute | solution.py:74
  43.3 16.4 %collective-permute-start.14 = (bf16[6,96,768]{2,1,0:T(8,128)(2,1)S(1)}, bf16[6,96,768]{2,1,0:T(8,128)(2,1)S(1)}, u32[]{:S(2)}, u32[]{:S(2)}) collective-permute-start(bf16[6,96,768]{2,1,0:T(8,128)(2,1)S(1)} %collective-permute-done.7.refs_1_), channel_id=1, source_target_pairs={{0,4},{4,0},{8,12},{12,8},{16,20},{20,16},{24,28},{28,24},{1,5},{5... | collective-permute-start | bytes 2654216 | tf_op jit(solution)/shard_map/round1/swap/ppermute | solution.py:70
  45.2 18.0 %collective-permute-start.12 = (bf16[6,96,768]{2,1,0:T(8,128)(2,1)S(1)}, bf16[6,96,768]{2,1,0:T(8,128)(2,1)}, u32[]{:S(2)}, u32[]{:S(2)}) collective-permute-start(bf16[6,96,768]{2,1,0:T(8,128)(2,1)S(1)} %round1.1.refs_0_.refs_9_), channel_id=1, source_target_pairs={{0,8},{4,20},{8,0},{12,28},{16,24},{20,4},{24,16},{28,12},{1,9},{5... | collective-permute-start | bytes 2654216 | tf_op jit(solution)/shard_map/round1/near/ppermute | solution.py:70
  46.5 13.2 %collective-permute-start.13 = (bf16[3,96,768]{2,1,0:T(8,128)(2,1)S(1)}, bf16[3,96,768]{2,1,0:T(8,128)(2,1)S(1)}, u32[]{:S(2)}, u32[]{:S(2)}) collective-permute-start(bf16[3,96,768]{2,1,0:T(8,128)(2,1)S(1)} %slice.26), channel_id=1, source_target_pairs={{0,20},{4,8},{8,28},{12,0},{16,4},{20,24},{24,12},{28,16},{1,21},{... | collective-permute-start | bytes 1327112 | tf_op jit(solution)/shard_map/round1/far/ppermute | solution.py:70
  46.9 12.8 %collective-permute-start.10 = (bf16[160,768]{1,0:T(8,128)(2,1)S(1)}, bf16[160,768]{1,0:T(8,128)(2,1)S(1)}, u32[]{:S(2)}, u32[]{:S(2)}) collective-permute-start(bf16[160,768]{1,0:T(8,128)(2,1)S(1)} %copy-done.26), channel_id=1, source_target_pairs={{0,3},{1,0},{2,1},{3,2},{4,5},{5,6},{6,7},{7,4},{8,11},{9,8},{10,9... | collective-permute-start | bytes 737288 | tf_op jit(solution)/shard_map/round1/planes2/beside/ppermute | solution.py:79
  48.7 11.0 %collective-permute-start.11 = (bf16[80,768]{1,0:T(8,128)(2,1)S(1)}, bf16[80,768]{1,0:T(8,128)(2,1)S(1)}, u32[]{:S(2)}, u32[]{:S(2)}) collective-permute-start(bf16[80,768]{1,0:T(8,128)(2,1)S(1)} %pad_maximum_fusion.2.refs_4_), channel_id=1, source_target_pairs={{0,2},{1,3},{2,0},{3,1},{4,6},{5,7},{6,4},{7,5},{8,10},{9,11},{10,... | collective-permute-start | bytes 368648 | tf_op jit(solution)/shard_map/round1/planes2/across/ppermute | solution.py:74
  66.4 19.7 %collective-permute-start.20 = (bf16[8,80,768]{2,1,0:T(8,128)(2,1)}, bf16[8,80,768]{2,1,0:T(8,128)(2,1)}, u32[]{:S(2)}, u32[]{:S(2)}) collective-permute-start(bf16[8,80,768]{2,1,0:T(8,128)(2,1)} %round2.3.refs_2_), channel_id=1, source_target_pairs={{0,8},{4,20},{8,0},{12,28},{16,24},{20,4},{24,16},{28,12},{1,9},{5... | collective-permute-start | bytes 2949128 | tf_op jit(solution)/shard_map/round2/near/ppermute | solution.py:70
  67.6 18.6 %collective-permute-start.22 = (bf16[6,96,768]{2,1,0:T(8,128)(2,1)}, bf16[6,96,768]{2,1,0:T(8,128)(2,1)}, u32[]{:S(2)}, u32[]{:S(2)}) collective-permute-start(bf16[6,96,768]{2,1,0:T(8,128)(2,1)} %collective-permute-done.12.refs_1_.refs_10_), channel_id=1, source_target_pairs={{0,4},{4,0},{8,12},{12,8},{16,20},{20,16},{24,28},{28,24},{1,5},{5... | collective-permute-start | bytes 2654216 | tf_op jit(solution)/shard_map/round2/swap/ppermute | solution.py:70
  69.1 17.0 %collective-permute-start.21 = (bf16[3,96,768]{2,1,0:T(8,128)(2,1)S(1)}, bf16[3,96,768]{2,1,0:T(8,128)(2,1)}, u32[]{:S(2)}, u32[]{:S(2)}) collective-permute-start(bf16[3,96,768]{2,1,0:T(8,128)(2,1)S(1)} %slice.27), channel_id=1, source_target_pairs={{0,20},{4,8},{8,28},{12,0},{16,4},{20,24},{24,12},{28,16},{1,21},{... | collective-permute-start | bytes 1327112 | tf_op jit(solution)/shard_map/round2/far/ppermute | solution.py:70
  69.7 16.4 %collective-permute-start.18 = (bf16[192,768]{1,0:T(8,128)(2,1)}, bf16[192,768]{1,0:T(8,128)(2,1)S(1)}, u32[]{:S(2)}, u32[]{:S(2)}) collective-permute-start(bf16[192,768]{1,0:T(8,128)(2,1)} %constant_dynamic-slice_fusion.1), channel_id=1, source_target_pairs={{0,3},{1,0},{2,1},{3,2},{4,5},{5,6},{6,7},{7,4},{8,11},{9,8},{10,9... | collective-permute-start | bytes 884744 | tf_op jit(solution)/shard_map/round2/planes3/beside/ppermute | solution.py:79
  73.3 12.8 %collective-permute-start.19 = (bf16[96,768]{1,0:T(8,128)(2,1)}, bf16[96,768]{1,0:T(8,128)(2,1)S(1)}, u32[]{:S(2)}, u32[]{:S(2)}) collective-permute-start(bf16[96,768]{1,0:T(8,128)(2,1)} %constant_dynamic-slice_fusion.2), channel_id=1, source_target_pairs={{0,2},{1,3},{2,0},{3,1},{4,6},{5,7},{6,4},{7,5},{8,10},{9,11},{10,... | collective-permute-start | bytes 442376 | tf_op jit(solution)/shard_map/round2/planes3/across/ppermute | solution.py:74
  86.1 21.2 %collective-permute-start.29 = (bf16[8,80,768]{2,1,0:T(8,128)(2,1)}, bf16[8,80,768]{2,1,0:T(8,128)(2,1)}, u32[]{:S(2)}, u32[]{:S(2)}) collective-permute-start(bf16[8,80,768]{2,1,0:T(8,128)(2,1)} %collective-permute-done.20.refs_3_), channel_id=1, source_target_pairs={{0,4},{4,0},{8,12},{12,8},{16,20},{20,16},{24,28},{28,24},{1,5},{5... | collective-permute-start | bytes 2949128 | tf_op jit(solution)/shard_map/round3/swap/ppermute | solution.py:70
  89.1 15.0 %collective-permute-start.28 = (bf16[4,80,768]{2,1,0:T(8,128)(2,1)}, bf16[4,80,768]{2,1,0:T(8,128)(2,1)}, u32[]{:S(2)}, u32[]{:S(2)}) collective-permute-start(bf16[4,80,768]{2,1,0:T(8,128)(2,1)} %slice.28), channel_id=1, source_target_pairs={{0,20},{4,8},{8,28},{12,0},{16,4},{20,24},{24,12},{28,16},{1,21},{... | collective-permute-start | bytes 1474568 | tf_op jit(solution)/shard_map/round3/far/ppermute | solution.py:70
  93.8 13.6 %collective-permute-start.27 = (bf16[3,96,768]{2,1,0:T(8,128)(2,1)}, bf16[3,96,768]{2,1,0:T(8,128)(2,1)}, u32[]{:S(2)}, u32[]{:S(2)}) collective-permute-start(bf16[3,96,768]{2,1,0:T(8,128)(2,1)} %get-tuple-element.88.refs_8_.refs_1_), channel_id=1, source_target_pairs={{0,8},{4,20},{8,0},{12,28},{16,24},{20,4},{24,16},{28,12},{1,9},{5... | collective-permute-start | bytes 1327112 | tf_op jit(solution)/shard_map/round3/near/ppermute | solution.py:70
  162.8 18.7 %collective-permute-start.36 = (bf16[304,768]{1,0:T(8,128)(2,1)}, bf16[304,768]{1,0:T(8,128)(2,1)S(1)}, u32[]{:S(2)}, u32[]{:S(2)}) collective-permute-start(bf16[304,768]{1,0:T(8,128)(2,1)} %get-tuple-element.106), channel_id=1, source_target_pairs={{0,8},{4,12},{8,0},{12,4},{16,24},{20,28},{24,16},{28,20},{1,9},{5... | collective-permute-start | bytes 1400840 | tf_op jit(solution)/shard_map/x/ppermute | solution.py:70
  164.2 21.3 %collective-permute-start.37 = (bf16[304,768]{1,0:T(8,128)(2,1)}, bf16[304,768]{1,0:T(8,128)(2,1)}, u32[]{:S(2)}, u32[]{:S(2)}) collective-permute-start(bf16[304,768]{1,0:T(8,128)(2,1)} %get-tuple-element.107), channel_id=1, source_target_pairs={{0,16},{4,20},{8,24},{12,28},{16,0},{20,4},{24,8},{28,12},{1,17},{... | collective-permute-start | bytes 1400840 | tf_op jit(solution)/shard_map/y/ppermute | solution.py:70
  164.9 22.3 %collective-permute-start.38 = (bf16[304,768]{1,0:T(8,128)(2,1)}, bf16[304,768]{1,0:T(8,128)(2,1)}, u32[]{:S(2)}, u32[]{:S(2)}) collective-permute-start(bf16[304,768]{1,0:T(8,128)(2,1)} %get-tuple-element.108), channel_id=1, source_target_pairs={{0,24},{4,28},{8,16},{12,20},{16,8},{20,12},{24,0},{28,4},{1,25},{... | collective-permute-start | bytes 1400840 | tf_op jit(solution)/shard_map/far/ppermute | solution.py:70
  190.7 21.5 %collective-permute-start.39 = (bf16[96,768]{1,0:T(8,128)(2,1)}, bf16[96,768]{1,0:T(8,128)(2,1)S(1)}, u32[]{:S(2)}, u32[]{:S(2)}) collective-permute-start(bf16[96,768]{1,0:T(8,128)(2,1)} %get-tuple-element.110), channel_id=1, source_target_pairs={{0,1},{1,2},{2,3},{3,0},{4,5},{5,6},{6,7},{7,4},{8,9},{9,10},{10,1... | collective-permute-start | bytes 442376 | tf_op jit(solution)/shard_map/stack0/ppermute | solution.py:74
  192.8 19.4 %collective-permute-start.40 = (bf16[96,768]{1,0:T(8,128)(2,1)}, bf16[96,768]{1,0:T(8,128)(2,1)S(1)}, u32[]{:S(2)}, u32[]{:S(2)}) collective-permute-start(bf16[96,768]{1,0:T(8,128)(2,1)} %get-tuple-element.111), channel_id=1, source_target_pairs={{0,2},{1,3},{2,0},{3,1},{4,6},{5,7},{6,4},{7,5},{8,10},{9,11},{10,... | collective-permute-start | bytes 442376 | tf_op jit(solution)/shard_map/stack1/ppermute | solution.py:74
  193.8 18.4 %collective-permute-start.41 = (bf16[96,768]{1,0:T(8,128)(2,1)S(1)}, bf16[96,768]{1,0:T(8,128)(2,1)S(1)}, u32[]{:S(2)}, u32[]{:S(2)}) collective-permute-start(bf16[96,768]{1,0:T(8,128)(2,1)S(1)} %get-tuple-element.112), channel_id=1, source_target_pairs={{0,3},{1,0},{2,1},{3,2},{4,7},{5,4},{6,5},{7,6},{8,11},{9,8},{10,9... | collective-permute-start | bytes 442376 | tf_op jit(solution)/shard_map/stack2/ppermute | solution.py:74
  (59 other events, 619.9 us)
